TPU v7x, 32 devices: a whole 2x2x4 slice. The times are simulated.
32 devices in a mesh: seq: 8 (over z, x), ch: 4 (over y, core).
Axes of the slice: x: 2, y: 2, z: 4, core: 2. Of those that a mesh axis runs over, the one named last changes fastest.
Arguments:
- gate_rows: bfloat16 [4096, 2048], P(('seq', 'ch')), may hold values from -6 to 6
- key_rows: bfloat16 [4096, 2048], P(('seq', 'ch')), may hold values from -6 to 6
- value_rows: bfloat16 [4096, 2048], P(('seq', 'ch')), may hold values from -6 to 6
- spectrum: float32 [2, 16, 512, 2048], P(None, 'seq', None, 'ch'), may hold values from -6 to 6
- skip_bias: float32 [2048], replicated, may hold values from -1 to 1
Outputs:
- gated: bfloat16 [4096, 2048], P(('seq', 'ch'))
All inputs are finite; a program needn't handle non-finite values.
Results may differ from a plain program's by a relative error of at most 0.0049.
Values may be sent and summed in bfloat16 or wider, within the bound.
No kernel may reach another device: no remote copies, remote signals or barrier semaphores. Data moves between devices by JAX's collectives and lax.ppermute only.
A program may use at most 128 MiB of HBM per device.

v0:
```python
import functools
import math

import jax
import jax.numpy as jnp
import numpy as np
from jax import lax
from jax.experimental import pallas as pl
from jax.experimental.pallas import tpu as pltpu
from jax.sharding import PartitionSpec as P

highest = lax.Precision.HIGHEST
LANES = 128
MIB = 1 << 20


def phase_table(first, second, modulus):
    turns = first[:, None] * second[None, :] % modulus
    angles = turns.astype(jnp.float32) * (2.0 * math.pi / modulus)
    return (jnp.cos(angles), jnp.sin(angles))


def convolve(product, spectrum):
    seq_count = lax.axis_size("seq")
    tokens, width = product.shape
    length_two = 2 * seq_count * tokens
    offsets = jnp.arange(2 * seq_count, dtype=jnp.int32)
    places = jnp.arange(seq_count, dtype=jnp.int32)
    residues = jnp.arange(tokens, dtype=jnp.int32)
    off_cos, off_sin = phase_table(offsets, places, 2 * seq_count)
    res_cos, res_sin = phase_table(residues, residues, tokens)
    block = tokens // seq_count
    device = lax.axis_index("seq")
    pieces = lax.all_to_all(
        product.reshape(1, tokens, width), "seq", split_axis=1, concat_axis=0, tiled=True
    )
    values = pieces.astype(jnp.float32)
    real_part = jnp.einsum("kp,prc->krc", off_cos, values, precision=highest)
    imag_part = -jnp.einsum("kp,prc->krc", off_sin, values, precision=highest)
    own_rows = device * block + jnp.arange(block, dtype=jnp.int32)
    tw_cos, tw_sin = phase_table(offsets, own_rows, length_two)
    tw_cos = tw_cos[:, :, None]
    tw_sin = tw_sin[:, :, None]
    real_part, imag_part = (
        real_part * tw_cos + imag_part * tw_sin,
        imag_part * tw_cos - real_part * tw_sin,
    )
    real_part, imag_part = (
        lax.all_to_all(real_part, "seq", split_axis=0, concat_axis=1, tiled=True),
        lax.all_to_all(imag_part, "seq", split_axis=0, concat_axis=1, tiled=True),
    )
    real_next = jnp.einsum("grc,rs->gsc", real_part, res_cos, precision=highest) + jnp.einsum(
        "grc,rs->gsc", imag_part, res_sin, precision=highest
    )
    imag_next = jnp.einsum("grc,rs->gsc", imag_part, res_cos, precision=highest) - jnp.einsum(
        "grc,rs->gsc", real_part, res_sin, precision=highest
    )
    spec_real = spectrum[0]
    spec_imag = spectrum[1]
    real_part = real_next * spec_real - imag_next * spec_imag
    imag_part = real_next * spec_imag + imag_next * spec_real
    real_next = jnp.einsum("gsc,sr->grc", real_part, res_cos, precision=highest) - jnp.einsum(
        "gsc,sr->grc", imag_part, res_sin, precision=highest
    )
    imag_next = jnp.einsum("gsc,sr->grc", imag_part, res_cos, precision=highest) + jnp.einsum(
        "gsc,sr->grc", real_part, res_sin, precision=highest
    )
    own_offsets = 2 * device + jnp.arange(2, dtype=jnp.int32)
    un_cos, un_sin = phase_table(own_offsets, residues, length_two)
    un_cos = un_cos[:, :, None]
    un_sin = un_sin[:, :, None]
    real_part = real_next * un_cos - imag_next * un_sin
    imag_part = imag_next * un_cos + real_next * un_sin
    real_part, imag_part = (
        lax.all_to_all(real_part, "seq", split_axis=1, concat_axis=0, tiled=True),
        lax.all_to_all(imag_part, "seq", split_axis=1, concat_axis=0, tiled=True),
    )
    field = jnp.einsum("kp,krc->prc", off_cos, real_part, precision=highest) - jnp.einsum(
        "kp,krc->prc", off_sin, imag_part, precision=highest
    )
    field = field / length_two
    field = lax.all_to_all(field, "seq", split_axis=0, concat_axis=1, tiled=True)
    return field.reshape(tokens, width)


def any_mesh(gate_rows, key_rows, value_rows, spectrum, skip_bias):
    own = (key_rows.astype(jnp.float32) * value_rows.astype(jnp.float32)).astype(jnp.bfloat16)
    product = lax.all_to_all(own, "ch", split_axis=1, concat_axis=0, tiled=True)
    field = convolve(product, spectrum)
    field = lax.all_to_all(field, "ch", split_axis=0, concat_axis=1, tiled=True)
    gated = gate_rows.astype(jnp.float32) * (
        field + skip_bias[None, :] * own.astype(jnp.float32)
    )
    return gated.astype(jnp.bfloat16)


SEQ, CH, HALF = 8, 4, 4
DEVICES = SEQ * CH
ROOT = math.sqrt(0.5)
VMEM = pl.BlockSpec(memory_space=pltpu.VMEM)
STEP = 16


def swap(array, axis, mask, count):
    return lax.ppermute(array, axis, [(i, i ^ mask) for i in range(count)])


def columns_of(device):
    seq, ch = divmod(device, CH)
    return pl.ds((ch * HALF + seq % HALF) * LANES, LANES)


def rows_at(index, first=0):
    return pl.ds(pl.multiple_of(first + index * STEP, STEP), STEP)


def times(a, b):
    return a[0] * b[0] - a[1] * b[1], a[0] * b[1] + a[1] * b[0]


def root_16(power):
    return math.cos(power * math.pi / 8), math.sin(power * math.pi / 8)


def product_kernel(key_ref, value_ref, out_ref):
    for device in range(DEVICES // 2):
        at = columns_of(device)
        product = (key_ref[:, at].astype(jnp.float32) * value_ref[:, at].astype(jnp.float32)).astype(jnp.bfloat16)
        out_ref[device] = product
        out_ref[device + DEVICES // 2] = product


def four_real(a0, a1, a2, a3):
    even, odd = a0 + a2, a1 + a3
    less, more = (a1 - a3) * ROOT, odd * ROOT
    return (
        (even + odd, None),
        (a0 + less, -(a2 + more)),
        (a0 - a2, a3 - a1),
        (a0 - less, a2 - more),
        (even - odd, None),
    )


def residues_of(values, sign):
    even = four_real(*values[0::2])
    odd = four_real(*[v * sign for v in values[1::2]])
    out = [None] * SEQ
    out[0] = (even[0][0] + odd[0][0], None)
    out[4] = (even[4][0], -odd[4][0])
    for j in (1, 2, 3):
        turned = times(odd[j], root_16(-j))
        out[j] = (even[j][0] + turned[0], even[j][1] + turned[1])
        out[8 - j] = (even[j][0] - turned[0], turned[1] - even[j][1])
    return out


def four_back(zero, four, one, two, three):
    plus, minus = zero + four, zero - four
    half_way = (one[0] - three[0]) * ROOT
    across = (one[1] + three[1]) * ROOT
    return (
        plus + two[0] + (one[0] + three[0]),
        minus - two[1] + (half_way - across),
        plus - two[0] + (three[1] - one[1]),
        minus + two[1] - (half_way + across),
    )


def blocks_of(parts):
    sums, turned = [], []
    for j in (1, 2, 3):
        a, b = parts[j], parts[8 - j]
        sums.append((a[0] + b[0], a[1] - b[1]))
        turned.append(times((a[0] - b[0], a[1] + b[1]), root_16(j)))
    even = four_back(parts[0][0], parts[4][0], *sums)
    odd = four_back(parts[0][0], -parts[4][1], *turned)
    return [value for pair in zip(even, odd) for value in pair]


def sign_of_half():
    return jnp.where(lax.axis_index("seq") < HALF, 1.0, -1.0).astype(jnp.float32)


def twiddles(table, j):
    cos = jnp.broadcast_to(table[:, j : j + 1], (STEP, LANES))
    sin = jnp.broadcast_to(table[:, SEQ + j : SEQ + j + 1], (STEP, LANES))
    return cos, sin


def forward_kernel(tokens, table_ref, dft_ref, re_ref, im_ref, stage):
    half = lax.axis_index("seq") // HALF
    sign = sign_of_half()
    size = tokens.shape[1]

    def rows_of(index, carry):
        at = rows_at(index)
        table = table_ref[half, at, :]
        parts = residues_of([tokens[p, at, :].astype(jnp.float32) for p in range(SEQ)], sign)
        for j, (real, imag) in enumerate(parts):
            cos, sin = twiddles(table, j)
            if imag is None:
                real, imag = real * cos, -(real * sin)
            else:
                real, imag = real * cos + imag * sin, imag * cos - real * sin
            to = pl.ds(j * LANES, LANES)
            real = real.astype(jnp.bfloat16)
            stage[at, to] = real
            stage[rows_at(index, size), to] = imag.astype(jnp.bfloat16)
            stage[rows_at(index, 2 * size), to] = -real
        return carry

    lax.fori_loop(0, size // STEP, rows_of, 0)
    for pair in range(HALF):
        to = pl.ds(pair * 2 * LANES, 2 * LANES)
        re_ref[:, to] = jnp.dot(dft_ref[...], stage[pl.ds(0, 2 * size), to], preferred_element_type=jnp.float32)
        im_ref[:, to] = jnp.dot(dft_ref[...], stage[pl.ds(size, 2 * size), to], preferred_element_type=jnp.float32)


def inverse_kernel(*refs):
    spec, (re_ref, im_ref, table_ref, dft_ref, out_ref, stage, back_re, back_im) = refs[:HALF], refs[HALF:]
    seq = lax.axis_index("seq")
    half, place = seq // HALF, seq % HALF
    sign = sign_of_half()
    size = re_ref.shape[0]
    for member in range(HALF):
        for odd in range(2):
            to = pl.ds(pl.multiple_of((2 * (place ^ member) + odd) * LANES, LANES), LANES)
            x = re_ref[:, to], im_ref[:, to]
            h = spec[member][0, odd].astype(jnp.float32), spec[member][1, odd].astype(jnp.float32)
            y_re, y_im = times(x, h)
            y_re, y_im = y_re.astype(jnp.bfloat16), y_im.astype(jnp.bfloat16)
            to = pl.ds((2 * member + odd) * LANES, LANES)
            stage[pl.ds(0, size), to] = y_im
            stage[pl.ds(size, size), to] = y_re
            stage[pl.ds(2 * size, size), to] = -y_im
        to = pl.ds(member * 2 * LANES, 2 * LANES)
        into = pl.ds(pl.multiple_of((place ^ member) * 2 * LANES, 2 * LANES), 2 * LANES)
        back_im[:, into] = jnp.dot(dft_ref[...], stage[pl.ds(0, 2 * size), to], preferred_element_type=jnp.float32)
        back_re[:, into] = jnp.dot(dft_ref[...], stage[pl.ds(size, 2 * size), to], preferred_element_type=jnp.float32)
    scale = 1.0 / (2 * SEQ * size)

    def rows_of(index, carry):
        at = rows_at(index)
        table = table_ref[half, at, :]
        parts = []
        for j in range(SEQ):
            to = pl.ds(j * LANES, LANES)
            parts.append(times((back_re[at, to], back_im[at, to]), twiddles(table, j)))
        for p, value in enumerate(blocks_of(parts)):
            out_ref[p, at, :] = (value * (scale * sign if p % 2 else scale)).astype(jnp.bfloat16)
        return carry

    lax.fori_loop(0, size // STEP, rows_of, 0)


def gate_kernel(gate_ref, key_ref, value_ref, skip_ref, field_ref, out_ref):
    for device in range(DEVICES // 2):
        at = columns_of(device)
        product = (key_ref[:, at].astype(jnp.float32) * value_ref[:, at].astype(jnp.float32)).astype(jnp.bfloat16)
        field = field_ref[device].astype(jnp.float32) + field_ref[device + DEVICES // 2].astype(jnp.float32)
        gated = gate_ref[:, at].astype(jnp.float32) * (field + skip_ref[:, at] * product.astype(jnp.float32))
        out_ref[:, at] = gated.astype(jnp.bfloat16)


def call(kernel, name, ins, outs, scratch=(), limit=40 * MIB):
    return pl.pallas_call(
        kernel,
        out_shape=tuple(jax.ShapeDtypeStruct(shape, dtype) for shape, dtype in outs),
        in_specs=[VMEM for _ in ins],
        out_specs=tuple(VMEM for _ in outs),
        scratch_shapes=list(scratch),
        compiler_params=pltpu.CompilerParams(vmem_limit_bytes=limit),
        name=name,
    )(*ins)


def halves(gate_rows, key_rows, value_rows, spectrum, skip_bias):
    bf16, f32 = jnp.bfloat16, jnp.float32
    rows, channels = key_rows.shape
    size = rows * CH
    length_two = 2 * SEQ * size
    everywhere = ("seq", "ch")
    place = lax.axis_index("seq") % HALF

    angles = np.arange(size)[:, None] * np.arange(size)[None, :] % size * (2.0 * np.pi / size)
    dft = jnp.asarray(np.concatenate([np.cos(angles), np.sin(angles)], axis=1), bf16)
    angles = np.arange(size)[:, None] * np.arange(2 * SEQ)[None, :] * (2.0 * np.pi / length_two)
    table = np.stack([np.cos(angles), np.sin(angles)], axis=1).reshape(size, 2, 2, SEQ)
    table = jnp.asarray(table.transpose(2, 0, 1, 3).reshape(2, size, 2 * SEQ), f32)

    spec = [
        lax.dynamic_slice_in_dim(spectrum, (place ^ member) * LANES, LANES, axis=3).astype(bf16)
        for member in range(HALF)
    ]
    sends = call(product_kernel, "product", [key_rows, value_rows], [((DEVICES, rows, LANES), bf16)])[0]
    tokens = lax.all_to_all(sends, everywhere, split_axis=0, concat_axis=0, tiled=True).reshape(SEQ, size, LANES)
    spec = [spec[0]] + [swap(spec[member], "seq", member, SEQ) for member in range(1, HALF)]
    freq = call(
        forward_kernel,
        "forward",
        [tokens, table, dft],
        [((size, SEQ * LANES), f32)] * 2,
        [pltpu.VMEM((3 * size, SEQ * LANES), bf16)],
    )
    shares = call(
        inverse_kernel,
        "inverse",
        [*spec, *freq, table, dft],
        [((SEQ, size, LANES), bf16)],
        [pltpu.VMEM((3 * size, SEQ * LANES), bf16)] + [pltpu.VMEM((size, SEQ * LANES), f32)] * 2,
    )[0].reshape(DEVICES, rows, LANES)
    field = lax.all_to_all(shares, everywhere, split_axis=0, concat_axis=0, tiled=True)
    return call(
        gate_kernel,
        "gate",
        [gate_rows, key_rows, value_rows, skip_bias.reshape(1, channels), field],
        [((rows, channels), bf16)],
    )[0]


def solution(mesh):
    placed = (
        P(("seq", "ch"), None),
        P(("seq", "ch"), None),
        P(("seq", "ch"), None),
        P(None, "seq", None, "ch"),
        P(),
    )
    shape = dict(mesh.shape)
    body = halves if (shape["seq"], shape["ch"]) == (SEQ, CH) else any_mesh
    return jax.shard_map(
        body, mesh=mesh, in_specs=placed, out_specs=P(("seq", "ch"), None), check_vma=False
    )
```

profile of v0, /device:TPU:0, one launch (start us, length us, event | category | flops | bytes accessed | tf_op | source)
XLA Modules:
  0.0 94.3 jit_solution(2457234240867726188)
XLA Ops:
  0.0 0.0 copy-start
  0.0 0.0 copy-start.1
  0.0 0.0 copy-start.2
  0.0 1.2 %copy-done.2 = bf16[128,2048]{1,0:T(8,128)(2,1)S(1)} copy-done((bf16[128,2048]{1,0:T(8,128)(2,1)S(1)}, bf16[128,2048]{1,0:T(8,128)(2,1)}, u32[]{:S(2)}) %copy-start.2) | copy-done | bytes 524312
  1.2 0.0 copy-start.4
  1.2 1.0 %copy-done.4 = bf16[128,2048]{1,0:T(8,128)(2,1)S(1)} copy-done((bf16[128,2048]{1,0:T(8,128)(2,1)S(1)}, bf16[128,2048]{1,0:T(8,128)(2,1)}, u32[]{:S(2)}) %copy-start.4) | copy-done | bytes 524312
  2.2 1.1 %product.1 = bf16[32,128,128]{2,1,0:T(8,128)(2,1)} custom-call(bf16[128,2048]{1,0:T(8,128)(2,1)S(1)} %copy-done.2, bf16[128,2048]{1,0:T(8,128)(2,1)S(1)} %copy-done.4), custom_call_target="tpu_custom_call" | custom-call | tf_op jit(solution)/shard_map/product/pallas_call | solution.py:267
  3.3 7.3 %all-to-all-start = ((bf16[32,128,128]{2,1,0:T(8,128)(2,1)}), bf16[32,128,128]{2,1,0:T(8,128)(2,1)S(1)}, u32[]{:S(2)}, u32[]{:S(2)}) async-start(bf16[32,128,128]{2,1,0:T(8,128)(2,1)} %product.1), calls=%async_computation | async-start | bytes 2097152 | tf_op jit(solution)/shard_map/all_to_all | solution.py:297
  10.7 3.5 %dynamic-slice_convert_fusion = (bf16[2,2,512,128]{3,2,1,0:T(8,128)(2,1)}, bf16[2,2,512,128]{3,2,1,0:T(8,128)(2,1)}, bf16[2,2,512,128]{3,2,1,0:T(8,128)(2,1)S(1)}, bf16[2,2,512,128]{3,2,1,0:T(8,128)(2,1)}) fusion(f32[2,2,512,512]{3,2,1,0:T(8,128)} %param.10, s32[]{:T(128)S(6)} %select_n.23, s32[]{:T(128)S(6)} %select_n.21, s32[]{:T(128)S(6)} %select_n.20, ...), kind=kLoop, calls=%fused_computation | loop fusion | bytes 4194320 | tf_op jit(solution)/shard_map/convert_element_type | solution.py:293
  14.2 2.7 %collective-permute-start.2 = (bf16[2,2,512,128]{3,2,1,0:T(8,128)(2,1)}, bf16[2,2,512,128]{3,2,1,0:T(8,128)(2,1)}, u32[]{:S(2)}, u32[]{:S(2)}) collective-permute-start(bf16[2,2,512,128]{3,2,1,0:T(8,128)(2,1)} %get-tuple-element.9), channel_id=1, source_target_pairs={{0,12},{4,8},{8,4},{12,0},{16,28},{20,24},{24,20},{28,16},{1,13},{... | collective-permute-start | bytes 1572872 | tf_op jit(solution)/shard_map/ppermute | solution.py:105
  16.9 0.6 collective-permute-start
  17.4 0.3 collective-permute-start.1
  17.7 19.2 %all-to-all-done = bf16[32,128,128]{2,1,0:T(8,128)(2,1)S(1)} async-done(((bf16[32,128,128]{2,1,0:T(8,128)(2,1)}), bf16[32,128,128]{2,1,0:T(8,128)(2,1)S(1)}, u32[]{:S(2)}, u32[]{:S(2)}) %all-to-all-start) | async-done | bytes 1048608 | tf_op jit(solution)/shard_map/all_to_all | solution.py:297
  36.9 0.0 copy-done
  36.9 0.0 copy-done.1
  36.9 6.3 %forward.1 = (f32[512,1024]{1,0:T(8,128)S(1)}, f32[512,1024]{1,0:T(8,128)S(1)}) custom-call(bf16[8,512,128]{2,1,0:T(8,128)(2,1)S(1)} %bitcast.4, f32[2,512,16]{2,1,0:T(8,128)S(1)} %copy-done.1, bf16[512,1024]{1,0:T(8,128)(2,1)S(1)} %copy-done), custom_call_target="tpu_custom_call" | custom-call | tf_op jit(solution)/shard_map/forward/pallas_call | solution.py:267
  43.2 0.0 collective-permute-done.2.refs_3_
  43.2 4.7 %collective-permute-done.refs_1_ = bf16[2,2,512,128]{3,2,1,0:T(8,128)(2,1)} collective-permute-done((bf16[2,2,512,128]{3,2,1,0:T(8,128)(2,1)}, bf16[2,2,512,128]{3,2,1,0:T(8,128)(2,1)}, u32[]{:S(2)}, u32[]{:S(2)}) %collective-permute-start) | collective-permute-done | bytes 524320 | tf_op jit(solution)/shard_map/ppermute | solution.py:105
  47.8 5.2 %collective-permute-done.1.refs_2_ = bf16[2,2,512,128]{3,2,1,0:T(8,128)(2,1)} collective-permute-done((bf16[2,2,512,128]{3,2,1,0:T(8,128)(2,1)}, bf16[2,2,512,128]{3,2,1,0:T(8,128)(2,1)}, u32[]{:S(2)}, u32[]{:S(2)}) %collective-permute-start.1) | collective-permute-done | bytes 524320 | tf_op jit(solution)/shard_map/ppermute | solution.py:105
  53.0 0.0 copy-start.3
  53.0 0.0 copy-start.5
  53.0 0.0 copy-start.6
  53.0 0.0 copy-start.7
  53.0 8.4 %inverse.1 = bf16[8,512,128]{2,1,0:T(8,128)(2,1)S(1)} custom-call(bf16[2,2,512,128]{3,2,1,0:T(8,128)(2,1)S(1)} %get-tuple-element.11.refs_0_, bf16[2,2,512,128]{3,2,1,0:T(8,128)(2,1)} %collective-permute-done.refs_1_, bf16[2,2,512,128]{3,2,1,0:T(8,128)(2,1)} %collective-permute-done.1.refs_2_, bf16[2,2,512,128]{3,2,1,0:T(8,128)(2,1)} %collective-permute-done.2.refs_3_, ...), custom_call_target="tpu_custom_call" | custom-call | tf_op jit(solution)/shard_map/inverse/pallas_call | solution.py:267
  61.4 31.6 %all_to_all.10.field_ref = bf16[32,128,128]{2,1,0:T(8,128)(2,1)S(1)} all-to-all(bf16[32,128,128]{2,1,0:T(8,128)(2,1)S(1)} %bitcast.3), channel_id=1, replica_groups=mesh['seq'=8,'ch'=4] {'seq','ch'}, dimensions={0} | all-to-all | bytes 2097152 | tf_op jit(solution)/shard_map/all_to_all | solution.py:313
  93.0 0.0 copy-done.3
  93.0 0.0 copy-done.5
  93.0 0.0 copy-done.6
  93.0 0.0 copy-done.7
  93.0 1.2 %gate.1 = bf16[128,2048]{1,0:T(8,128)(2,1)} custom-call(bf16[128,2048]{1,0:T(8,128)(2,1)S(1)} %copy-done.6, bf16[128,2048]{1,0:T(8,128)(2,1)S(1)} %copy-done.3, bf16[128,2048]{1,0:T(8,128)(2,1)S(1)} %copy-done.5, f32[1,2048]{1,0:T(1,128)S(1)} %bitcast.5, bf16[32,128,128]{2,1,0:T(8,128)(2,1)S(1)} %all_to_all.10.field_ref), custom_call_target="tpu_custom_call" | custom-call | tf_op jit(solution)/shard_map/gate/pallas_call | solution.py:267
Async XLA Ops:
  0.0 36.9 %copy-start = (bf16[512,1024]{1,0:T(8,128)(2,1)S(1)}, bf16[512,1024]{1,0:T(8,128)(2,1)}, u32[]{:S(2)}) copy-start(bf16[512,1024]{1,0:T(8,128)(2,1)} %constant.33.clone.dft_ref.refs_7_) | copy-start | bytes 3145732
  0.0 36.9 %copy-start.1 = (f32[2,512,16]{2,1,0:T(8,128)S(1)}, f32[2,512,16]{2,1,0:T(8,128)}, u32[]{:S(2)}) copy-start(f32[2,512,16]{2,1,0:T(8,128)} %constant.34.clone.table_ref.refs_6_) | copy-start | bytes 196612
  0.0 1.2 %copy-start.2 = (bf16[128,2048]{1,0:T(8,128)(2,1)S(1)}, bf16[128,2048]{1,0:T(8,128)(2,1)}, u32[]{:S(2)}) copy-start(bf16[128,2048]{1,0:T(8,128)(2,1)} %key_ref.3) | copy-start | bytes 1572868
  1.2 1.0 %copy-start.4 = (bf16[128,2048]{1,0:T(8,128)(2,1)S(1)}, bf16[128,2048]{1,0:T(8,128)(2,1)}, u32[]{:S(2)}) copy-start(bf16[128,2048]{1,0:T(8,128)(2,1)} %value_ref.3) | copy-start | bytes 1572868
  3.3 33.5 %all-to-all-start = ((bf16[32,128,128]{2,1,0:T(8,128)(2,1)}), bf16[32,128,128]{2,1,0:T(8,128)(2,1)S(1)}, u32[]{:S(2)}, u32[]{:S(2)}) async-start(bf16[32,128,128]{2,1,0:T(8,128)(2,1)} %product.1), calls=%async_computation | async-start | bytes 2097152 | tf_op jit(solution)/shard_map/all_to_all | solution.py:297
  14.2 28.9 %collective-permute-start.2 = (bf16[2,2,512,128]{3,2,1,0:T(8,128)(2,1)}, bf16[2,2,512,128]{3,2,1,0:T(8,128)(2,1)}, u32[]{:S(2)}, u32[]{:S(2)}) collective-permute-start(bf16[2,2,512,128]{3,2,1,0:T(8,128)(2,1)} %get-tuple-element.9), channel_id=1, source_target_pairs={{0,12},{4,8},{8,4},{12,0},{16,28},{20,24},{24,20},{28,16},{1,13},{... | collective-permute-start | bytes 1572872 | tf_op jit(solution)/shard_map/ppermute | solution.py:105
  16.9 31.0 %collective-permute-start = (bf16[2,2,512,128]{3,2,1,0:T(8,128)(2,1)}, bf16[2,2,512,128]{3,2,1,0:T(8,128)(2,1)}, u32[]{:S(2)}, u32[]{:S(2)}) collective-permute-start(bf16[2,2,512,128]{3,2,1,0:T(8,128)(2,1)} %get-tuple-element.10), channel_id=1, source_target_pairs={{0,4},{4,0},{8,12},{12,8},{16,20},{20,16},{24,28},{28,24},{1,5},{5... | collective-permute-start | bytes 1572872 | tf_op jit(solution)/shard_map/ppermute | solution.py:105
  17.4 35.6 %collective-permute-start.1 = (bf16[2,2,512,128]{3,2,1,0:T(8,128)(2,1)}, bf16[2,2,512,128]{3,2,1,0:T(8,128)(2,1)}, u32[]{:S(2)}, u32[]{:S(2)}) collective-permute-start(bf16[2,2,512,128]{3,2,1,0:T(8,128)(2,1)} %get-tuple-element.12), channel_id=1, source_target_pairs={{0,8},{4,12},{8,0},{12,4},{16,24},{20,28},{24,16},{28,20},{1,9},{5... | collective-permute-start | bytes 1572872 | tf_op jit(solution)/shard_map/ppermute | solution.py:105
  53.0 40.0 %copy-start.3 = (bf16[128,2048]{1,0:T(8,128)(2,1)S(1)}, bf16[128,2048]{1,0:T(8,128)(2,1)}, u32[]{:S(2)}) copy-start(bf16[128,2048]{1,0:T(8,128)(2,1)} %key_ref.3) | copy-start | bytes 1572868
  53.0 40.0 %copy-start.5 = (bf16[128,2048]{1,0:T(8,128)(2,1)S(1)}, bf16[128,2048]{1,0:T(8,128)(2,1)}, u32[]{:S(2)}) copy-start(bf16[128,2048]{1,0:T(8,128)(2,1)} %value_ref.3) | copy-start | bytes 1572868
  53.0 40.0 %copy-start.6 = (bf16[128,2048]{1,0:T(8,128)(2,1)S(1)}, bf16[128,2048]{1,0:T(8,128)(2,1)}, u32[]{:S(2)}) copy-start(bf16[128,2048]{1,0:T(8,128)(2,1)} %gate_ref.1) | copy-start | bytes 1572868
  53.0 40.0 %copy-start.7 = (f32[2048]{0:T(1024)S(1)}, f32[2048]{0:T(1024)}, u32[]{:S(2)}) copy-start(f32[2048]{0:T(1024)} %param.11) | copy-start | bytes 24580
where the time goes:
time: 94.5 us; the launch traced here: 94.3 us
  blocking collectives  31.6 us (33%)
  waiting for transfers between devices  29 us (31%)
  Pallas kernels  17 us (18%)
  starting transfers between devices  10.8 us (11%)
  local copies, waits for them, and re-layouts  5.76 us (6%)
    all_to_all x1, blocking collectives, halves(): lax.all_to_all(shares, everywhere, split_axis=0, concat_axis=0, tiled=True)  31.6 us
    all_to_all x1, waiting for transfers between devices, halves(): lax.all_to_all(sends, everywhere, split_axis=0, concat_axis=0, tiled=True)  19.2 us
    pallas_call x4, Pallas kernels, call(): pl.pallas_call(kernel, out_shape=tuple((jax.ShapeDtypeStruct(shape, dtype...  17 us
    ppermute x3, waiting for transfers between devices, swap(): return lax.ppermute(array, axis, [(i, i ^ mask) for i in range(count)])  9.86 us
    all_to_all x1, starting transfers between devices, halves(): lax.all_to_all(sends, everywhere, split_axis=0, concat_axis=0, tiled=True)  7.3 us
    convert_element_type x1, local copies, waits for them, and re-layouts, halves(): lax.dynamic_slice_in_dim(spectrum, (place ^ member) * LANES, LANES, axis=3)  3.54 us
    ppermute x3, starting transfers between devices, swap(): return lax.ppermute(array, axis, [(i, i ^ mask) for i in range(count)])  3.49 us
    unnamed x16, local copies, waits for them, and re-layouts  2.22 us
  transfers between devices with their start and end apart: 4, of which 3 were waited for; matrix products, arithmetic and copies ran while one was open for 4% of the time, Pallas kernels for 7%

commit v1 on v0

--- a/solution.py
+++ b/solution.py
@@ -97,6 +97,7 @@
 SEQ, CH, HALF = 8, 4, 4
 DEVICES = SEQ * CH
 ROOT = math.sqrt(0.5)
+EARLY, LATE = (0, 1, 2), (3,)
 VMEM = pl.BlockSpec(memory_space=pltpu.VMEM)
 STEP = 16
 
@@ -122,12 +123,62 @@
     return math.cos(power * math.pi / 8), math.sin(power * math.pi / 8)
 
 
-def product_kernel(key_ref, value_ref, out_ref):
-    for device in range(DEVICES // 2):
-        at = columns_of(device)
-        product = (key_ref[:, at].astype(jnp.float32) * value_ref[:, at].astype(jnp.float32)).astype(jnp.bfloat16)
-        out_ref[device] = product
-        out_ref[device + DEVICES // 2] = product
+def product_kernel(key_hbm, value_hbm, out_ref, key, value, sems):
+    groups = DEVICES // 2
+    width = key.shape[1] // CH
+    copies = []
+    for ch in range(CH):
+        at = pl.ds(ch * width, width)
+        copies.append(
+            [
+                pltpu.make_async_copy(source.at[:, at], to.at[:, at], sems.at[which, ch])
+                for which, (source, to) in enumerate(((key_hbm, key), (value_hbm, value)))
+            ]
+        )
+        for copy in copies[-1]:
+            copy.start()
+    for ch in range(CH):
+        for copy in copies[ch]:
+            copy.wait()
+        for member in range(HALF):
+            device = member * CH + ch
+            at = columns_of(device)
+            product = (key[:, at].astype(jnp.float32) * value[:, at].astype(jnp.float32)).astype(jnp.bfloat16)
+            out_ref[device] = product
+            out_ref[device + groups] = product
+
+
+def spectrum_kernel(place_ref, *refs):
+    spec, members = refs[:HALF], refs[HALF:]
+    rows = members[0].shape[3]
+    for member in range(HALF):
+        for part in range(2):
+            for odd in range(2):
+                for bit in range(2):
+                    values = spec[member][part, odd, pl.ds(bit, rows, stride=2), :]
+                    members[member][part, odd, bit] = values.astype(jnp.bfloat16)
+
+
+def members_of(spectrum, steps=4):
+    size = spectrum.shape[2]
+    piece = size // steps
+    place = (lax.axis_index("seq") % HALF).astype(jnp.int32).reshape(1)
+    spec_blocks = [
+        pl.BlockSpec((2, 2, piece, LANES), lambda i, place, member=member: (0, 0, i, place[0] ^ member))
+        for member in range(HALF)
+    ]
+    return pl.pallas_call(
+        spectrum_kernel,
+        grid_spec=pltpu.PrefetchScalarGridSpec(
+            num_scalar_prefetch=1,
+            grid=(steps,),
+            in_specs=spec_blocks,
+            out_specs=[pl.BlockSpec((2, 2, 2, piece // 2, LANES), lambda i, place: (0, 0, 0, i, 0))] * HALF,
+        ),
+        out_shape=[jax.ShapeDtypeStruct((2, 2, 2, size // 2, LANES), jnp.bfloat16)] * HALF,
+        compiler_params=pltpu.CompilerParams(vmem_limit_bytes=56 * MIB),
+        name="spectrum",
+    )(place, *[spectrum] * HALF)
 
 
 def four_real(a0, a1, a2, a3):
@@ -182,76 +233,113 @@
     return jnp.where(lax.axis_index("seq") < HALF, 1.0, -1.0).astype(jnp.float32)
 
 
-def twiddles(table, j):
-    cos = jnp.broadcast_to(table[:, j : j + 1], (STEP, LANES))
-    sin = jnp.broadcast_to(table[:, SEQ + j : SEQ + j + 1], (STEP, LANES))
-    return cos, sin
-
-
-def forward_kernel(tokens, table_ref, dft_ref, re_ref, im_ref, stage):
-    half = lax.axis_index("seq") // HALF
+def turn_table(size):
+    angles = np.arange(2 * SEQ)[:, None] * np.arange(size)[None, :] * (2.0 * np.pi / (2 * SEQ * size))
+    angles = angles.reshape(2, SEQ, size)
+    between = np.broadcast_to(np.arange(size) * (2.0 * np.pi / size), (2, 1, size))
+    angles = np.concatenate([angles, between], axis=1)
+    table = np.stack([np.cos(angles), np.sin(angles)], axis=2).astype(np.float32)
+    return jnp.asarray(np.repeat(table[..., None], LANES, axis=-1))
+
+
+def forward_kernel(tokens, table, dft_ref, re_ref, im_ref, stage):
     sign = sign_of_half()
     size = tokens.shape[1]
+    short = size // 2
+
+    def rows_of(index, carry):
+        both = []
+        for first in (0, short):
+            at = rows_at(index, first)
+            parts = residues_of([tokens[p, at, :].astype(jnp.float32) for p in range(SEQ)], sign)
+            turned = []
+            for j, (real, imag) in enumerate(parts):
+                cos, sin = table[j, 0, at, :], table[j, 1, at, :]
+                if imag is None:
+                    turned.append((real * cos, -(real * sin)))
+                else:
+                    turned.append((real * cos + imag * sin, imag * cos - real * sin))
+            both.append(turned)
+        at = rows_at(index)
+        cos, sin = table[SEQ, 0, at, :], table[SEQ, 1, at, :]
+        for j in range(SEQ):
+            a, b = both[0][j], both[1][j]
+            less = a[0] - b[0], a[1] - b[1]
+            pair = (a[0] + b[0], a[1] + b[1]), (less[0] * cos + less[1] * sin, less[1] * cos - less[0] * sin)
+            for bit, (real, imag) in enumerate(pair):
+                to = pl.ds((bit * SEQ + j) * LANES, LANES)
+                real = real.astype(jnp.bfloat16)
+                stage[at, to] = real
+                stage[rows_at(index, short), to] = imag.astype(jnp.bfloat16)
+                stage[rows_at(index, size), to] = -real
+        return carry
+
+    lax.fori_loop(0, short // STEP, rows_of, 0)
+    re_ref[...] = jnp.dot(dft_ref[...], stage[pl.ds(0, size), :], preferred_element_type=jnp.float32)
+    im_ref[...] = jnp.dot(dft_ref[...], stage[pl.ds(short, size), :], preferred_element_type=jnp.float32)
+
+
+def filter_members(members, spec, re_ref, im_ref, dft_ref, back_re, back_im, stage):
+    place = lax.axis_index("seq") % HALF
+    short = re_ref.shape[0]
+    size = 2 * short
+    for index, member in enumerate(members):
+        for odd in range(2):
+            for bit in range(2):
+                column = bit * SEQ + 2 * (place ^ member) + odd
+                at = pl.ds(pl.multiple_of(column * LANES, LANES), LANES)
+                h = spec[index][0, odd, bit].astype(jnp.float32), spec[index][1, odd, bit].astype(jnp.float32)
+                y_re, y_im = times((re_ref[:, at], im_ref[:, at]), h)
+                y_re, y_im = y_re.astype(jnp.bfloat16), y_im.astype(jnp.bfloat16)
+                to = pl.ds((odd * 2 + bit) * LANES, LANES)
+                stage[index, pl.ds(0, short), to] = y_im
+                stage[index, pl.ds(short, short), to] = y_re
+                stage[index, pl.ds(size, short), to] = -y_im
+        back_im[place ^ member] = jnp.dot(
+            dft_ref[...], stage[index, pl.ds(0, size), :], preferred_element_type=jnp.float32
+        )
+        back_re[place ^ member] = jnp.dot(
+            dft_ref[...], stage[index, pl.ds(short, size), :], preferred_element_type=jnp.float32
+        )
+
+
+def early_kernel(*refs):
+    spec, (re_ref, im_ref, dft_ref, back_re, back_im, stage) = refs[: len(EARLY)], refs[len(EARLY) :]
+    filter_members(EARLY, spec, re_ref, im_ref, dft_ref, back_re, back_im, stage)
+
+
+def late_kernel(*refs):
+    spec, refs = refs[: len(LATE)], refs[len(LATE) :]
+    early_re, early_im, re_ref, im_ref, table, dft_ref, out_ref, back_re, back_im, stage = refs
+    sign = sign_of_half()
+    place = lax.axis_index("seq") % HALF
+    short = re_ref.shape[0]
+    size = 2 * short
+    filter_members(LATE, spec, re_ref, im_ref, dft_ref, back_re, back_im, stage)
+    for member in EARLY:
+        back_re[place ^ member] = early_re[place ^ member]
+        back_im[place ^ member] = early_im[place ^ member]
+    scale = 1.0 / (2 * SEQ * size)
 
     def rows_of(index, carry):
         at = rows_at(index)
-        table = table_ref[half, at, :]
-        parts = residues_of([tokens[p, at, :].astype(jnp.float32) for p in range(SEQ)], sign)
-        for j, (real, imag) in enumerate(parts):
-            cos, sin = twiddles(table, j)
-            if imag is None:
-                real, imag = real * cos, -(real * sin)
-            else:
-                real, imag = real * cos + imag * sin, imag * cos - real * sin
-            to = pl.ds(j * LANES, LANES)
-            real = real.astype(jnp.bfloat16)
-            stage[at, to] = real
-            stage[rows_at(index, size), to] = imag.astype(jnp.bfloat16)
-            stage[rows_at(index, 2 * size), to] = -real
+        late = rows_at(index, short)
+        cos, sin = table[SEQ, 0, at, :], table[SEQ, 1, at, :]
+        parts = [], []
+        for j in range(SEQ):
+            pair = []
+            for bit in range(2):
+                to = pl.ds((j % 2 * 2 + bit) * LANES, LANES)
+                pair.append((back_re[j // 2, at, to], back_im[j // 2, at, to]))
+            a, b = pair[0], times(pair[1], (cos, sin))
+            parts[0].append(times((a[0] + b[0], a[1] + b[1]), (table[j, 0, at, :], table[j, 1, at, :])))
+            parts[1].append(times((a[0] - b[0], a[1] - b[1]), (table[j, 0, late, :], table[j, 1, late, :])))
+        for where, values in zip((at, late), parts):
+            for p, value in enumerate(blocks_of(values)):
+                out_ref[p, where, :] = (value * (scale * sign if p % 2 else scale)).astype(jnp.bfloat16)
         return carry
 
-    lax.fori_loop(0, size // STEP, rows_of, 0)
-    for pair in range(HALF):
-        to = pl.ds(pair * 2 * LANES, 2 * LANES)
-        re_ref[:, to] = jnp.dot(dft_ref[...], stage[pl.ds(0, 2 * size), to], preferred_element_type=jnp.float32)
-        im_ref[:, to] = jnp.dot(dft_ref[...], stage[pl.ds(size, 2 * size), to], preferred_element_type=jnp.float32)
-
-
-def inverse_kernel(*refs):
-    spec, (re_ref, im_ref, table_ref, dft_ref, out_ref, stage, back_re, back_im) = refs[:HALF], refs[HALF:]
-    seq = lax.axis_index("seq")
-    half, place = seq // HALF, seq % HALF
-    sign = sign_of_half()
-    size = re_ref.shape[0]
-    for member in range(HALF):
-        for odd in range(2):
-            to = pl.ds(pl.multiple_of((2 * (place ^ member) + odd) * LANES, LANES), LANES)
-            x = re_ref[:, to], im_ref[:, to]
-            h = spec[member][0, odd].astype(jnp.float32), spec[member][1, odd].astype(jnp.float32)
-            y_re, y_im = times(x, h)
-            y_re, y_im = y_re.astype(jnp.bfloat16), y_im.astype(jnp.bfloat16)
-            to = pl.ds((2 * member + odd) * LANES, LANES)
-            stage[pl.ds(0, size), to] = y_im
-            stage[pl.ds(size, size), to] = y_re
-            stage[pl.ds(2 * size, size), to] = -y_im
-        to = pl.ds(member * 2 * LANES, 2 * LANES)
-        into = pl.ds(pl.multiple_of((place ^ member) * 2 * LANES, 2 * LANES), 2 * LANES)
-        back_im[:, into] = jnp.dot(dft_ref[...], stage[pl.ds(0, 2 * size), to], preferred_element_type=jnp.float32)
-        back_re[:, into] = jnp.dot(dft_ref[...], stage[pl.ds(size, 2 * size), to], preferred_element_type=jnp.float32)
-    scale = 1.0 / (2 * SEQ * size)
-
-    def rows_of(index, carry):
-        at = rows_at(index)
-        table = table_ref[half, at, :]
-        parts = []
-        for j in range(SEQ):
-            to = pl.ds(j * LANES, LANES)
-            parts.append(times((back_re[at, to], back_im[at, to]), twiddles(table, j)))
-        for p, value in enumerate(blocks_of(parts)):
-            out_ref[p, at, :] = (value * (scale * sign if p % 2 else scale)).astype(jnp.bfloat16)
-        return carry
-
-    lax.fori_loop(0, size // STEP, rows_of, 0)
+    lax.fori_loop(0, short // STEP, rows_of, 0)
 
 
 def gate_kernel(gate_ref, key_ref, value_ref, skip_ref, field_ref, out_ref):
@@ -263,11 +351,11 @@
         out_ref[:, at] = gated.astype(jnp.bfloat16)
 
 
-def call(kernel, name, ins, outs, scratch=(), limit=40 * MIB):
+def call(kernel, name, ins, outs, scratch=(), limit=24 * MIB, hbm=()):
     return pl.pallas_call(
         kernel,
         out_shape=tuple(jax.ShapeDtypeStruct(shape, dtype) for shape, dtype in outs),
-        in_specs=[VMEM for _ in ins],
+        in_specs=[pl.BlockSpec(memory_space=pl.ANY) if index in hbm else VMEM for index, _ in enumerate(ins)],
         out_specs=tuple(VMEM for _ in outs),
         scratch_shapes=list(scratch),
         compiler_params=pltpu.CompilerParams(vmem_limit_bytes=limit),
@@ -279,36 +367,46 @@
     bf16, f32 = jnp.bfloat16, jnp.float32
     rows, channels = key_rows.shape
     size = rows * CH
-    length_two = 2 * SEQ * size
+    short = size // 2
     everywhere = ("seq", "ch")
-    place = lax.axis_index("seq") % HALF
-
-    angles = np.arange(size)[:, None] * np.arange(size)[None, :] % size * (2.0 * np.pi / size)
+
+    angles = np.arange(short)[:, None] * np.arange(short)[None, :] % short * (2.0 * np.pi / short)
     dft = jnp.asarray(np.concatenate([np.cos(angles), np.sin(angles)], axis=1), bf16)
-    angles = np.arange(size)[:, None] * np.arange(2 * SEQ)[None, :] * (2.0 * np.pi / length_two)
-    table = np.stack([np.cos(angles), np.sin(angles)], axis=1).reshape(size, 2, 2, SEQ)
-    table = jnp.asarray(table.transpose(2, 0, 1, 3).reshape(2, size, 2 * SEQ), f32)
-
-    spec = [
-        lax.dynamic_slice_in_dim(spectrum, (place ^ member) * LANES, LANES, axis=3).astype(bf16)
-        for member in range(HALF)
-    ]
-    sends = call(product_kernel, "product", [key_rows, value_rows], [((DEVICES, rows, LANES), bf16)])[0]
+    table = lax.dynamic_index_in_dim(turn_table(size), lax.axis_index("seq") // HALF, 0, keepdims=False)
+
+    sends = call(
+        product_kernel,
+        "product",
+        [key_rows, value_rows],
+        [((DEVICES, rows, LANES), bf16)],
+        [pltpu.VMEM((rows, channels), bf16)] * 2 + [pltpu.SemaphoreType.DMA((2, CH))],
+        limit=56 * MIB,
+        hbm=(0, 1),
+    )[0]
+    spec, table = lax.optimization_barrier((members_of(spectrum), table))
     tokens = lax.all_to_all(sends, everywhere, split_axis=0, concat_axis=0, tiled=True).reshape(SEQ, size, LANES)
     spec = [spec[0]] + [swap(spec[member], "seq", member, SEQ) for member in range(1, HALF)]
     freq = call(
         forward_kernel,
         "forward",
         [tokens, table, dft],
-        [((size, SEQ * LANES), f32)] * 2,
-        [pltpu.VMEM((3 * size, SEQ * LANES), bf16)],
+        [((short, 2 * SEQ * LANES), f32)] * 2,
+        [pltpu.VMEM((3 * short, 2 * SEQ * LANES), bf16)],
+    )
+    back = ((HALF, short, 4 * LANES), f32)
+    early = call(
+        early_kernel,
+        "early_members",
+        [*[spec[member] for member in EARLY], *freq, dft],
+        [back] * 2,
+        [pltpu.VMEM((len(EARLY), 3 * short, 4 * LANES), bf16)],
     )
     shares = call(
-        inverse_kernel,
-        "inverse",
-        [*spec, *freq, table, dft],
+        late_kernel,
+        "late_member",
+        [*[spec[member] for member in LATE], *early, *freq, table, dft],
         [((SEQ, size, LANES), bf16)],
-        [pltpu.VMEM((3 * size, SEQ * LANES), bf16)] + [pltpu.VMEM((size, SEQ * LANES), f32)] * 2,
+        [pltpu.VMEM(*back)] * 2 + [pltpu.VMEM((len(LATE), 3 * short, 4 * LANES), bf16)],
     )[0].reshape(DEVICES, rows, LANES)
     field = lax.all_to_all(shares, everywhere, split_axis=0, concat_axis=0, tiled=True)
     return call(

time: 94.5 us -> 86.9 us (0.920)
  waiting for transfers between devices: 29 us -> 23 us
  blocking collectives: 31.6 us -> 29.8 us
  local copies, waits for them, and re-layouts: 5.76 us -> 7.31 us
  Pallas kernels: 17 us -> 15.6 us
    pallas_call x4 -> x5, Pallas kernels: 17 us -> 11.3 us  [call(): pl.pallas_call(kernel, out_shape=tuple((jax.ShapeDtypeStruct(shape, dtype...]
    all_to_all x1, waiting for transfers between devices: 19.2 us -> 13.6 us  [halves(): lax.all_to_all(sends, everywhere, split_axis=0, concat_axis=0, tiled=True)]
    squeeze x0 -> x1, local copies, waits for them, and re-layouts: none -> 4.94 us  [halves(): lax.dynamic_index_in_dim(turn_table(size), lax.axis_index('seq') // HALF,...]
    pallas_call x0 -> x1, Pallas kernels: none -> 4.29 us  [members_of(): pl.pallas_call(spectrum_kernel, grid_spec=pltpu.PrefetchScalarGridSpec(nu...]
    convert_element_type x1 -> x0, local copies, waits for them, and re-layouts: 3.54 us -> none  [halves(): lax.dynamic_slice_in_dim(spectrum, (place ^ member) * LANES, LANES, axis=3)]
    all_to_all x1, blocking collectives: 31.6 us -> 29.8 us  [halves(): lax.all_to_all(shares, everywhere, split_axis=0, concat_axis=0, tiled=True)]
  transfers between devices with their start and end apart: 4 -> 4, of which waited for: 3 -> 2; matrix products, arithmetic and copies ran while one was open for 4% -> 6% of each run, Pallas kernels for 7% -> 11%
where the time goes in v1:
time: 86.9 us; the launch traced here: 86.6 us
  blocking collectives  29.8 us (34%)
  waiting for transfers between devices  23 us (26%)
  Pallas kernels  15.6 us (18%)
  starting transfers between devices  10.8 us (12%)
  local copies, waits for them, and re-layouts  7.31 us (8%)
    all_to_all x1, blocking collectives, halves(): lax.all_to_all(shares, everywhere, split_axis=0, concat_axis=0, tiled=True)  29.8 us
    all_to_all x1, waiting for transfers between devices, halves(): lax.all_to_all(sends, everywhere, split_axis=0, concat_axis=0, tiled=True)  13.6 us
    pallas_call x5, Pallas kernels, call(): pl.pallas_call(kernel, out_shape=tuple((jax.ShapeDtypeStruct(shape, dtype...  11.3 us
    ppermute x3, waiting for transfers between devices, swap(): return lax.ppermute(array, axis, [(i, i ^ mask) for i in range(count)])  9.37 us
    all_to_all x1, starting transfers between devices, halves(): lax.all_to_all(sends, everywhere, split_axis=0, concat_axis=0, tiled=True)  7.3 us
    squeeze x1, local copies, waits for them, and re-layouts, halves(): lax.dynamic_index_in_dim(turn_table(size), lax.axis_index('seq') // HALF,...  4.94 us
    pallas_call x1, Pallas kernels, members_of(): pl.pallas_call(spectrum_kernel, grid_spec=pltpu.PrefetchScalarGridSpec(nu...  4.29 us
    ppermute x3, starting transfers between devices, swap(): return lax.ppermute(array, axis, [(i, i ^ mask) for i in range(count)])  3.49 us
  transfers between devices with their start and end apart: 4, of which 2 were waited for; matrix products, arithmetic and copies ran while one was open for 6% of the time, Pallas kernels for 11%

profile of v1, /device:TPU:0, one launch (start us, length us, event | category | flops | bytes accessed | tf_op | source)
XLA Modules:
  0.0 86.6 jit_solution(2045494623290964261)
XLA Ops:
  0.0 2.4 %product.1 = bf16[32,128,128]{2,1,0:T(8,128)(2,1)} custom-call(bf16[128,2048]{1,0:T(8,128)(2,1)} %key_ref.1, bf16[128,2048]{1,0:T(8,128)(2,1)} %value_ref.1), custom_call_target="tpu_custom_call" | custom-call | tf_op jit(solution)/shard_map/product/pallas_call | solution.py:355
  2.4 7.3 %all-to-all-start = ((bf16[32,128,128]{2,1,0:T(8,128)(2,1)}), bf16[32,128,128]{2,1,0:T(8,128)(2,1)S(1)}, u32[]{:S(2)}, u32[]{:S(2)}) async-start(bf16[32,128,128]{2,1,0:T(8,128)(2,1)} %product.1), calls=%async_computation | async-start | bytes 2097152 | tf_op jit(solution)/shard_map/all_to_all | solution.py:387
  9.7 4.3 %spectrum.1 = (bf16[2,2,2,256,128]{4,3,2,1,0:T(8,128)(2,1)}, bf16[2,2,2,256,128]{4,3,2,1,0:T(8,128)(2,1)}, bf16[2,2,2,256,128]{4,3,2,1,0:T(8,128)(2,1)}, bf16[2,2,2,256,128]{4,3,2,1,0:T(8,128)(2,1)}) custom-call(s32[1]{0:T(128)} %bitcast.1.place_ref, f32[2,2,512,512]{3,2,1,0:T(8,128)} %refs_3_.1, f32[2,2,512,512]{3,2,1,0:T(8,128)} %refs_3_.1, ...), custom_call_target="tpu_custom_call" | custom-call | tf_op jit(solution)/shard_map/spectrum/pallas_call | solution.py:170
  14.0 0.0 copy-start.2
  14.0 0.0 copy-start.5
  14.0 4.9 %dynamic-slice_bitcast_fusion.table.refs_5_ = f32[9,2,512,128]{3,2,1,0:T(8,128)} fusion(f32[2,9,2,512,128]{4,3,2,1,0:T(8,128)} %constant.41.clone, s32[]{:T(128)S(6)} %select_n.17), kind=kLoop, calls=%fused_computation | loop fusion | bytes 9437188 | tf_op jit(solution)/shard_map/jit(dynamic_index_in_dim)/squeeze | solution.py:375
  19.0 1.8 %collective-permute-start.1 = (bf16[2,2,2,256,128]{4,3,2,1,0:T(8,128)(2,1)}, bf16[2,2,2,256,128]{4,3,2,1,0:T(8,128)(2,1)S(1)}, u32[]{:S(2)}, u32[]{:S(2)}) collective-permute-start(bf16[2,2,2,256,128]{4,3,2,1,0:T(8,128)(2,1)} %get-tuple-element.24), channel_id=1, source_target_pairs={{0,4},{4,0},{8,12},{12,8},{16,20},{20,16},{24,28},{28,24},{1,5},{5... | collective-permute-start | bytes 1572872 | tf_op jit(solution)/shard_map/ppermute | solution.py:106
  20.7 1.5 %collective-permute-start.2 = (bf16[2,2,2,256,128]{4,3,2,1,0:T(8,128)(2,1)}, bf16[2,2,2,256,128]{4,3,2,1,0:T(8,128)(2,1)S(1)}, u32[]{:S(2)}, u32[]{:S(2)}) collective-permute-start(bf16[2,2,2,256,128]{4,3,2,1,0:T(8,128)(2,1)} %get-tuple-element.25), channel_id=1, source_target_pairs={{0,8},{4,12},{8,0},{12,4},{16,24},{20,28},{24,16},{28,20},{1,9},{5... | collective-permute-start | bytes 1572872 | tf_op jit(solution)/shard_map/ppermute | solution.py:106
  22.2 0.3 collective-permute-start
  22.5 13.6 %all-to-all-done = bf16[32,128,128]{2,1,0:T(8,128)(2,1)S(1)} async-done(((bf16[32,128,128]{2,1,0:T(8,128)(2,1)}), bf16[32,128,128]{2,1,0:T(8,128)(2,1)S(1)}, u32[]{:S(2)}, u32[]{:S(2)}) %all-to-all-start) | async-done | bytes 1048608 | tf_op jit(solution)/shard_map/all_to_all | solution.py:387
  36.1 0.0 copy-done.2
  36.1 0.0 copy-start
  36.1 2.3 %copy-done = f32[9,2,512,128]{3,2,1,0:T(8,128)S(1)} copy-done((f32[9,2,512,128]{3,2,1,0:T(8,128)S(1)}, f32[9,2,512,128]{3,2,1,0:T(8,128)}, u32[]{:S(2)}) %copy-start) | copy-done | bytes 4718616
  38.4 3.3 %forward.1 = (f32[256,2048]{1,0:T(8,128)S(1)}, f32[256,2048]{1,0:T(8,128)S(1)}) custom-call(bf16[8,512,128]{2,1,0:T(8,128)(2,1)S(1)} %bitcast.7, f32[9,2,512,128]{3,2,1,0:T(8,128)S(1)} %copy-done, bf16[256,512]{1,0:T(8,128)(2,1)S(1)} %copy-done.2), custom_call_target="tpu_custom_call" | custom-call | tf_op jit(solution)/shard_map/forward/pallas_call | solution.py:355
  41.7 0.0 copy-start.1
  41.7 0.0 collective-permute-done.1.refs_1_
  41.7 0.0 collective-permute-done.2.refs_2_
  41.7 0.0 copy-done.5
  41.7 1.7 %early_members.1 = (f32[4,256,512]{2,1,0:T(8,128)S(1)}, f32[4,256,512]{2,1,0:T(8,128)S(1)}) custom-call(bf16[2,2,2,256,128]{4,3,2,1,0:T(8,128)(2,1)S(1)} %copy-done.5, bf16[2,2,2,256,128]{4,3,2,1,0:T(8,128)(2,1)S(1)} %collective-permute-done.1.refs_1_, bf16[2,2,2,256,128]{4,3,2,1,0:T(8,128)(2,1)S(1)} %collective-permute-done.2.refs_2_, ...), custom_call_target="tpu_custom_call" | custom-call | tf_op jit(solution)/shard_map/early_members/pallas_call | solution.py:355
  43.4 9.4 %collective-permute-done.refs_0_ = bf16[2,2,2,256,128]{4,3,2,1,0:T(8,128)(2,1)S(1)} collective-permute-done((bf16[2,2,2,256,128]{4,3,2,1,0:T(8,128)(2,1)}, bf16[2,2,2,256,128]{4,3,2,1,0:T(8,128)(2,1)S(1)}, u32[]{:S(2)}, u32[]{:S(2)}) %collective-permute-start) | collective-permute-done | bytes 524320 | tf_op jit(solution)/shard_map/ppermute | solution.py:106
  52.8 0.0 copy-done.1
  52.8 0.0 copy-start.3
  52.8 0.0 copy-start.4
  52.8 0.0 copy-start.6
  52.8 0.0 copy-start.7
  52.8 2.7 %late_member.1 = bf16[8,512,128]{2,1,0:T(8,128)(2,1)S(1)} custom-call(bf16[2,2,2,256,128]{4,3,2,1,0:T(8,128)(2,1)S(1)} %collective-permute-done.refs_0_, f32[4,256,512]{2,1,0:T(8,128)S(1)} %get-tuple-element.29.refs_1_, f32[4,256,512]{2,1,0:T(8,128)S(1)} %get-tuple-element.30.refs_2_, f32[256,2048]{1,0:T(8,128)S(1)} %get-tuple-element.27.refs_3_, ...), custom_call_target="tpu_custom_call" | custom-call | tf_op jit(solution)/shard_map/late_member/pallas_call | solution.py:355
  55.5 29.8 %all_to_all.10.field_ref = bf16[32,128,128]{2,1,0:T(8,128)(2,1)S(1)} all-to-all(bf16[32,128,128]{2,1,0:T(8,128)(2,1)S(1)} %bitcast.6), channel_id=1, replica_groups=mesh['seq'=8,'ch'=4] {'seq','ch'}, dimensions={0} | all-to-all | bytes 2097152 | tf_op jit(solution)/shard_map/all_to_all | solution.py:411
  85.3 0.0 copy-done.3
  85.3 0.0 copy-done.4
  85.3 0.0 copy-done.6
  85.3 0.0 copy-done.7
  85.4 1.2 %gate.1 = bf16[128,2048]{1,0:T(8,128)(2,1)} custom-call(bf16[128,2048]{1,0:T(8,128)(2,1)S(1)} %copy-done.6, bf16[128,2048]{1,0:T(8,128)(2,1)S(1)} %copy-done.3, bf16[128,2048]{1,0:T(8,128)(2,1)S(1)} %copy-done.4, f32[1,2048]{1,0:T(1,128)S(1)} %bitcast.8, bf16[32,128,128]{2,1,0:T(8,128)(2,1)S(1)} %all_to_all.10.field_ref), custom_call_target="tpu_custom_call" | custom-call | tf_op jit(solution)/shard_map/gate/pallas_call | solution.py:355
Async XLA Ops:
  2.4 33.7 %all-to-all-start = ((bf16[32,128,128]{2,1,0:T(8,128)(2,1)}), bf16[32,128,128]{2,1,0:T(8,128)(2,1)S(1)}, u32[]{:S(2)}, u32[]{:S(2)}) async-start(bf16[32,128,128]{2,1,0:T(8,128)(2,1)} %product.1), calls=%async_computation | async-start | bytes 2097152 | tf_op jit(solution)/shard_map/all_to_all | solution.py:387
  14.0 22.0 %copy-start.2 = (bf16[256,512]{1,0:T(8,128)(2,1)S(1)}, bf16[256,512]{1,0:T(8,128)(2,1)}, u32[]{:S(2)}) copy-start(bf16[256,512]{1,0:T(8,128)(2,1)} %constant.40.clone.dft_ref.refs_5_.refs_6_) | copy-start | bytes 786436
  14.0 27.7 %copy-start.5 = (bf16[2,2,2,256,128]{4,3,2,1,0:T(8,128)(2,1)S(1)}, bf16[2,2,2,256,128]{4,3,2,1,0:T(8,128)(2,1)}, u32[]{:S(2)}) copy-start(bf16[2,2,2,256,128]{4,3,2,1,0:T(8,128)(2,1)} %get-tuple-element.23.refs_0_) | copy-start | bytes 1572868
  19.0 22.7 %collective-permute-start.1 = (bf16[2,2,2,256,128]{4,3,2,1,0:T(8,128)(2,1)}, bf16[2,2,2,256,128]{4,3,2,1,0:T(8,128)(2,1)S(1)}, u32[]{:S(2)}, u32[]{:S(2)}) collective-permute-start(bf16[2,2,2,256,128]{4,3,2,1,0:T(8,128)(2,1)} %get-tuple-element.24), channel_id=1, source_target_pairs={{0,4},{4,0},{8,12},{12,8},{16,20},{20,16},{24,28},{28,24},{1,5},{5... | collective-permute-start | bytes 1572872 | tf_op jit(solution)/shard_map/ppermute | solution.py:106
  20.7 20.9 %collective-permute-start.2 = (bf16[2,2,2,256,128]{4,3,2,1,0:T(8,128)(2,1)}, bf16[2,2,2,256,128]{4,3,2,1,0:T(8,128)(2,1)S(1)}, u32[]{:S(2)}, u32[]{:S(2)}) collective-permute-start(bf16[2,2,2,256,128]{4,3,2,1,0:T(8,128)(2,1)} %get-tuple-element.25), channel_id=1, source_target_pairs={{0,8},{4,12},{8,0},{12,4},{16,24},{20,28},{24,16},{28,20},{1,9},{5... | collective-permute-start | bytes 1572872 | tf_op jit(solution)/shard_map/ppermute | solution.py:106
  22.2 30.6 %collective-permute-start = (bf16[2,2,2,256,128]{4,3,2,1,0:T(8,128)(2,1)}, bf16[2,2,2,256,128]{4,3,2,1,0:T(8,128)(2,1)S(1)}, u32[]{:S(2)}, u32[]{:S(2)}) collective-permute-start(bf16[2,2,2,256,128]{4,3,2,1,0:T(8,128)(2,1)} %get-tuple-element.22), channel_id=1, source_target_pairs={{0,12},{4,8},{8,4},{12,0},{16,28},{20,24},{24,20},{28,16},{1,13},{... | collective-permute-start | bytes 1572872 | tf_op jit(solution)/shard_map/ppermute | solution.py:106
  36.1 2.3 %copy-start = (f32[9,2,512,128]{3,2,1,0:T(8,128)S(1)}, f32[9,2,512,128]{3,2,1,0:T(8,128)}, u32[]{:S(2)}) copy-start(f32[9,2,512,128]{3,2,1,0:T(8,128)} %dynamic-slice_bitcast_fusion.table.refs_5_) | copy-start | bytes 14155780
  41.7 11.1 %copy-start.1 = (f32[9,2,512,128]{3,2,1,0:T(8,128)S(1)}, f32[9,2,512,128]{3,2,1,0:T(8,128)}, u32[]{:S(2)}) copy-start(f32[9,2,512,128]{3,2,1,0:T(8,128)} %dynamic-slice_bitcast_fusion.table.refs_5_) | copy-start | bytes 14155780
  52.8 32.5 %copy-start.3 = (bf16[128,2048]{1,0:T(8,128)(2,1)S(1)}, bf16[128,2048]{1,0:T(8,128)(2,1)}, u32[]{:S(2)}) copy-start(bf16[128,2048]{1,0:T(8,128)(2,1)} %key_ref.1) | copy-start | bytes 1572868
  52.8 32.5 %copy-start.4 = (bf16[128,2048]{1,0:T(8,128)(2,1)S(1)}, bf16[128,2048]{1,0:T(8,128)(2,1)}, u32[]{:S(2)}) copy-start(bf16[128,2048]{1,0:T(8,128)(2,1)} %value_ref.1) | copy-start | bytes 1572868
  52.8 32.5 %copy-start.6 = (bf16[128,2048]{1,0:T(8,128)(2,1)S(1)}, bf16[128,2048]{1,0:T(8,128)(2,1)}, u32[]{:S(2)}) copy-start(bf16[128,2048]{1,0:T(8,128)(2,1)} %gate_ref.1) | copy-start | bytes 1572868
  52.8 32.5 %copy-start.7 = (f32[2048]{0:T(1024)S(1)}, f32[2048]{0:T(1024)}, u32[]{:S(2)}) copy-start(f32[2048]{0:T(1024)} %param.11) | copy-start | bytes 24580

commit v2 on v1

--- a/solution.py
+++ b/solution.py
@@ -97,7 +97,7 @@
 SEQ, CH, HALF = 8, 4, 4
 DEVICES = SEQ * CH
 ROOT = math.sqrt(0.5)
-EARLY, LATE = (0, 1, 2), (3,)
+EARLY, LATE = (0, 1, 3), (2,)
 VMEM = pl.BlockSpec(memory_space=pltpu.VMEM)
 STEP = 16
 
@@ -149,9 +149,10 @@
 
 
 def spectrum_kernel(place_ref, *refs):
-    spec, members = refs[:HALF], refs[HALF:]
+    count = len(refs) // 2
+    spec, members = refs[:count], refs[count:]
     rows = members[0].shape[3]
-    for member in range(HALF):
+    for member in range(count):
         for part in range(2):
             for odd in range(2):
                 for bit in range(2):
@@ -159,13 +160,13 @@
                     members[member][part, odd, bit] = values.astype(jnp.bfloat16)
 
 
-def members_of(spectrum, steps=4):
+def members_of(spectrum, which, steps=4):
     size = spectrum.shape[2]
     piece = size // steps
     place = (lax.axis_index("seq") % HALF).astype(jnp.int32).reshape(1)
     spec_blocks = [
         pl.BlockSpec((2, 2, piece, LANES), lambda i, place, member=member: (0, 0, i, place[0] ^ member))
-        for member in range(HALF)
+        for member in which
     ]
     return pl.pallas_call(
         spectrum_kernel,
@@ -173,12 +174,12 @@
             num_scalar_prefetch=1,
             grid=(steps,),
             in_specs=spec_blocks,
-            out_specs=[pl.BlockSpec((2, 2, 2, piece // 2, LANES), lambda i, place: (0, 0, 0, i, 0))] * HALF,
+            out_specs=[pl.BlockSpec((2, 2, 2, piece // 2, LANES), lambda i, place: (0, 0, 0, i, 0))] * len(which),
         ),
-        out_shape=[jax.ShapeDtypeStruct((2, 2, 2, size // 2, LANES), jnp.bfloat16)] * HALF,
+        out_shape=[jax.ShapeDtypeStruct((2, 2, 2, size // 2, LANES), jnp.bfloat16)] * len(which),
         compiler_params=pltpu.CompilerParams(vmem_limit_bytes=56 * MIB),
         name="spectrum",
-    )(place, *[spectrum] * HALF)
+    )(place, *[spectrum] * len(which))
 
 
 def four_real(a0, a1, a2, a3):
@@ -342,6 +343,12 @@
     lax.fori_loop(0, short // STEP, rows_of, 0)
 
 
+def table_kernel(after, table_hbm, table, sem):
+    copy = pltpu.make_async_copy(table_hbm.at[lax.axis_index("seq") // HALF], table, sem)
+    copy.start()
+    copy.wait()
+
+
 def gate_kernel(gate_ref, key_ref, value_ref, skip_ref, field_ref, out_ref):
     for device in range(DEVICES // 2):
         at = columns_of(device)
@@ -351,7 +358,7 @@
         out_ref[:, at] = gated.astype(jnp.bfloat16)
 
 
-def call(kernel, name, ins, outs, scratch=(), limit=24 * MIB, hbm=()):
+def call(kernel, name, ins, outs, scratch=(), limit=24 * MIB, hbm=(), cost=None):
     return pl.pallas_call(
         kernel,
         out_shape=tuple(jax.ShapeDtypeStruct(shape, dtype) for shape, dtype in outs),
@@ -359,6 +366,7 @@
         out_specs=tuple(VMEM for _ in outs),
         scratch_shapes=list(scratch),
         compiler_params=pltpu.CompilerParams(vmem_limit_bytes=limit),
+        cost_estimate=cost,
         name=name,
     )(*ins)
 
@@ -372,7 +380,7 @@
 
     angles = np.arange(short)[:, None] * np.arange(short)[None, :] % short * (2.0 * np.pi / short)
     dft = jnp.asarray(np.concatenate([np.cos(angles), np.sin(angles)], axis=1), bf16)
-    table = lax.dynamic_index_in_dim(turn_table(size), lax.axis_index("seq") // HALF, 0, keepdims=False)
+    table = turn_table(size)
 
     sends = call(
         product_kernel,
@@ -383,9 +391,21 @@
         limit=56 * MIB,
         hbm=(0, 1),
     )[0]
-    spec, table = lax.optimization_barrier((members_of(spectrum), table))
+    (last,) = members_of(spectrum, (3,), steps=2)
+    last = swap(last, "seq", 3, SEQ)
+    cost = pl.CostEstimate(flops=40000000000, bytes_accessed=1 << 20, transcendentals=0)
+    (table,) = call(
+        table_kernel,
+        "table",
+        [last, table],
+        [(table.shape[1:], f32)],
+        [pltpu.SemaphoreType.DMA],
+        hbm=(0, 1),
+        cost=cost,
+    )
+    spec = members_of(spectrum, (0, 1, 2))
     tokens = lax.all_to_all(sends, everywhere, split_axis=0, concat_axis=0, tiled=True).reshape(SEQ, size, LANES)
-    spec = [spec[0]] + [swap(spec[member], "seq", member, SEQ) for member in range(1, HALF)]
+    spec = [spec[0]] + [swap(spec[member], "seq", member, SEQ) for member in (1, 2)] + [last]
     freq = call(
         forward_kernel,
         "forward",

time: 86.9 us -> 81.7 us (0.940)
  waiting for transfers between devices: 23 us -> 13.4 us
  Pallas kernels: 15.6 us -> 17.5 us
  blocking collectives: 29.8 us -> 31 us
    ppermute x3, waiting for transfers between devices: 9.37 us -> 1.89 us  [swap(): return lax.ppermute(array, axis, [(i, i ^ mask) for i in range(count)])]
    unnamed x16 -> x20, local copies, waits for them, and re-layouts: 2.37 us -> 8.17 us
    squeeze x1 -> x0, local copies, waits for them, and re-layouts: 4.94 us -> none  [halves(): lax.dynamic_index_in_dim(turn_table(size), lax.axis_index('seq') // HALF,...]
    ppermute x3, starting transfers between devices: 3.49 us -> 7.19 us  [swap(): return lax.ppermute(array, axis, [(i, i ^ mask) for i in range(count)])]
    all_to_all x1, starting transfers between devices: 7.3 us -> 3.92 us  [halves(): lax.all_to_all(sends, everywhere, split_axis=0, concat_axis=0, tiled=True)]
    all_to_all x1, waiting for transfers between devices: 13.6 us -> 11.5 us  [halves(): lax.all_to_all(sends, everywhere, split_axis=0, concat_axis=0, tiled=True)]
    pallas_call x1 -> x2, Pallas kernels: 4.29 us -> 5.89 us  [members_of(): pl.pallas_call(spectrum_kernel, grid_spec=pltpu.PrefetchScalarGridSpec(nu...]
    all_to_all x1, blocking collectives: 29.8 us -> 31 us  [halves(): lax.all_to_all(shares, everywhere, split_axis=0, concat_axis=0, tiled=True)]
  transfers between devices with their start and end apart: 4 -> 4, of which waited for: 2 -> 3; matrix products, arithmetic and copies ran while one was open for 6% -> 0% of each run, Pallas kernels for 11% -> 14%
where the time goes in v2:
time: 81.7 us; the launch traced here: 81.3 us
  blocking collectives  31 us (38%)
  Pallas kernels  17.5 us (21%)
  waiting for transfers between devices  13.4 us (16%)
  starting transfers between devices  11.1 us (14%)
  local copies, waits for them, and re-layouts  8.17 us (10%)
    all_to_all x1, blocking collectives, halves(): lax.all_to_all(shares, everywhere, split_axis=0, concat_axis=0, tiled=True)  31 us
    pallas_call x6, Pallas kernels, call(): pl.pallas_call(kernel, out_shape=tuple((jax.ShapeDtypeStruct(shape, dtype...  11.6 us
    all_to_all x1, waiting for transfers between devices, halves(): lax.all_to_all(sends, everywhere, split_axis=0, concat_axis=0, tiled=True)  11.5 us
    unnamed x20, local copies, waits for them, and re-layouts  8.17 us
    ppermute x3, starting transfers between devices, swap(): return lax.ppermute(array, axis, [(i, i ^ mask) for i in range(count)])  7.19 us
    pallas_call x2, Pallas kernels, members_of(): pl.pallas_call(spectrum_kernel, grid_spec=pltpu.PrefetchScalarGridSpec(nu...  5.89 us
    all_to_all x1, starting transfers between devices, halves(): lax.all_to_all(sends, everywhere, split_axis=0, concat_axis=0, tiled=True)  3.92 us
    ppermute x3, waiting for transfers between devices, swap(): return lax.ppermute(array, axis, [(i, i ^ mask) for i in range(count)])  1.89 us
  transfers between devices with their start and end apart: 4, of which 3 were waited for; matrix products, arithmetic and copies ran while one was open for 0% of the time, Pallas kernels for 14%

profile of v2, /device:TPU:0, one launch (start us, length us, event | category | flops | bytes accessed | tf_op | source)
XLA Modules:
  0.0 81.3 jit_solution(7245553075343474833)
XLA Ops:
  0.0 2.0 %spectrum.3 = bf16[2,2,2,256,128]{4,3,2,1,0:T(8,128)(2,1)} custom-call(s32[1]{0:T(128)} %bitcast.1.place_ref, f32[2,2,512,512]{3,2,1,0:T(8,128)} %refs_0_.3), custom_call_target="tpu_custom_call" | custom-call | tf_op jit(solution)/shard_map/spectrum/pallas_call | solution.py:171
  2.0 4.0 %collective-permute-start.2 = (bf16[2,2,2,256,128]{4,3,2,1,0:T(8,128)(2,1)}, bf16[2,2,2,256,128]{4,3,2,1,0:T(8,128)(2,1)S(1)}, u32[]{:S(2)}, u32[]{:S(2)}) collective-permute-start(bf16[2,2,2,256,128]{4,3,2,1,0:T(8,128)(2,1)} %spectrum.3), channel_id=1, source_target_pairs={{0,12},{4,8},{8,4},{12,0},{16,28},{20,24},{24,20},{28,16},{1,13},{... | collective-permute-start | bytes 1572872 | tf_op jit(solution)/shard_map/ppermute | solution.py:106
  5.9 2.4 %product.1 = bf16[32,128,128]{2,1,0:T(8,128)(2,1)} custom-call(bf16[128,2048]{1,0:T(8,128)(2,1)} %key_ref.1, bf16[128,2048]{1,0:T(8,128)(2,1)} %value_ref.1), custom_call_target="tpu_custom_call" | custom-call | tf_op jit(solution)/shard_map/product/pallas_call | solution.py:362
  8.3 3.9 %all-to-all-start = ((bf16[32,128,128]{2,1,0:T(8,128)(2,1)}), bf16[32,128,128]{2,1,0:T(8,128)(2,1)S(1)}, u32[]{:S(2)}, u32[]{:S(2)}) async-start(bf16[32,128,128]{2,1,0:T(8,128)(2,1)} %product.1), calls=%async_computation | async-start | bytes 2097152 | tf_op jit(solution)/shard_map/all_to_all | solution.py:407
  12.2 3.9 %spectrum.2 = (bf16[2,2,2,256,128]{4,3,2,1,0:T(8,128)(2,1)}, bf16[2,2,2,256,128]{4,3,2,1,0:T(8,128)(2,1)}, bf16[2,2,2,256,128]{4,3,2,1,0:T(8,128)(2,1)}) custom-call(s32[1]{0:T(128)} %bitcast.1.place_ref, f32[2,2,512,512]{3,2,1,0:T(8,128)} %refs_0_.3, f32[2,2,512,512]{3,2,1,0:T(8,128)} %refs_0_.3, f32[2,2,512,512]{3,2,1,0:T(8,128)} %refs_0_.3), custom_call_target="tpu_custom_call" | custom-call | tf_op jit(solution)/shard_map/spectrum/pallas_call | solution.py:171
  16.2 1.8 %collective-permute-start = (bf16[2,2,2,256,128]{4,3,2,1,0:T(8,128)(2,1)}, bf16[2,2,2,256,128]{4,3,2,1,0:T(8,128)(2,1)S(1)}, u32[]{:S(2)}, u32[]{:S(2)}) collective-permute-start(bf16[2,2,2,256,128]{4,3,2,1,0:T(8,128)(2,1)} %get-tuple-element.12), channel_id=1, source_target_pairs={{0,8},{4,12},{8,0},{12,4},{16,24},{20,28},{24,16},{28,20},{1,9},{5... | collective-permute-start | bytes 1572872 | tf_op jit(solution)/shard_map/ppermute | solution.py:106
  17.9 0.0 copy-start.3
  17.9 1.5 %collective-permute-start.1 = (bf16[2,2,2,256,128]{4,3,2,1,0:T(8,128)(2,1)}, bf16[2,2,2,256,128]{4,3,2,1,0:T(8,128)(2,1)S(1)}, u32[]{:S(2)}, u32[]{:S(2)}) collective-permute-start(bf16[2,2,2,256,128]{4,3,2,1,0:T(8,128)(2,1)} %get-tuple-element.14), channel_id=1, source_target_pairs={{0,4},{4,0},{8,12},{12,8},{16,20},{20,16},{24,28},{28,24},{1,5},{5... | collective-permute-start | bytes 1572872 | tf_op jit(solution)/shard_map/ppermute | solution.py:106
  19.4 1.0 %collective-permute-done.2.after.refs_2_ = bf16[2,2,2,256,128]{4,3,2,1,0:T(8,128)(2,1)S(1)} collective-permute-done((bf16[2,2,2,256,128]{4,3,2,1,0:T(8,128)(2,1)}, bf16[2,2,2,256,128]{4,3,2,1,0:T(8,128)(2,1)S(1)}, u32[]{:S(2)}, u32[]{:S(2)}) %collective-permute-start.2) | collective-permute-done | bytes 524320 | tf_op jit(solution)/shard_map/ppermute | solution.py:106
  20.4 0.0 copy-start.9
  20.4 3.7 %copy-done.9 = f32[2,9,2,512,128]{4,3,2,1,0:T(8,128)S(1)} copy-done((f32[2,9,2,512,128]{4,3,2,1,0:T(8,128)S(1)}, f32[2,9,2,512,128]{4,3,2,1,0:T(8,128)}, u32[]{:S(2)}) %copy-start.9) | copy-done | bytes 9437208
  24.0 0.3 table.1.refs_5_
  24.4 0.0 copy-start
  24.4 2.1 %copy-done = f32[9,2,512,128]{3,2,1,0:T(8,128)} copy-done((f32[9,2,512,128]{3,2,1,0:T(8,128)}, f32[9,2,512,128]{3,2,1,0:T(8,128)S(1)}, u32[]{:S(2)}) %copy-start) | copy-done | bytes 4718616
  26.5 11.5 %all-to-all-done = bf16[32,128,128]{2,1,0:T(8,128)(2,1)S(1)} async-done(((bf16[32,128,128]{2,1,0:T(8,128)(2,1)}), bf16[32,128,128]{2,1,0:T(8,128)(2,1)S(1)}, u32[]{:S(2)}, u32[]{:S(2)}) %all-to-all-start) | async-done | bytes 1048608 | tf_op jit(solution)/shard_map/all_to_all | solution.py:407
  38.0 0.0 copy-done.3
  38.0 0.0 copy-start.1
  38.0 2.3 %copy-done.1 = f32[9,2,512,128]{3,2,1,0:T(8,128)S(1)} copy-done((f32[9,2,512,128]{3,2,1,0:T(8,128)S(1)}, f32[9,2,512,128]{3,2,1,0:T(8,128)}, u32[]{:S(2)}) %copy-start.1) | copy-done | bytes 4718616
  40.4 0.0 copy-start.6
  40.4 3.3 %forward.1 = (f32[256,2048]{1,0:T(8,128)S(1)}, f32[256,2048]{1,0:T(8,128)S(1)}) custom-call(bf16[8,512,128]{2,1,0:T(8,128)(2,1)S(1)} %bitcast.5, f32[9,2,512,128]{3,2,1,0:T(8,128)S(1)} %copy-done.1, bf16[256,512]{1,0:T(8,128)(2,1)S(1)} %copy-done.3), custom_call_target="tpu_custom_call" | custom-call | tf_op jit(solution)/shard_map/forward/pallas_call | solution.py:362
  43.7 0.0 collective-permute-done.1.refs_1_
  43.7 0.0 copy-done.6
  43.7 0.0 copy-start.2
  43.7 1.7 %early_members.1 = (f32[4,256,512]{2,1,0:T(8,128)S(1)}, f32[4,256,512]{2,1,0:T(8,128)S(1)}) custom-call(bf16[2,2,2,256,128]{4,3,2,1,0:T(8,128)(2,1)S(1)} %copy-done.6, bf16[2,2,2,256,128]{4,3,2,1,0:T(8,128)(2,1)S(1)} %collective-permute-done.1.refs_1_, bf16[2,2,2,256,128]{4,3,2,1,0:T(8,128)(2,1)S(1)} %collective-permute-done.2.after.refs_2_, ...), custom_call_target="tpu_custom_call" | custom-call | tf_op jit(solution)/shard_map/early_members/pallas_call | solution.py:362
  45.4 0.9 %collective-permute-done.refs_0_ = bf16[2,2,2,256,128]{4,3,2,1,0:T(8,128)(2,1)S(1)} collective-permute-done((bf16[2,2,2,256,128]{4,3,2,1,0:T(8,128)(2,1)}, bf16[2,2,2,256,128]{4,3,2,1,0:T(8,128)(2,1)S(1)}, u32[]{:S(2)}, u32[]{:S(2)}) %collective-permute-start) | collective-permute-done | bytes 524320 | tf_op jit(solution)/shard_map/ppermute | solution.py:106
  46.3 0.0 copy-done.2
  46.4 2.7 %late_member.1 = bf16[8,512,128]{2,1,0:T(8,128)(2,1)S(1)} custom-call(bf16[2,2,2,256,128]{4,3,2,1,0:T(8,128)(2,1)S(1)} %collective-permute-done.refs_0_, f32[4,256,512]{2,1,0:T(8,128)S(1)} %get-tuple-element.17.refs_1_, f32[4,256,512]{2,1,0:T(8,128)S(1)} %get-tuple-element.18.refs_2_, f32[256,2048]{1,0:T(8,128)S(1)} %get-tuple-element.15.refs_3_, ...), custom_call_target="tpu_custom_call" | custom-call | tf_op jit(solution)/shard_map/late_member/pallas_call | solution.py:362
  49.0 0.0 copy-start.4
  49.0 0.0 copy-start.5
  49.0 0.0 copy-start.7
  49.1 0.0 copy-start.8
  49.1 31.0 %all_to_all.10.field_ref = bf16[32,128,128]{2,1,0:T(8,128)(2,1)S(1)} all-to-all(bf16[32,128,128]{2,1,0:T(8,128)(2,1)S(1)} %bitcast.4), channel_id=1, replica_groups=mesh['seq'=8,'ch'=4] {'seq','ch'}, dimensions={0} | all-to-all | bytes 2097152 | tf_op jit(solution)/shard_map/all_to_all | solution.py:431
  80.0 0.0 copy-done.4
  80.0 0.0 copy-done.5
  80.0 0.0 copy-done.7
  80.0 0.0 copy-done.8
  80.0 1.2 %gate.1 = bf16[128,2048]{1,0:T(8,128)(2,1)} custom-call(bf16[128,2048]{1,0:T(8,128)(2,1)S(1)} %copy-done.7, bf16[128,2048]{1,0:T(8,128)(2,1)S(1)} %copy-done.4, bf16[128,2048]{1,0:T(8,128)(2,1)S(1)} %copy-done.5, f32[1,2048]{1,0:T(1,128)S(1)} %bitcast.6, bf16[32,128,128]{2,1,0:T(8,128)(2,1)S(1)} %all_to_all.10.field_ref), custom_call_target="tpu_custom_call" | custom-call | tf_op jit(solution)/shard_map/gate/pallas_call | solution.py:362
Async XLA Ops:
  2.0 18.4 %collective-permute-start.2 = (bf16[2,2,2,256,128]{4,3,2,1,0:T(8,128)(2,1)}, bf16[2,2,2,256,128]{4,3,2,1,0:T(8,128)(2,1)S(1)}, u32[]{:S(2)}, u32[]{:S(2)}) collective-permute-start(bf16[2,2,2,256,128]{4,3,2,1,0:T(8,128)(2,1)} %spectrum.3), channel_id=1, source_target_pairs={{0,12},{4,8},{8,4},{12,0},{16,28},{20,24},{24,20},{28,16},{1,13},{... | collective-permute-start | bytes 1572872 | tf_op jit(solution)/shard_map/ppermute | solution.py:106
  8.3 29.7 %all-to-all-start = ((bf16[32,128,128]{2,1,0:T(8,128)(2,1)}), bf16[32,128,128]{2,1,0:T(8,128)(2,1)S(1)}, u32[]{:S(2)}, u32[]{:S(2)}) async-start(bf16[32,128,128]{2,1,0:T(8,128)(2,1)} %product.1), calls=%async_computation | async-start | bytes 2097152 | tf_op jit(solution)/shard_map/all_to_all | solution.py:407
  16.2 30.2 %collective-permute-start = (bf16[2,2,2,256,128]{4,3,2,1,0:T(8,128)(2,1)}, bf16[2,2,2,256,128]{4,3,2,1,0:T(8,128)(2,1)S(1)}, u32[]{:S(2)}, u32[]{:S(2)}) collective-permute-start(bf16[2,2,2,256,128]{4,3,2,1,0:T(8,128)(2,1)} %get-tuple-element.12), channel_id=1, source_target_pairs={{0,8},{4,12},{8,0},{12,4},{16,24},{20,28},{24,16},{28,20},{1,9},{5... | collective-permute-start | bytes 1572872 | tf_op jit(solution)/shard_map/ppermute | solution.py:106
  17.9 20.1 %copy-start.3 = (bf16[256,512]{1,0:T(8,128)(2,1)S(1)}, bf16[256,512]{1,0:T(8,128)(2,1)}, u32[]{:S(2)}) copy-start(bf16[256,512]{1,0:T(8,128)(2,1)} %constant.25.clone.dft_ref.refs_5_.refs_6_) | copy-start | bytes 786436
  17.9 25.7 %collective-permute-start.1 = (bf16[2,2,2,256,128]{4,3,2,1,0:T(8,128)(2,1)}, bf16[2,2,2,256,128]{4,3,2,1,0:T(8,128)(2,1)S(1)}, u32[]{:S(2)}, u32[]{:S(2)}) collective-permute-start(bf16[2,2,2,256,128]{4,3,2,1,0:T(8,128)(2,1)} %get-tuple-element.14), channel_id=1, source_target_pairs={{0,4},{4,0},{8,12},{12,8},{16,20},{20,16},{24,28},{28,24},{1,5},{5... | collective-permute-start | bytes 1572872 | tf_op jit(solution)/shard_map/ppermute | solution.py:106
  20.4 3.7 %copy-start.9 = (f32[2,9,2,512,128]{4,3,2,1,0:T(8,128)S(1)}, f32[2,9,2,512,128]{4,3,2,1,0:T(8,128)}, u32[]{:S(2)}) copy-start(f32[2,9,2,512,128]{4,3,2,1,0:T(8,128)} %constant.26.clone.table_hbm) | copy-start | bytes 28311556
  24.4 2.1 %copy-start = (f32[9,2,512,128]{3,2,1,0:T(8,128)}, f32[9,2,512,128]{3,2,1,0:T(8,128)S(1)}, u32[]{:S(2)}) copy-start(f32[9,2,512,128]{3,2,1,0:T(8,128)S(1)} %table.1.refs_5_) | copy-start | bytes 14155780
  38.0 2.3 %copy-start.1 = (f32[9,2,512,128]{3,2,1,0:T(8,128)S(1)}, f32[9,2,512,128]{3,2,1,0:T(8,128)}, u32[]{:S(2)}) copy-start(f32[9,2,512,128]{3,2,1,0:T(8,128)} %copy-done) | copy-start | bytes 14155780
  40.4 3.3 %copy-start.6 = (bf16[2,2,2,256,128]{4,3,2,1,0:T(8,128)(2,1)S(1)}, bf16[2,2,2,256,128]{4,3,2,1,0:T(8,128)(2,1)}, u32[]{:S(2)}) copy-start(bf16[2,2,2,256,128]{4,3,2,1,0:T(8,128)(2,1)} %get-tuple-element.13.refs_0_) | copy-start | bytes 1572868
  43.7 2.7 %copy-start.2 = (f32[9,2,512,128]{3,2,1,0:T(8,128)S(1)}, f32[9,2,512,128]{3,2,1,0:T(8,128)}, u32[]{:S(2)}) copy-start(f32[9,2,512,128]{3,2,1,0:T(8,128)} %copy-done) | copy-start | bytes 14155780
  49.0 31.0 %copy-start.4 = (bf16[128,2048]{1,0:T(8,128)(2,1)S(1)}, bf16[128,2048]{1,0:T(8,128)(2,1)}, u32[]{:S(2)}) copy-start(bf16[128,2048]{1,0:T(8,128)(2,1)} %key_ref.1) | copy-start | bytes 1572868
  49.0 31.0 %copy-start.5 = (bf16[128,2048]{1,0:T(8,128)(2,1)S(1)}, bf16[128,2048]{1,0:T(8,128)(2,1)}, u32[]{:S(2)}) copy-start(bf16[128,2048]{1,0:T(8,128)(2,1)} %value_ref.1) | copy-start | bytes 1572868
  49.0 31.0 %copy-start.7 = (bf16[128,2048]{1,0:T(8,128)(2,1)S(1)}, bf16[128,2048]{1,0:T(8,128)(2,1)}, u32[]{:S(2)}) copy-start(bf16[128,2048]{1,0:T(8,128)(2,1)} %gate_ref.1) | copy-start | bytes 1572868
  49.1 31.0 %copy-start.8 = (f32[2048]{0:T(1024)S(1)}, f32[2048]{0:T(1024)}, u32[]{:S(2)}) copy-start(f32[2048]{0:T(1024)} %param.11) | copy-start | bytes 24580

commit v3 on v2

--- a/solution.py
+++ b/solution.py
@@ -98,7 +98,9 @@
 DEVICES = SEQ * CH
 ROOT = math.sqrt(0.5)
 EARLY, LATE = (0, 1, 3), (2,)
+NEAR = 64
 VMEM = pl.BlockSpec(memory_space=pltpu.VMEM)
+SMEM = pl.BlockSpec(memory_space=pltpu.SMEM)
 STEP = 16
 
 
@@ -243,30 +245,47 @@
     return jnp.asarray(np.repeat(table[..., None], LANES, axis=-1))
 
 
-def forward_kernel(tokens, table, dft_ref, re_ref, im_ref, stage):
+def split_table(size):
+    turns = np.arange(2 * SEQ).reshape(2, SEQ) / (2 * SEQ * size)
+    turns = 2 * np.pi * np.concatenate([turns, np.full((2, 1), 1 / size)], axis=1)
+    near, far = (turns[:, :, None] * tokens for tokens in (np.arange(NEAR), np.arange(0, size, NEAR)))
+    near = np.repeat(np.stack([np.cos(near), np.sin(near)], axis=2)[..., None], LANES, axis=-1)
+    far = np.stack([np.cos(far), np.sin(far)], axis=3).reshape(-1)
+    return jnp.asarray(near, jnp.float32), jnp.asarray(far, jnp.float32)
+
+
+def forward_kernel(tokens, near, far, dft_ref, re_ref, im_ref, stage):
+    half = lax.axis_index("seq") // HALF
     sign = sign_of_half()
     size = tokens.shape[1]
     short = size // 2
+    chunks = NEAR // STEP
+
+    def twiddle(j, a, at):
+        index = ((half * (SEQ + 1) + j) * (size // NEAR) + a) * 2
+        return times((near[j, 0, at, :], near[j, 1, at, :]), (far[index], far[index + 1]))
 
     def rows_of(index, carry):
+        a = index // chunks
+        near_at = rows_at(index % chunks)
         both = []
-        for first in (0, short):
-            at = rows_at(index, first)
+        for late in range(2):
+            at = rows_at(index, late * short)
             parts = residues_of([tokens[p, at, :].astype(jnp.float32) for p in range(SEQ)], sign)
             turned = []
             for j, (real, imag) in enumerate(parts):
-                cos, sin = table[j, 0, at, :], table[j, 1, at, :]
+                cos, sin = twiddle(j, a + late * (short // NEAR), near_at)
                 if imag is None:
                     turned.append((real * cos, -(real * sin)))
                 else:
                     turned.append((real * cos + imag * sin, imag * cos - real * sin))
             both.append(turned)
         at = rows_at(index)
-        cos, sin = table[SEQ, 0, at, :], table[SEQ, 1, at, :]
+        cos, sin = twiddle(SEQ, a, near_at)
         for j in range(SEQ):
-            a, b = both[0][j], both[1][j]
-            less = a[0] - b[0], a[1] - b[1]
-            pair = (a[0] + b[0], a[1] + b[1]), (less[0] * cos + less[1] * sin, less[1] * cos - less[0] * sin)
+            x, y = both[0][j], both[1][j]
+            less = x[0] - y[0], x[1] - y[1]
+            pair = (x[0] + y[0], x[1] + y[1]), (less[0] * cos + less[1] * sin, less[1] * cos - less[0] * sin)
             for bit, (real, imag) in enumerate(pair):
                 to = pl.ds((bit * SEQ + j) * LANES, LANES)
                 real = real.astype(jnp.bfloat16)
@@ -275,7 +294,7 @@
                 stage[rows_at(index, size), to] = -real
         return carry
 
-    lax.fori_loop(0, short // STEP, rows_of, 0)
+    lax.fori_loop(0, short // STEP, rows_of, 0, unroll=2)
     re_ref[...] = jnp.dot(dft_ref[...], stage[pl.ds(0, size), :], preferred_element_type=jnp.float32)
     im_ref[...] = jnp.dot(dft_ref[...], stage[pl.ds(short, size), :], preferred_element_type=jnp.float32)
 
@@ -340,33 +359,48 @@
                 out_ref[p, where, :] = (value * (scale * sign if p % 2 else scale)).astype(jnp.bfloat16)
         return carry
 
-    lax.fori_loop(0, short // STEP, rows_of, 0)
-
-
-def table_kernel(after, table_hbm, table, sem):
-    copy = pltpu.make_async_copy(table_hbm.at[lax.axis_index("seq") // HALF], table, sem)
-    copy.start()
-    copy.wait()
-
-
-def gate_kernel(gate_ref, key_ref, value_ref, skip_ref, field_ref, out_ref):
-    for device in range(DEVICES // 2):
-        at = columns_of(device)
-        product = (key_ref[:, at].astype(jnp.float32) * value_ref[:, at].astype(jnp.float32)).astype(jnp.bfloat16)
-        field = field_ref[device].astype(jnp.float32) + field_ref[device + DEVICES // 2].astype(jnp.float32)
-        gated = gate_ref[:, at].astype(jnp.float32) * (field + skip_ref[:, at] * product.astype(jnp.float32))
-        out_ref[:, at] = gated.astype(jnp.bfloat16)
-
-
-def call(kernel, name, ins, outs, scratch=(), limit=24 * MIB, hbm=(), cost=None):
+    lax.fori_loop(0, short // STEP, rows_of, 0, unroll=2)
+
+
+def table_kernel(after, table_hbm, near_hbm, table, near, sems):
+    half = lax.axis_index("seq") // HALF
+    copies = [
+        pltpu.make_async_copy(source.at[half], to, sems.at[index])
+        for index, (source, to) in enumerate(((table_hbm, table), (near_hbm, near)))
+    ]
+    for copy in copies:
+        copy.start()
+    for copy in copies:
+        copy.wait()
+
+
+def gate_kernel(gate_ref, key_ref, value_ref, skip_ref, field_ref, out_hbm, held, sems):
+    copies = []
+    for ch in range(CH):
+        for member in range(HALF):
+            device = member * CH + ch
+            at = columns_of(device)
+            product = (key_ref[:, at].astype(jnp.float32) * value_ref[:, at].astype(jnp.float32)).astype(jnp.bfloat16)
+            field = field_ref[device].astype(jnp.float32) + field_ref[device + DEVICES // 2].astype(jnp.float32)
+            gated = gate_ref[:, at].astype(jnp.float32) * (field + skip_ref[:, at] * product.astype(jnp.float32))
+            held[:, at] = gated.astype(jnp.bfloat16)
+        columns = pl.ds(ch * HALF * LANES, HALF * LANES)
+        copies.append(pltpu.make_async_copy(held.at[:, columns], out_hbm.at[:, columns], sems.at[ch]))
+        copies[-1].start()
+    for copy in copies:
+        copy.wait()
+
+
+def call(kernel, name, ins, outs, scratch=(), limit=24 * MIB, hbm=(), cost=None, aliases=None, to_hbm=False):
     return pl.pallas_call(
         kernel,
         out_shape=tuple(jax.ShapeDtypeStruct(shape, dtype) for shape, dtype in outs),
-        in_specs=[pl.BlockSpec(memory_space=pl.ANY) if index in hbm else VMEM for index, _ in enumerate(ins)],
-        out_specs=tuple(VMEM for _ in outs),
+        in_specs=[pl.BlockSpec(memory_space=pl.ANY) if index in hbm else SMEM if x.ndim == 1 else VMEM for index, x in enumerate(ins)],
+        out_specs=tuple(pl.BlockSpec(memory_space=pl.ANY) if to_hbm else VMEM for _ in outs),
         scratch_shapes=list(scratch),
         compiler_params=pltpu.CompilerParams(vmem_limit_bytes=limit),
         cost_estimate=cost,
+        input_output_aliases=aliases or {},
         name=name,
     )(*ins)
 
@@ -381,6 +415,7 @@
     angles = np.arange(short)[:, None] * np.arange(short)[None, :] % short * (2.0 * np.pi / short)
     dft = jnp.asarray(np.concatenate([np.cos(angles), np.sin(angles)], axis=1), bf16)
     table = turn_table(size)
+    near, far = split_table(size)
 
     sends = call(
         product_kernel,
@@ -394,13 +429,13 @@
     (last,) = members_of(spectrum, (3,), steps=2)
     last = swap(last, "seq", 3, SEQ)
     cost = pl.CostEstimate(flops=40000000000, bytes_accessed=1 << 20, transcendentals=0)
-    (table,) = call(
+    table, near = call(
         table_kernel,
         "table",
-        [last, table],
-        [(table.shape[1:], f32)],
-        [pltpu.SemaphoreType.DMA],
-        hbm=(0, 1),
+        [last, table, near],
+        [(table.shape[1:], f32), (near.shape[1:], f32)],
+        [pltpu.SemaphoreType.DMA((2,))],
+        hbm=(0, 1, 2),
         cost=cost,
     )
     spec = members_of(spectrum, (0, 1, 2))
@@ -409,7 +444,7 @@
     freq = call(
         forward_kernel,
         "forward",
-        [tokens, table, dft],
+        [tokens, near, far, dft],
         [((short, 2 * SEQ * LANES), f32)] * 2,
         [pltpu.VMEM((3 * short, 2 * SEQ * LANES), bf16)],
     )
@@ -434,6 +469,8 @@
         "gate",
         [gate_rows, key_rows, value_rows, skip_bias.reshape(1, channels), field],
         [((rows, channels), bf16)],
+        [pltpu.VMEM((rows, channels), bf16), pltpu.SemaphoreType.DMA((CH,))],
+        to_hbm=True,
     )[0]
 
 

time: 81.7 us -> 81.5 us (level)
  local copies, waits for them, and re-layouts: 8.17 us -> 5.84 us
  Pallas kernels: 17.5 us -> 19.7 us
    unnamed x20 -> x22, local copies, waits for them, and re-layouts: 8.17 us -> 5.84 us
    pallas_call x6, Pallas kernels: 11.6 us -> 13.7 us  [call(): pl.pallas_call(kernel, out_shape=tuple((jax.ShapeDtypeStruct(shape, dtype...]
  transfers between devices with their start and end apart: 4 -> 4, of which waited for: 3 -> 3; matrix products, arithmetic and copies ran while one was open for 0% -> 0% of each run, Pallas kernels for 14% -> 17%
where the time goes in v3:
time: 81.5 us; the launch traced here: 81.1 us
  blocking collectives  31 us (38%)
  Pallas kernels  19.7 us (24%)
  waiting for transfers between devices  13.4 us (16%)
  starting transfers between devices  11.1 us (14%)
  local copies, waits for them, and re-layouts  5.84 us (7%)
    all_to_all x1, blocking collectives, halves(): lax.all_to_all(shares, everywhere, split_axis=0, concat_axis=0, tiled=True)  31 us
    pallas_call x6, Pallas kernels, call(): pl.pallas_call(kernel, out_shape=tuple((jax.ShapeDtypeStruct(shape, dtype...  13.7 us
    all_to_all x1, waiting for transfers between devices, halves(): lax.all_to_all(sends, everywhere, split_axis=0, concat_axis=0, tiled=True)  11.4 us
    ppermute x3, starting transfers between devices, swap(): return lax.ppermute(array, axis, [(i, i ^ mask) for i in range(count)])  7.19 us
    pallas_call x2, Pallas kernels, members_of(): pl.pallas_call(spectrum_kernel, grid_spec=pltpu.PrefetchScalarGridSpec(nu...  5.98 us
    unnamed x22, local copies, waits for them, and re-layouts  5.84 us
    all_to_all x1, starting transfers between devices, halves(): lax.all_to_all(sends, everywhere, split_axis=0, concat_axis=0, tiled=True)  3.92 us
    ppermute x3, waiting for transfers between devices, swap(): return lax.ppermute(array, axis, [(i, i ^ mask) for i in range(count)])  1.94 us
  transfers between devices with their start and end apart: 4, of which 3 were waited for; matrix products, arithmetic and copies ran while one was open for 0% of the time, Pallas kernels for 17%

profile of v3, /device:TPU:0, one launch (start us, length us, event | category | flops | bytes accessed | tf_op | source)
XLA Modules:
  0.0 81.1 jit_solution(9509698291008103916)
XLA Ops:
  0.0 2.0 %spectrum.3 = bf16[2,2,2,256,128]{4,3,2,1,0:T(8,128)(2,1)} custom-call(s32[1]{0:T(128)} %bitcast.1.place_ref, f32[2,2,512,512]{3,2,1,0:T(8,128)} %refs_0_.3), custom_call_target="tpu_custom_call" | custom-call | tf_op jit(solution)/shard_map/spectrum/pallas_call | solution.py:173
  2.0 4.0 %collective-permute-start.2 = (bf16[2,2,2,256,128]{4,3,2,1,0:T(8,128)(2,1)}, bf16[2,2,2,256,128]{4,3,2,1,0:T(8,128)(2,1)S(1)}, u32[]{:S(2)}, u32[]{:S(2)}) collective-permute-start(bf16[2,2,2,256,128]{4,3,2,1,0:T(8,128)(2,1)} %spectrum.3), channel_id=1, source_target_pairs={{0,12},{4,8},{8,4},{12,0},{16,28},{20,24},{24,20},{28,16},{1,13},{... | collective-permute-start | bytes 1572872 | tf_op jit(solution)/shard_map/ppermute | solution.py:108
  5.9 2.4 %product.1 = bf16[32,128,128]{2,1,0:T(8,128)(2,1)} custom-call(bf16[128,2048]{1,0:T(8,128)(2,1)} %key_ref.1, bf16[128,2048]{1,0:T(8,128)(2,1)} %value_ref.1), custom_call_target="tpu_custom_call" | custom-call | tf_op jit(solution)/shard_map/product/pallas_call | solution.py:395
  8.3 3.9 %all-to-all-start = ((bf16[32,128,128]{2,1,0:T(8,128)(2,1)}), bf16[32,128,128]{2,1,0:T(8,128)(2,1)S(1)}, u32[]{:S(2)}, u32[]{:S(2)}) async-start(bf16[32,128,128]{2,1,0:T(8,128)(2,1)} %product.1), calls=%async_computation | async-start | bytes 2097152 | tf_op jit(solution)/shard_map/all_to_all | solution.py:442
  12.2 0.0 copy-start.10
  12.2 4.0 %spectrum.2 = (bf16[2,2,2,256,128]{4,3,2,1,0:T(8,128)(2,1)}, bf16[2,2,2,256,128]{4,3,2,1,0:T(8,128)(2,1)}, bf16[2,2,2,256,128]{4,3,2,1,0:T(8,128)(2,1)}) custom-call(s32[1]{0:T(128)} %bitcast.1.place_ref, f32[2,2,512,512]{3,2,1,0:T(8,128)} %refs_0_.3, f32[2,2,512,512]{3,2,1,0:T(8,128)} %refs_0_.3, f32[2,2,512,512]{3,2,1,0:T(8,128)} %refs_0_.3), custom_call_target="tpu_custom_call" | custom-call | tf_op jit(solution)/shard_map/spectrum/pallas_call | solution.py:173
  16.3 1.8 %collective-permute-start = (bf16[2,2,2,256,128]{4,3,2,1,0:T(8,128)(2,1)}, bf16[2,2,2,256,128]{4,3,2,1,0:T(8,128)(2,1)S(1)}, u32[]{:S(2)}, u32[]{:S(2)}) collective-permute-start(bf16[2,2,2,256,128]{4,3,2,1,0:T(8,128)(2,1)} %get-tuple-element.14), channel_id=1, source_target_pairs={{0,8},{4,12},{8,0},{12,4},{16,24},{20,28},{24,16},{28,20},{1,9},{5... | collective-permute-start | bytes 1572872 | tf_op jit(solution)/shard_map/ppermute | solution.py:108
  18.0 0.0 copy-start.2
  18.0 0.0 copy-start.8
  18.0 1.5 %collective-permute-start.1 = (bf16[2,2,2,256,128]{4,3,2,1,0:T(8,128)(2,1)}, bf16[2,2,2,256,128]{4,3,2,1,0:T(8,128)(2,1)}, u32[]{:S(2)}, u32[]{:S(2)}) collective-permute-start(bf16[2,2,2,256,128]{4,3,2,1,0:T(8,128)(2,1)} %get-tuple-element.16), channel_id=1, source_target_pairs={{0,4},{4,0},{8,12},{12,8},{16,20},{20,16},{24,28},{28,24},{1,5},{5... | collective-permute-start | bytes 1572872 | tf_op jit(solution)/shard_map/ppermute | solution.py:108
  19.5 0.8 %collective-permute-done.2.after.refs_2_ = bf16[2,2,2,256,128]{4,3,2,1,0:T(8,128)(2,1)S(1)} collective-permute-done((bf16[2,2,2,256,128]{4,3,2,1,0:T(8,128)(2,1)}, bf16[2,2,2,256,128]{4,3,2,1,0:T(8,128)(2,1)S(1)}, u32[]{:S(2)}, u32[]{:S(2)}) %collective-permute-start.2) | collective-permute-done | bytes 524320 | tf_op jit(solution)/shard_map/ppermute | solution.py:108
  20.3 0.0 copy-done.10
  20.3 0.0 copy-start.9
  20.3 3.7 %copy-done.9 = f32[2,9,2,512,128]{4,3,2,1,0:T(8,128)S(1)} copy-done((f32[2,9,2,512,128]{4,3,2,1,0:T(8,128)S(1)}, f32[2,9,2,512,128]{4,3,2,1,0:T(8,128)}, u32[]{:S(2)}) %copy-start.9) | copy-done | bytes 9437208
  24.0 0.5 table.1
  24.5 0.0 copy-start
  24.5 2.1 %copy-done = f32[9,2,512,128]{3,2,1,0:T(8,128)} copy-done((f32[9,2,512,128]{3,2,1,0:T(8,128)}, f32[9,2,512,128]{3,2,1,0:T(8,128)S(1)}, u32[]{:S(2)}) %copy-start) | copy-done | bytes 4718616
  26.6 0.0 copy-start.5
  26.6 11.4 %all-to-all-done = bf16[32,128,128]{2,1,0:T(8,128)(2,1)S(1)} async-done(((bf16[32,128,128]{2,1,0:T(8,128)(2,1)}), bf16[32,128,128]{2,1,0:T(8,128)(2,1)S(1)}, u32[]{:S(2)}, u32[]{:S(2)}) %all-to-all-start) | async-done | bytes 1048608 | tf_op jit(solution)/shard_map/all_to_all | solution.py:442
  38.0 0.0 copy-done.2
  38.0 0.0 copy-done.8
  38.0 4.2 %forward.1 = (f32[256,2048]{1,0:T(8,128)S(1)}, f32[256,2048]{1,0:T(8,128)S(1)}) custom-call(bf16[8,512,128]{2,1,0:T(8,128)(2,1)S(1)} %bitcast.5, f32[9,2,64,128]{3,2,1,0:T(8,128)S(1)} %get-tuple-element.17.near, f32[288]{0:T(512)S(1)} %copy-done.8, bf16[256,512]{1,0:T(8,128)(2,1)S(1)} %copy-done.2), custom_call_target="tpu_custom_call" | custom-call | tf_op jit(solution)/shard_map/forward/pallas_call | solution.py:395
  42.3 0.0 collective-permute-done.1.refs_1_
  42.3 0.0 copy-done.5
  42.3 0.0 copy-start.1
  42.3 2.9 %early_members.1 = (f32[4,256,512]{2,1,0:T(8,128)S(1)}, f32[4,256,512]{2,1,0:T(8,128)S(1)}) custom-call(bf16[2,2,2,256,128]{4,3,2,1,0:T(8,128)(2,1)S(1)} %copy-done.5, bf16[2,2,2,256,128]{4,3,2,1,0:T(8,128)(2,1)} %collective-permute-done.1.refs_1_, bf16[2,2,2,256,128]{4,3,2,1,0:T(8,128)(2,1)S(1)} %collective-permute-done.2.after.refs_2_, ...), custom_call_target="tpu_custom_call" | custom-call | tf_op jit(solution)/shard_map/early_members/pallas_call | solution.py:395
  45.2 1.1 %collective-permute-done.refs_0_ = bf16[2,2,2,256,128]{4,3,2,1,0:T(8,128)(2,1)S(1)} collective-permute-done((bf16[2,2,2,256,128]{4,3,2,1,0:T(8,128)(2,1)}, bf16[2,2,2,256,128]{4,3,2,1,0:T(8,128)(2,1)S(1)}, u32[]{:S(2)}, u32[]{:S(2)}) %collective-permute-start) | collective-permute-done | bytes 524320 | tf_op jit(solution)/shard_map/ppermute | solution.py:108
  46.3 0.0 copy-done.1
  46.3 2.6 %late_member.1 = bf16[8,512,128]{2,1,0:T(8,128)(2,1)S(1)} custom-call(bf16[2,2,2,256,128]{4,3,2,1,0:T(8,128)(2,1)S(1)} %collective-permute-done.refs_0_, f32[4,256,512]{2,1,0:T(8,128)S(1)} %get-tuple-element.20.refs_1_, f32[4,256,512]{2,1,0:T(8,128)S(1)} %get-tuple-element.21.refs_2_, f32[256,2048]{1,0:T(8,128)S(1)} %get-tuple-element.18.refs_3_, ...), custom_call_target="tpu_custom_call" | custom-call | tf_op jit(solution)/shard_map/late_member/pallas_call | solution.py:395
  48.9 0.0 copy-start.3
  48.9 0.0 copy-start.4
  48.9 0.0 copy-start.6
  48.9 0.0 copy-start.7
  49.0 31.0 %all_to_all.10.field_ref = bf16[32,128,128]{2,1,0:T(8,128)(2,1)S(1)} all-to-all(bf16[32,128,128]{2,1,0:T(8,128)(2,1)S(1)} %bitcast.4), channel_id=1, replica_groups=mesh['seq'=8,'ch'=4] {'seq','ch'}, dimensions={0} | all-to-all | bytes 2097152 | tf_op jit(solution)/shard_map/all_to_all | solution.py:466
  79.9 0.0 copy-done.3
  79.9 0.0 copy-done.4
  79.9 0.0 copy-done.6
  79.9 0.0 copy-done.7
  79.9 1.1 %gate.1 = bf16[128,2048]{1,0:T(8,128)(2,1)} custom-call(bf16[128,2048]{1,0:T(8,128)(2,1)S(1)} %copy-done.6, bf16[128,2048]{1,0:T(8,128)(2,1)S(1)} %copy-done.3, bf16[128,2048]{1,0:T(8,128)(2,1)S(1)} %copy-done.4, f32[1,2048]{1,0:T(1,128)S(1)} %bitcast.6, bf16[32,128,128]{2,1,0:T(8,128)(2,1)S(1)} %all_to_all.10.field_ref), custom_call_target="tpu_custom_call" | custom-call | tf_op jit(solution)/shard_map/gate/pallas_call | solution.py:395
Async XLA Ops:
  2.0 18.4 %collective-permute-start.2 = (bf16[2,2,2,256,128]{4,3,2,1,0:T(8,128)(2,1)}, bf16[2,2,2,256,128]{4,3,2,1,0:T(8,128)(2,1)S(1)}, u32[]{:S(2)}, u32[]{:S(2)}) collective-permute-start(bf16[2,2,2,256,128]{4,3,2,1,0:T(8,128)(2,1)} %spectrum.3), channel_id=1, source_target_pairs={{0,12},{4,8},{8,4},{12,0},{16,28},{20,24},{24,20},{28,16},{1,13},{... | collective-permute-start | bytes 1572872 | tf_op jit(solution)/shard_map/ppermute | solution.py:108
  8.3 29.7 %all-to-all-start = ((bf16[32,128,128]{2,1,0:T(8,128)(2,1)}), bf16[32,128,128]{2,1,0:T(8,128)(2,1)S(1)}, u32[]{:S(2)}, u32[]{:S(2)}) async-start(bf16[32,128,128]{2,1,0:T(8,128)(2,1)} %product.1), calls=%async_computation | async-start | bytes 2097152 | tf_op jit(solution)/shard_map/all_to_all | solution.py:442
  12.2 8.1 %copy-start.10 = (f32[2,9,2,64,128]{4,3,2,1,0:T(8,128)S(1)}, f32[2,9,2,64,128]{4,3,2,1,0:T(8,128)}, u32[]{:S(2)}) copy-start(f32[2,9,2,64,128]{4,3,2,1,0:T(8,128)} %constant.31.clone.near_hbm) | copy-start | bytes 3538948
  16.3 30.1 %collective-permute-start = (bf16[2,2,2,256,128]{4,3,2,1,0:T(8,128)(2,1)}, bf16[2,2,2,256,128]{4,3,2,1,0:T(8,128)(2,1)S(1)}, u32[]{:S(2)}, u32[]{:S(2)}) collective-permute-start(bf16[2,2,2,256,128]{4,3,2,1,0:T(8,128)(2,1)} %get-tuple-element.14), channel_id=1, source_target_pairs={{0,8},{4,12},{8,0},{12,4},{16,24},{20,28},{24,16},{28,20},{1,9},{5... | collective-permute-start | bytes 1572872 | tf_op jit(solution)/shard_map/ppermute | solution.py:108
  18.0 20.0 %copy-start.2 = (bf16[256,512]{1,0:T(8,128)(2,1)S(1)}, bf16[256,512]{1,0:T(8,128)(2,1)}, u32[]{:S(2)}) copy-start(bf16[256,512]{1,0:T(8,128)(2,1)} %constant.29.clone.dft_ref.refs_5_.refs_6_) | copy-start | bytes 786436
  18.0 20.0 %copy-start.8 = (f32[288]{0:T(512)S(1)}, f32[288]{0:T(512)}, u32[]{:S(2)}) copy-start(f32[288]{0:T(512)} %constant.32.clone.far) | copy-start | bytes 3460
  18.0 24.2 %collective-permute-start.1 = (bf16[2,2,2,256,128]{4,3,2,1,0:T(8,128)(2,1)}, bf16[2,2,2,256,128]{4,3,2,1,0:T(8,128)(2,1)}, u32[]{:S(2)}, u32[]{:S(2)}) collective-permute-start(bf16[2,2,2,256,128]{4,3,2,1,0:T(8,128)(2,1)} %get-tuple-element.16), channel_id=1, source_target_pairs={{0,4},{4,0},{8,12},{12,8},{16,20},{20,16},{24,28},{28,24},{1,5},{5... | collective-permute-start | bytes 1572872 | tf_op jit(solution)/shard_map/ppermute | solution.py:108
  20.3 3.7 %copy-start.9 = (f32[2,9,2,512,128]{4,3,2,1,0:T(8,128)S(1)}, f32[2,9,2,512,128]{4,3,2,1,0:T(8,128)}, u32[]{:S(2)}) copy-start(f32[2,9,2,512,128]{4,3,2,1,0:T(8,128)} %constant.30.clone.table_hbm) | copy-start | bytes 28311556
  24.5 2.1 %copy-start = (f32[9,2,512,128]{3,2,1,0:T(8,128)}, f32[9,2,512,128]{3,2,1,0:T(8,128)S(1)}, u32[]{:S(2)}) copy-start(f32[9,2,512,128]{3,2,1,0:T(8,128)S(1)} %get-tuple-element.22.refs_5_) | copy-start | bytes 14155780
  26.6 15.7 %copy-start.5 = (bf16[2,2,2,256,128]{4,3,2,1,0:T(8,128)(2,1)S(1)}, bf16[2,2,2,256,128]{4,3,2,1,0:T(8,128)(2,1)}, u32[]{:S(2)}) copy-start(bf16[2,2,2,256,128]{4,3,2,1,0:T(8,128)(2,1)} %get-tuple-element.15.refs_0_) | copy-start | bytes 1572868
  42.3 4.1 %copy-start.1 = (f32[9,2,512,128]{3,2,1,0:T(8,128)S(1)}, f32[9,2,512,128]{3,2,1,0:T(8,128)}, u32[]{:S(2)}) copy-start(f32[9,2,512,128]{3,2,1,0:T(8,128)} %copy-done) | copy-start | bytes 14155780
  48.9 31.0 %copy-start.3 = (bf16[128,2048]{1,0:T(8,128)(2,1)S(1)}, bf16[128,2048]{1,0:T(8,128)(2,1)}, u32[]{:S(2)}) copy-start(bf16[128,2048]{1,0:T(8,128)(2,1)} %key_ref.1) | copy-start | bytes 1572868
  48.9 31.0 %copy-start.4 = (bf16[128,2048]{1,0:T(8,128)(2,1)S(1)}, bf16[128,2048]{1,0:T(8,128)(2,1)}, u32[]{:S(2)}) copy-start(bf16[128,2048]{1,0:T(8,128)(2,1)} %value_ref.1) | copy-start | bytes 1572868
  48.9 31.0 %copy-start.6 = (bf16[128,2048]{1,0:T(8,128)(2,1)S(1)}, bf16[128,2048]{1,0:T(8,128)(2,1)}, u32[]{:S(2)}) copy-start(bf16[128,2048]{1,0:T(8,128)(2,1)} %gate_ref.1) | copy-start | bytes 1572868
  48.9 31.0 %copy-start.7 = (f32[2048]{0:T(1024)S(1)}, f32[2048]{0:T(1024)}, u32[]{:S(2)}) copy-start(f32[2048]{0:T(1024)} %param.13) | copy-start | bytes 24580

commit v4 on v3

--- a/solution.py
+++ b/solution.py
@@ -362,7 +362,7 @@
     lax.fori_loop(0, short // STEP, rows_of, 0, unroll=2)
 
 
-def table_kernel(after, table_hbm, near_hbm, table, near, sems):
+def table_kernel(member, table_hbm, near_hbm, table, near, out_ref, held, sems):
     half = lax.axis_index("seq") // HALF
     copies = [
         pltpu.make_async_copy(source.at[half], to, sems.at[index])
@@ -370,6 +370,12 @@
     ]
     for copy in copies:
         copy.start()
+    rows = out_ref.shape[3]
+    for part in range(2):
+        for odd in range(2):
+            held[...] = member[part, odd].astype(jnp.float32)
+            for bit in range(2):
+                out_ref[part, odd, bit] = held[pl.ds(bit, rows, stride=2), :].astype(jnp.bfloat16)
     for copy in copies:
         copy.wait()
 
@@ -426,16 +432,17 @@
         limit=56 * MIB,
         hbm=(0, 1),
     )[0]
-    (last,) = members_of(spectrum, (3,), steps=2)
+    opposite = lax.axis_index("seq") % HALF ^ 3
+    last = lax.dynamic_slice_in_dim(spectrum, opposite * LANES, LANES, axis=3).astype(bf16)
     last = swap(last, "seq", 3, SEQ)
     cost = pl.CostEstimate(flops=40000000000, bytes_accessed=1 << 20, transcendentals=0)
-    table, near = call(
+    table, near, last = call(
         table_kernel,
         "table",
         [last, table, near],
-        [(table.shape[1:], f32), (near.shape[1:], f32)],
-        [pltpu.SemaphoreType.DMA((2,))],
-        hbm=(0, 1, 2),
+        [(table.shape[1:], f32), (near.shape[1:], f32), ((2, 2, 2, short, LANES), bf16)],
+        [pltpu.VMEM((size, LANES), f32), pltpu.SemaphoreType.DMA((2,))],
+        hbm=(1, 2),
         cost=cost,
     )
     spec = members_of(spectrum, (0, 1, 2))

time: 81.5 us -> 80.7 us (level)
  local copies, waits for them, and re-layouts: 5.84 us -> 9.79 us
  Pallas kernels: 19.7 us -> 16.6 us
  waiting for transfers between devices: 13.4 us -> 11.6 us
    all_to_all x1, waiting for transfers between devices: 11.4 us -> 8.66 us  [halves(): lax.all_to_all(sends, everywhere, split_axis=0, concat_axis=0, tiled=True)]
    unnamed x22 -> x30, local copies, waits for them, and re-layouts: 5.84 us -> 8.5 us
    pallas_call x2 -> x1, Pallas kernels: 5.98 us -> 4.03 us  [members_of(): pl.pallas_call(spectrum_kernel, grid_spec=pltpu.PrefetchScalarGridSpec(nu...]
    convert_element_type x0 -> x1, local copies, waits for them, and re-layouts: none -> 1.29 us  [halves(): lax.dynamic_slice_in_dim(spectrum, opposite * LANES, LANES, axis=3)]
    pallas_call x6, Pallas kernels: 13.7 us -> 12.6 us  [call(): pl.pallas_call(kernel, out_shape=tuple((jax.ShapeDtypeStruct(shape, dtype...]
    ppermute x3, waiting for transfers between devices: 1.94 us -> 2.9 us  [swap(): return lax.ppermute(array, axis, [(i, i ^ mask) for i in range(count)])]
  transfers between devices with their start and end apart: 4 -> 4, of which waited for: 3 -> 3; matrix products, arithmetic and copies ran while one was open for 0% -> 0% of each run, Pallas kernels for 17% -> 16%
where the time goes in v4:
time: 80.7 us; the launch traced here: 80.3 us
  blocking collectives  30.9 us (38%)
  Pallas kernels  16.6 us (21%)
  waiting for transfers between devices  11.6 us (14%)
  starting transfers between devices  11.2 us (14%)
  local copies, waits for them, and re-layouts  9.79 us (12%)
    all_to_all x1, blocking collectives, halves(): lax.all_to_all(shares, everywhere, split_axis=0, concat_axis=0, tiled=True)  30.9 us
    pallas_call x6, Pallas kernels, call(): pl.pallas_call(kernel, out_shape=tuple((jax.ShapeDtypeStruct(shape, dtype...  12.6 us
    all_to_all x1, waiting for transfers between devices, halves(): lax.all_to_all(sends, everywhere, split_axis=0, concat_axis=0, tiled=True)  8.66 us
    unnamed x30, local copies, waits for them, and re-layouts  8.5 us
    ppermute x3, starting transfers between devices, swap(): return lax.ppermute(array, axis, [(i, i ^ mask) for i in range(count)])  7.25 us
    pallas_call x1, Pallas kernels, members_of(): pl.pallas_call(spectrum_kernel, grid_spec=pltpu.PrefetchScalarGridSpec(nu...  4.03 us
    all_to_all x1, starting transfers between devices, halves(): lax.all_to_all(sends, everywhere, split_axis=0, concat_axis=0, tiled=True)  3.92 us
    ppermute x3, waiting for transfers between devices, swap(): return lax.ppermute(array, axis, [(i, i ^ mask) for i in range(count)])  2.9 us
  transfers between devices with their start and end apart: 4, of which 3 were waited for; matrix products, arithmetic and copies ran while one was open for 0% of the time, Pallas kernels for 16%

profile of v4, /device:TPU:0, one launch (start us, length us, event | category | flops | bytes accessed | tf_op | source)
XLA Modules:
  0.0 80.3 jit_solution(5363950447172625409)
XLA Ops:
  0.0 1.3 %dynamic-slice_convert_fusion = bf16[2,2,512,128]{3,2,1,0:T(8,128)(2,1)S(1)} fusion(f32[2,2,512,512]{3,2,1,0:T(8,128)} %refs_2_.1, s32[]{:T(128)S(6)} %select_n.13), kind=kLoop, calls=%fused_computation | loop fusion | bytes 1048580 | tf_op jit(solution)/shard_map/convert_element_type | solution.py:436
  1.3 4.0 %collective-permute-start.2 = (bf16[2,2,512,128]{3,2,1,0:T(8,128)(2,1)S(1)}, bf16[2,2,512,128]{3,2,1,0:T(8,128)(2,1)S(1)}, u32[]{:S(2)}, u32[]{:S(2)}) collective-permute-start(bf16[2,2,512,128]{3,2,1,0:T(8,128)(2,1)S(1)} %dynamic-slice_convert_fusion), channel_id=1, source_target_pairs={{0,12},{4,8},{8,4},{12,0},{16,28},{20,24},{24,20},{28,16},{1,13},{... | collective-permute-start | bytes 1572872 | tf_op jit(solution)/shard_map/ppermute | solution.py:108
  5.3 2.4 %product.1 = bf16[32,128,128]{2,1,0:T(8,128)(2,1)} custom-call(bf16[128,2048]{1,0:T(8,128)(2,1)} %key_ref.1, bf16[128,2048]{1,0:T(8,128)(2,1)} %value_ref.1), custom_call_target="tpu_custom_call" | custom-call | tf_op jit(solution)/shard_map/product/pallas_call | solution.py:401
  7.7 3.9 %all-to-all-start = ((bf16[32,128,128]{2,1,0:T(8,128)(2,1)}), bf16[32,128,128]{2,1,0:T(8,128)(2,1)S(1)}, u32[]{:S(2)}, u32[]{:S(2)}) async-start(bf16[32,128,128]{2,1,0:T(8,128)(2,1)} %product.1), calls=%async_computation | async-start | bytes 2097152 | tf_op jit(solution)/shard_map/all_to_all | solution.py:449
  11.6 0.0 copy-start.14
  11.6 4.0 %spectrum.1 = (bf16[2,2,2,256,128]{4,3,2,1,0:T(8,128)(2,1)}, bf16[2,2,2,256,128]{4,3,2,1,0:T(8,128)(2,1)}, bf16[2,2,2,256,128]{4,3,2,1,0:T(8,128)(2,1)}) custom-call(s32[1]{0:T(128)} %bitcast.1.place_ref, f32[2,2,512,512]{3,2,1,0:T(8,128)} %refs_2_.1, f32[2,2,512,512]{3,2,1,0:T(8,128)} %refs_2_.1, f32[2,2,512,512]{3,2,1,0:T(8,128)} %refs_2_.1), custom_call_target="tpu_custom_call" | custom-call | tf_op jit(solution)/shard_map/spectrum/pallas_call | solution.py:173
  15.7 1.8 %collective-permute-start = (bf16[2,2,2,256,128]{4,3,2,1,0:T(8,128)(2,1)}, bf16[2,2,2,256,128]{4,3,2,1,0:T(8,128)(2,1)S(1)}, u32[]{:S(2)}, u32[]{:S(2)}) collective-permute-start(bf16[2,2,2,256,128]{4,3,2,1,0:T(8,128)(2,1)} %get-tuple-element.15), channel_id=1, source_target_pairs={{0,8},{4,12},{8,0},{12,4},{16,24},{20,28},{24,16},{28,20},{1,9},{5... | collective-permute-start | bytes 1572872 | tf_op jit(solution)/shard_map/ppermute | solution.py:108
  17.4 0.0 copy-start.2
  17.4 0.0 copy-start.10
  17.4 1.5 %collective-permute-start.1 = (bf16[2,2,2,256,128]{4,3,2,1,0:T(8,128)(2,1)}, bf16[2,2,2,256,128]{4,3,2,1,0:T(8,128)(2,1)S(1)}, u32[]{:S(2)}, u32[]{:S(2)}) collective-permute-start(bf16[2,2,2,256,128]{4,3,2,1,0:T(8,128)(2,1)} %get-tuple-element.17), channel_id=1, source_target_pairs={{0,4},{4,0},{8,12},{12,8},{16,20},{20,16},{24,28},{28,24},{1,5},{5... | collective-permute-start | bytes 1572872 | tf_op jit(solution)/shard_map/ppermute | solution.py:108
  18.9 0.6 collective-permute-done.2.member
  19.5 0.0 copy-start.11
  19.5 0.8 copy-done.11
  20.3 0.0 copy-done.14
  20.3 0.0 copy-start.12
  20.3 1.0 %copy-done.12 = bf16[2,2,512,128]{3,2,1,0:T(8,128)(2,1)S(1)} copy-done((bf16[2,2,512,128]{3,2,1,0:T(8,128)(2,1)S(1)}, bf16[2,2,512,128]{3,2,1,0:T(8,128)(2,1)}, u32[]{:S(2)}) %copy-start.12) | copy-done | bytes 524312
  21.4 0.0 copy-start.13
  21.4 3.7 %copy-done.13 = f32[2,9,2,512,128]{4,3,2,1,0:T(8,128)S(1)} copy-done((f32[2,9,2,512,128]{4,3,2,1,0:T(8,128)S(1)}, f32[2,9,2,512,128]{4,3,2,1,0:T(8,128)}, u32[]{:S(2)}) %copy-start.13) | copy-done | bytes 9437208
  25.0 0.6 table.1
  25.6 0.0 copy-start
  25.6 2.1 %copy-done = f32[9,2,512,128]{3,2,1,0:T(8,128)} copy-done((f32[9,2,512,128]{3,2,1,0:T(8,128)}, f32[9,2,512,128]{3,2,1,0:T(8,128)S(1)}, u32[]{:S(2)}) %copy-start) | copy-done | bytes 4718616
  27.8 0.0 copy-start.6
  27.8 0.8 copy-done.6
  28.6 0.0 copy-start.5
  28.6 8.7 %all-to-all-done = bf16[32,128,128]{2,1,0:T(8,128)(2,1)S(1)} async-done(((bf16[32,128,128]{2,1,0:T(8,128)(2,1)}), bf16[32,128,128]{2,1,0:T(8,128)(2,1)S(1)}, u32[]{:S(2)}, u32[]{:S(2)}) %all-to-all-start) | async-done | bytes 1048608 | tf_op jit(solution)/shard_map/all_to_all | solution.py:449
  37.2 0.0 copy-start.7
  37.2 0.0 copy-done.2
  37.2 0.0 copy-done.10
  37.2 4.2 %forward.1 = (f32[256,2048]{1,0:T(8,128)S(1)}, f32[256,2048]{1,0:T(8,128)S(1)}) custom-call(bf16[8,512,128]{2,1,0:T(8,128)(2,1)S(1)} %bitcast.5, f32[9,2,64,128]{3,2,1,0:T(8,128)S(1)} %get-tuple-element.19.near, f32[288]{0:T(512)S(1)} %copy-done.10, bf16[256,512]{1,0:T(8,128)(2,1)S(1)} %copy-done.2), custom_call_target="tpu_custom_call" | custom-call | tf_op jit(solution)/shard_map/forward/pallas_call | solution.py:401
  41.5 0.0 collective-permute-done.1.refs_1_
  41.5 0.0 copy-done.5
  41.5 0.0 copy-done.7
  41.5 0.0 copy-start.1
  41.5 1.7 %early_members.1 = (f32[4,256,512]{2,1,0:T(8,128)S(1)}, f32[4,256,512]{2,1,0:T(8,128)S(1)}) custom-call(bf16[2,2,2,256,128]{4,3,2,1,0:T(8,128)(2,1)S(1)} %copy-done.5, bf16[2,2,2,256,128]{4,3,2,1,0:T(8,128)(2,1)S(1)} %collective-permute-done.1.refs_1_, bf16[2,2,2,256,128]{4,3,2,1,0:T(8,128)(2,1)S(1)} %copy-done.7, ...), custom_call_target="tpu_custom_call" | custom-call | tf_op jit(solution)/shard_map/early_members/pallas_call | solution.py:401
  43.2 2.3 %collective-permute-done.refs_0_ = bf16[2,2,2,256,128]{4,3,2,1,0:T(8,128)(2,1)S(1)} collective-permute-done((bf16[2,2,2,256,128]{4,3,2,1,0:T(8,128)(2,1)}, bf16[2,2,2,256,128]{4,3,2,1,0:T(8,128)(2,1)S(1)}, u32[]{:S(2)}, u32[]{:S(2)}) %collective-permute-start) | collective-permute-done | bytes 524320 | tf_op jit(solution)/shard_map/ppermute | solution.py:108
  45.5 0.0 copy-done.1
  45.5 2.6 %late_member.1 = bf16[8,512,128]{2,1,0:T(8,128)(2,1)S(1)} custom-call(bf16[2,2,2,256,128]{4,3,2,1,0:T(8,128)(2,1)S(1)} %collective-permute-done.refs_0_, f32[4,256,512]{2,1,0:T(8,128)S(1)} %get-tuple-element.22.refs_1_, f32[4,256,512]{2,1,0:T(8,128)S(1)} %get-tuple-element.23.refs_2_, f32[256,2048]{1,0:T(8,128)S(1)} %get-tuple-element.20.refs_3_, ...), custom_call_target="tpu_custom_call" | custom-call | tf_op jit(solution)/shard_map/late_member/pallas_call | solution.py:401
  48.1 0.0 copy-start.3
  48.1 0.0 copy-start.4
  48.1 0.0 copy-start.8
  48.1 0.0 copy-start.9
  48.2 30.9 %all_to_all.10.field_ref = bf16[32,128,128]{2,1,0:T(8,128)(2,1)S(1)} all-to-all(bf16[32,128,128]{2,1,0:T(8,128)(2,1)S(1)} %bitcast.4), channel_id=1, replica_groups=mesh['seq'=8,'ch'=4] {'seq','ch'}, dimensions={0} | all-to-all | bytes 2097152 | tf_op jit(solution)/shard_map/all_to_all | solution.py:473
  79.1 0.0 copy-done.3
  79.1 0.0 copy-done.4
  79.1 0.0 copy-done.8
  79.1 0.0 copy-done.9
  79.1 1.1 %gate.1 = bf16[128,2048]{1,0:T(8,128)(2,1)} custom-call(bf16[128,2048]{1,0:T(8,128)(2,1)S(1)} %copy-done.8, bf16[128,2048]{1,0:T(8,128)(2,1)S(1)} %copy-done.3, bf16[128,2048]{1,0:T(8,128)(2,1)S(1)} %copy-done.4, f32[1,2048]{1,0:T(1,128)S(1)} %bitcast.6, bf16[32,128,128]{2,1,0:T(8,128)(2,1)S(1)} %all_to_all.10.field_ref), custom_call_target="tpu_custom_call" | custom-call | tf_op jit(solution)/shard_map/gate/pallas_call | solution.py:401
Async XLA Ops:
  1.3 18.2 %collective-permute-start.2 = (bf16[2,2,512,128]{3,2,1,0:T(8,128)(2,1)S(1)}, bf16[2,2,512,128]{3,2,1,0:T(8,128)(2,1)S(1)}, u32[]{:S(2)}, u32[]{:S(2)}) collective-permute-start(bf16[2,2,512,128]{3,2,1,0:T(8,128)(2,1)S(1)} %dynamic-slice_convert_fusion), channel_id=1, source_target_pairs={{0,12},{4,8},{8,4},{12,0},{16,28},{20,24},{24,20},{28,16},{1,13},{... | collective-permute-start | bytes 1572872 | tf_op jit(solution)/shard_map/ppermute | solution.py:108
  7.7 29.5 %all-to-all-start = ((bf16[32,128,128]{2,1,0:T(8,128)(2,1)}), bf16[32,128,128]{2,1,0:T(8,128)(2,1)S(1)}, u32[]{:S(2)}, u32[]{:S(2)}) async-start(bf16[32,128,128]{2,1,0:T(8,128)(2,1)} %product.1), calls=%async_computation | async-start | bytes 2097152 | tf_op jit(solution)/shard_map/all_to_all | solution.py:449
  11.6 8.7 %copy-start.14 = (f32[2,9,2,64,128]{4,3,2,1,0:T(8,128)S(1)}, f32[2,9,2,64,128]{4,3,2,1,0:T(8,128)}, u32[]{:S(2)}) copy-start(f32[2,9,2,64,128]{4,3,2,1,0:T(8,128)} %constant.37.clone.near_hbm) | copy-start | bytes 3538948
  15.7 29.9 %collective-permute-start = (bf16[2,2,2,256,128]{4,3,2,1,0:T(8,128)(2,1)}, bf16[2,2,2,256,128]{4,3,2,1,0:T(8,128)(2,1)S(1)}, u32[]{:S(2)}, u32[]{:S(2)}) collective-permute-start(bf16[2,2,2,256,128]{4,3,2,1,0:T(8,128)(2,1)} %get-tuple-element.15), channel_id=1, source_target_pairs={{0,8},{4,12},{8,0},{12,4},{16,24},{20,28},{24,16},{28,20},{1,9},{5... | collective-permute-start | bytes 1572872 | tf_op jit(solution)/shard_map/ppermute | solution.py:108
  17.4 19.8 %copy-start.2 = (bf16[256,512]{1,0:T(8,128)(2,1)S(1)}, bf16[256,512]{1,0:T(8,128)(2,1)}, u32[]{:S(2)}) copy-start(bf16[256,512]{1,0:T(8,128)(2,1)} %constant.35.clone.dft_ref.refs_5_.refs_6_) | copy-start | bytes 786436
  17.4 19.8 %copy-start.10 = (f32[288]{0:T(512)S(1)}, f32[288]{0:T(512)}, u32[]{:S(2)}) copy-start(f32[288]{0:T(512)} %constant.38.clone.far) | copy-start | bytes 3460
  17.4 24.0 %collective-permute-start.1 = (bf16[2,2,2,256,128]{4,3,2,1,0:T(8,128)(2,1)}, bf16[2,2,2,256,128]{4,3,2,1,0:T(8,128)(2,1)S(1)}, u32[]{:S(2)}, u32[]{:S(2)}) collective-permute-start(bf16[2,2,2,256,128]{4,3,2,1,0:T(8,128)(2,1)} %get-tuple-element.17), channel_id=1, source_target_pairs={{0,4},{4,0},{8,12},{12,8},{16,20},{20,16},{24,28},{28,24},{1,5},{5... | collective-permute-start | bytes 1572872 | tf_op jit(solution)/shard_map/ppermute | solution.py:108
  19.5 0.8 copy-start.11
  20.3 1.0 %copy-start.12 = (bf16[2,2,512,128]{3,2,1,0:T(8,128)(2,1)S(1)}, bf16[2,2,512,128]{3,2,1,0:T(8,128)(2,1)}, u32[]{:S(2)}) copy-start(bf16[2,2,512,128]{3,2,1,0:T(8,128)(2,1)} %copy-done.11) | copy-start | bytes 1572868
  21.4 3.7 %copy-start.13 = (f32[2,9,2,512,128]{4,3,2,1,0:T(8,128)S(1)}, f32[2,9,2,512,128]{4,3,2,1,0:T(8,128)}, u32[]{:S(2)}) copy-start(f32[2,9,2,512,128]{4,3,2,1,0:T(8,128)} %constant.36.clone.table_hbm) | copy-start | bytes 28311556
  25.6 2.1 %copy-start = (f32[9,2,512,128]{3,2,1,0:T(8,128)}, f32[9,2,512,128]{3,2,1,0:T(8,128)S(1)}, u32[]{:S(2)}) copy-start(f32[9,2,512,128]{3,2,1,0:T(8,128)S(1)} %get-tuple-element.24.refs_5_) | copy-start | bytes 14155780
  27.8 0.8 copy-start.6
  28.6 12.9 %copy-start.5 = (bf16[2,2,2,256,128]{4,3,2,1,0:T(8,128)(2,1)S(1)}, bf16[2,2,2,256,128]{4,3,2,1,0:T(8,128)(2,1)}, u32[]{:S(2)}) copy-start(bf16[2,2,2,256,128]{4,3,2,1,0:T(8,128)(2,1)} %get-tuple-element.16.refs_0_) | copy-start | bytes 1572868
  37.2 4.3 %copy-start.7 = (bf16[2,2,2,256,128]{4,3,2,1,0:T(8,128)(2,1)S(1)}, bf16[2,2,2,256,128]{4,3,2,1,0:T(8,128)(2,1)}, u32[]{:S(2)}) copy-start(bf16[2,2,2,256,128]{4,3,2,1,0:T(8,128)(2,1)} %copy-done.6) | copy-start | bytes 1572868
  41.5 4.0 %copy-start.1 = (f32[9,2,512,128]{3,2,1,0:T(8,128)S(1)}, f32[9,2,512,128]{3,2,1,0:T(8,128)}, u32[]{:S(2)}) copy-start(f32[9,2,512,128]{3,2,1,0:T(8,128)} %copy-done) | copy-start | bytes 14155780
  48.1 31.0 %copy-start.3 = (bf16[128,2048]{1,0:T(8,128)(2,1)S(1)}, bf16[128,2048]{1,0:T(8,128)(2,1)}, u32[]{:S(2)}) copy-start(bf16[128,2048]{1,0:T(8,128)(2,1)} %key_ref.1) | copy-start | bytes 1572868
  48.1 31.0 %copy-start.4 = (bf16[128,2048]{1,0:T(8,128)(2,1)S(1)}, bf16[128,2048]{1,0:T(8,128)(2,1)}, u32[]{:S(2)}) copy-start(bf16[128,2048]{1,0:T(8,128)(2,1)} %value_ref.1) | copy-start | bytes 1572868
  48.1 31.0 %copy-start.8 = (bf16[128,2048]{1,0:T(8,128)(2,1)S(1)}, bf16[128,2048]{1,0:T(8,128)(2,1)}, u32[]{:S(2)}) copy-start(bf16[128,2048]{1,0:T(8,128)(2,1)} %gate_ref.1) | copy-start | bytes 1572868
  48.1 31.0 %copy-start.9 = (f32[2048]{0:T(1024)S(1)}, f32[2048]{0:T(1024)}, u32[]{:S(2)}) copy-start(f32[2048]{0:T(1024)} %param.13) | copy-start | bytes 24580

commit v5 on v4

--- a/solution.py
+++ b/solution.py
@@ -336,12 +336,9 @@
     short = re_ref.shape[0]
     size = 2 * short
     filter_members(LATE, spec, re_ref, im_ref, dft_ref, back_re, back_im, stage)
-    for member in EARLY:
-        back_re[place ^ member] = early_re[place ^ member]
-        back_im[place ^ member] = early_im[place ^ member]
     scale = 1.0 / (2 * SEQ * size)
 
-    def rows_of(index, carry):
+    def rows_of(index, carry, last):
         at = rows_at(index)
         late = rows_at(index, short)
         cos, sin = table[SEQ, 0, at, :], table[SEQ, 1, at, :]
@@ -350,7 +347,7 @@
             pair = []
             for bit in range(2):
                 to = pl.ds((j % 2 * 2 + bit) * LANES, LANES)
-                pair.append((back_re[j // 2, at, to], back_im[j // 2, at, to]))
+                pair.append(tuple(ref[j // 2, at, to] for ref in ((back_re, back_im) if j // 2 == last else (early_re, early_im))))
             a, b = pair[0], times(pair[1], (cos, sin))
             parts[0].append(times((a[0] + b[0], a[1] + b[1]), (table[j, 0, at, :], table[j, 1, at, :])))
             parts[1].append(times((a[0] - b[0], a[1] - b[1]), (table[j, 0, late, :], table[j, 1, late, :])))
@@ -359,7 +356,11 @@
                 out_ref[p, where, :] = (value * (scale * sign if p % 2 else scale)).astype(jnp.bfloat16)
         return carry
 
-    lax.fori_loop(0, short // STEP, rows_of, 0, unroll=2)
+    for own in range(HALF):
+
+        @pl.when(place == own)
+        def _(last=own ^ LATE[0]):
+            lax.fori_loop(0, short // STEP, functools.partial(rows_of, last=last), 0, unroll=2)
 
 
 def table_kernel(member, table_hbm, near_hbm, table, near, out_ref, held, sems):

time: 80.7 us -> 80.3 us (level)
  no operation moved by 1% of the time
where the time goes in v5:
time: 80.3 us; the launch traced here: 79.9 us
  blocking collectives  30.9 us (38%)
  Pallas kernels  16.3 us (20%)
  waiting for transfers between devices  11.6 us (14%)
  starting transfers between devices  11.2 us (14%)
  local copies, waits for them, and re-layouts  9.79 us (12%)
    all_to_all x1, blocking collectives, halves(): lax.all_to_all(shares, everywhere, split_axis=0, concat_axis=0, tiled=True)  30.9 us
    pallas_call x6, Pallas kernels, call(): pl.pallas_call(kernel, out_shape=tuple((jax.ShapeDtypeStruct(shape, dtype...  12.3 us
    all_to_all x1, waiting for transfers between devices, halves(): lax.all_to_all(sends, everywhere, split_axis=0, concat_axis=0, tiled=True)  8.66 us
    unnamed x30, local copies, waits for them, and re-layouts  8.5 us
    ppermute x3, starting transfers between devices, swap(): return lax.ppermute(array, axis, [(i, i ^ mask) for i in range(count)])  7.25 us
    pallas_call x1, Pallas kernels, members_of(): pl.pallas_call(spectrum_kernel, grid_spec=pltpu.PrefetchScalarGridSpec(nu...  4.03 us
    all_to_all x1, starting transfers between devices, halves(): lax.all_to_all(sends, everywhere, split_axis=0, concat_axis=0, tiled=True)  3.92 us
    ppermute x3, waiting for transfers between devices, swap(): return lax.ppermute(array, axis, [(i, i ^ mask) for i in range(count)])  2.9 us
  transfers between devices with their start and end apart: 4, of which 3 were waited for; matrix products, arithmetic and copies ran while one was open for 0% of the time, Pallas kernels for 16%

profile of v5, /device:TPU:0, one launch (start us, length us, event | category | flops | bytes accessed | tf_op | source)
XLA Modules:
  0.0 79.9 jit_solution(1111671586078836239)
XLA Ops:
  0.0 1.3 %dynamic-slice_convert_fusion = bf16[2,2,512,128]{3,2,1,0:T(8,128)(2,1)S(1)} fusion(f32[2,2,512,512]{3,2,1,0:T(8,128)} %refs_2_.1, s32[]{:T(128)S(6)} %select_n.13), kind=kLoop, calls=%fused_computation | loop fusion | bytes 1048580 | tf_op jit(solution)/shard_map/convert_element_type | solution.py:437
  1.3 4.0 %collective-permute-start.2 = (bf16[2,2,512,128]{3,2,1,0:T(8,128)(2,1)S(1)}, bf16[2,2,512,128]{3,2,1,0:T(8,128)(2,1)S(1)}, u32[]{:S(2)}, u32[]{:S(2)}) collective-permute-start(bf16[2,2,512,128]{3,2,1,0:T(8,128)(2,1)S(1)} %dynamic-slice_convert_fusion), channel_id=1, source_target_pairs={{0,12},{4,8},{8,4},{12,0},{16,28},{20,24},{24,20},{28,16},{1,13},{... | collective-permute-start | bytes 1572872 | tf_op jit(solution)/shard_map/ppermute | solution.py:108
  5.3 2.4 %product.1 = bf16[32,128,128]{2,1,0:T(8,128)(2,1)} custom-call(bf16[128,2048]{1,0:T(8,128)(2,1)} %key_ref.1, bf16[128,2048]{1,0:T(8,128)(2,1)} %value_ref.1), custom_call_target="tpu_custom_call" | custom-call | tf_op jit(solution)/shard_map/product/pallas_call | solution.py:402
  7.7 3.9 %all-to-all-start = ((bf16[32,128,128]{2,1,0:T(8,128)(2,1)}), bf16[32,128,128]{2,1,0:T(8,128)(2,1)S(1)}, u32[]{:S(2)}, u32[]{:S(2)}) async-start(bf16[32,128,128]{2,1,0:T(8,128)(2,1)} %product.1), calls=%async_computation | async-start | bytes 2097152 | tf_op jit(solution)/shard_map/all_to_all | solution.py:450
  11.6 0.0 copy-start.14
  11.6 4.0 %spectrum.1 = (bf16[2,2,2,256,128]{4,3,2,1,0:T(8,128)(2,1)}, bf16[2,2,2,256,128]{4,3,2,1,0:T(8,128)(2,1)}, bf16[2,2,2,256,128]{4,3,2,1,0:T(8,128)(2,1)}) custom-call(s32[1]{0:T(128)} %bitcast.1.place_ref, f32[2,2,512,512]{3,2,1,0:T(8,128)} %refs_2_.1, f32[2,2,512,512]{3,2,1,0:T(8,128)} %refs_2_.1, f32[2,2,512,512]{3,2,1,0:T(8,128)} %refs_2_.1), custom_call_target="tpu_custom_call" | custom-call | tf_op jit(solution)/shard_map/spectrum/pallas_call | solution.py:173
  15.7 1.8 %collective-permute-start = (bf16[2,2,2,256,128]{4,3,2,1,0:T(8,128)(2,1)}, bf16[2,2,2,256,128]{4,3,2,1,0:T(8,128)(2,1)S(1)}, u32[]{:S(2)}, u32[]{:S(2)}) collective-permute-start(bf16[2,2,2,256,128]{4,3,2,1,0:T(8,128)(2,1)} %get-tuple-element.15), channel_id=1, source_target_pairs={{0,8},{4,12},{8,0},{12,4},{16,24},{20,28},{24,16},{28,20},{1,9},{5... | collective-permute-start | bytes 1572872 | tf_op jit(solution)/shard_map/ppermute | solution.py:108
  17.4 0.0 copy-start.2
  17.4 0.0 copy-start.10
  17.4 1.5 %collective-permute-start.1 = (bf16[2,2,2,256,128]{4,3,2,1,0:T(8,128)(2,1)}, bf16[2,2,2,256,128]{4,3,2,1,0:T(8,128)(2,1)S(1)}, u32[]{:S(2)}, u32[]{:S(2)}) collective-permute-start(bf16[2,2,2,256,128]{4,3,2,1,0:T(8,128)(2,1)} %get-tuple-element.17), channel_id=1, source_target_pairs={{0,4},{4,0},{8,12},{12,8},{16,20},{20,16},{24,28},{28,24},{1,5},{5... | collective-permute-start | bytes 1572872 | tf_op jit(solution)/shard_map/ppermute | solution.py:108
  18.9 0.6 collective-permute-done.2.member
  19.5 0.0 copy-start.11
  19.5 0.8 %copy-done.11 = bf16[2,2,512,128]{3,2,1,0:T(8,128)(2,1)} copy-done((bf16[2,2,512,128]{3,2,1,0:T(8,128)(2,1)}, bf16[2,2,512,128]{3,2,1,0:T(8,128)(2,1)S(1)}, u32[]{:S(2)}) %copy-start.11) | copy-done | bytes 524312
  20.3 0.0 copy-done.14
  20.3 0.0 copy-start.12
  20.3 1.0 %copy-done.12 = bf16[2,2,512,128]{3,2,1,0:T(8,128)(2,1)S(1)} copy-done((bf16[2,2,512,128]{3,2,1,0:T(8,128)(2,1)S(1)}, bf16[2,2,512,128]{3,2,1,0:T(8,128)(2,1)}, u32[]{:S(2)}) %copy-start.12) | copy-done | bytes 524312
  21.4 0.0 copy-start.13
  21.4 3.7 %copy-done.13 = f32[2,9,2,512,128]{4,3,2,1,0:T(8,128)S(1)} copy-done((f32[2,9,2,512,128]{4,3,2,1,0:T(8,128)S(1)}, f32[2,9,2,512,128]{4,3,2,1,0:T(8,128)}, u32[]{:S(2)}) %copy-start.13) | copy-done | bytes 9437208
  25.0 0.6 table.1
  25.6 0.0 copy-start
  25.6 2.1 %copy-done = f32[9,2,512,128]{3,2,1,0:T(8,128)} copy-done((f32[9,2,512,128]{3,2,1,0:T(8,128)}, f32[9,2,512,128]{3,2,1,0:T(8,128)S(1)}, u32[]{:S(2)}) %copy-start) | copy-done | bytes 4718616
  27.8 0.0 copy-start.6
  27.8 0.8 copy-done.6
  28.6 0.0 copy-start.5
  28.6 8.7 %all-to-all-done = bf16[32,128,128]{2,1,0:T(8,128)(2,1)S(1)} async-done(((bf16[32,128,128]{2,1,0:T(8,128)(2,1)}), bf16[32,128,128]{2,1,0:T(8,128)(2,1)S(1)}, u32[]{:S(2)}, u32[]{:S(2)}) %all-to-all-start) | async-done | bytes 1048608 | tf_op jit(solution)/shard_map/all_to_all | solution.py:450
  37.2 0.0 copy-start.7
  37.2 0.0 copy-done.2
  37.2 0.0 copy-done.10
  37.2 4.2 %forward.1 = (f32[256,2048]{1,0:T(8,128)S(1)}, f32[256,2048]{1,0:T(8,128)S(1)}) custom-call(bf16[8,512,128]{2,1,0:T(8,128)(2,1)S(1)} %bitcast.5, f32[9,2,64,128]{3,2,1,0:T(8,128)S(1)} %get-tuple-element.19.near, f32[288]{0:T(512)S(1)} %copy-done.10, bf16[256,512]{1,0:T(8,128)(2,1)S(1)} %copy-done.2), custom_call_target="tpu_custom_call" | custom-call | tf_op jit(solution)/shard_map/forward/pallas_call | solution.py:402
  41.5 0.0 collective-permute-done.1.refs_1_
  41.5 0.0 copy-done.5
  41.5 0.0 copy-done.7
  41.5 0.0 copy-start.1
  41.5 1.7 %early_members.1 = (f32[4,256,512]{2,1,0:T(8,128)S(1)}, f32[4,256,512]{2,1,0:T(8,128)S(1)}) custom-call(bf16[2,2,2,256,128]{4,3,2,1,0:T(8,128)(2,1)S(1)} %copy-done.5, bf16[2,2,2,256,128]{4,3,2,1,0:T(8,128)(2,1)S(1)} %collective-permute-done.1.refs_1_, bf16[2,2,2,256,128]{4,3,2,1,0:T(8,128)(2,1)S(1)} %copy-done.7, ...), custom_call_target="tpu_custom_call" | custom-call | tf_op jit(solution)/shard_map/early_members/pallas_call | solution.py:402
  43.2 2.3 %collective-permute-done.refs_0_ = bf16[2,2,2,256,128]{4,3,2,1,0:T(8,128)(2,1)S(1)} collective-permute-done((bf16[2,2,2,256,128]{4,3,2,1,0:T(8,128)(2,1)}, bf16[2,2,2,256,128]{4,3,2,1,0:T(8,128)(2,1)S(1)}, u32[]{:S(2)}, u32[]{:S(2)}) %collective-permute-start) | collective-permute-done | bytes 524320 | tf_op jit(solution)/shard_map/ppermute | solution.py:108
  45.5 0.0 copy-done.1
  45.5 2.2 %late_member.1 = bf16[8,512,128]{2,1,0:T(8,128)(2,1)S(1)} custom-call(bf16[2,2,2,256,128]{4,3,2,1,0:T(8,128)(2,1)S(1)} %collective-permute-done.refs_0_, f32[4,256,512]{2,1,0:T(8,128)S(1)} %get-tuple-element.22.refs_1_, f32[4,256,512]{2,1,0:T(8,128)S(1)} %get-tuple-element.23.refs_2_, f32[256,2048]{1,0:T(8,128)S(1)} %get-tuple-element.20.refs_3_, ...), custom_call_target="tpu_custom_call" | custom-call | tf_op jit(solution)/shard_map/late_member/pallas_call | solution.py:402
  47.8 0.0 copy-start.3
  47.8 0.0 copy-start.4
  47.8 0.0 copy-start.8
  47.8 0.0 copy-start.9
  47.8 30.9 %all_to_all.10.field_ref = bf16[32,128,128]{2,1,0:T(8,128)(2,1)S(1)} all-to-all(bf16[32,128,128]{2,1,0:T(8,128)(2,1)S(1)} %bitcast.4), channel_id=1, replica_groups=mesh['seq'=8,'ch'=4] {'seq','ch'}, dimensions={0} | all-to-all | bytes 2097152 | tf_op jit(solution)/shard_map/all_to_all | solution.py:474
  78.7 0.0 copy-done.3
  78.7 0.0 copy-done.4
  78.7 0.0 copy-done.8
  78.7 0.0 copy-done.9
  78.8 1.1 %gate.1 = bf16[128,2048]{1,0:T(8,128)(2,1)} custom-call(bf16[128,2048]{1,0:T(8,128)(2,1)S(1)} %copy-done.8, bf16[128,2048]{1,0:T(8,128)(2,1)S(1)} %copy-done.3, bf16[128,2048]{1,0:T(8,128)(2,1)S(1)} %copy-done.4, f32[1,2048]{1,0:T(1,128)S(1)} %bitcast.6, bf16[32,128,128]{2,1,0:T(8,128)(2,1)S(1)} %all_to_all.10.field_ref), custom_call_target="tpu_custom_call" | custom-call | tf_op jit(solution)/shard_map/gate/pallas_call | solution.py:402
Async XLA Ops:
  1.3 18.2 %collective-permute-start.2 = (bf16[2,2,512,128]{3,2,1,0:T(8,128)(2,1)S(1)}, bf16[2,2,512,128]{3,2,1,0:T(8,128)(2,1)S(1)}, u32[]{:S(2)}, u32[]{:S(2)}) collective-permute-start(bf16[2,2,512,128]{3,2,1,0:T(8,128)(2,1)S(1)} %dynamic-slice_convert_fusion), channel_id=1, source_target_pairs={{0,12},{4,8},{8,4},{12,0},{16,28},{20,24},{24,20},{28,16},{1,13},{... | collective-permute-start | bytes 1572872 | tf_op jit(solution)/shard_map/ppermute | solution.py:108
  7.7 29.5 %all-to-all-start = ((bf16[32,128,128]{2,1,0:T(8,128)(2,1)}), bf16[32,128,128]{2,1,0:T(8,128)(2,1)S(1)}, u32[]{:S(2)}, u32[]{:S(2)}) async-start(bf16[32,128,128]{2,1,0:T(8,128)(2,1)} %product.1), calls=%async_computation | async-start | bytes 2097152 | tf_op jit(solution)/shard_map/all_to_all | solution.py:450
  11.6 8.7 %copy-start.14 = (f32[2,9,2,64,128]{4,3,2,1,0:T(8,128)S(1)}, f32[2,9,2,64,128]{4,3,2,1,0:T(8,128)}, u32[]{:S(2)}) copy-start(f32[2,9,2,64,128]{4,3,2,1,0:T(8,128)} %constant.37.clone.near_hbm) | copy-start | bytes 3538948
  15.7 29.9 %collective-permute-start = (bf16[2,2,2,256,128]{4,3,2,1,0:T(8,128)(2,1)}, bf16[2,2,2,256,128]{4,3,2,1,0:T(8,128)(2,1)S(1)}, u32[]{:S(2)}, u32[]{:S(2)}) collective-permute-start(bf16[2,2,2,256,128]{4,3,2,1,0:T(8,128)(2,1)} %get-tuple-element.15), channel_id=1, source_target_pairs={{0,8},{4,12},{8,0},{12,4},{16,24},{20,28},{24,16},{28,20},{1,9},{5... | collective-permute-start | bytes 1572872 | tf_op jit(solution)/shard_map/ppermute | solution.py:108
  17.4 19.8 %copy-start.2 = (bf16[256,512]{1,0:T(8,128)(2,1)S(1)}, bf16[256,512]{1,0:T(8,128)(2,1)}, u32[]{:S(2)}) copy-start(bf16[256,512]{1,0:T(8,128)(2,1)} %constant.35.clone.dft_ref.refs_5_.refs_6_) | copy-start | bytes 786436
  17.4 19.8 %copy-start.10 = (f32[288]{0:T(512)S(1)}, f32[288]{0:T(512)}, u32[]{:S(2)}) copy-start(f32[288]{0:T(512)} %constant.38.clone.far) | copy-start | bytes 3460
  17.4 24.0 %collective-permute-start.1 = (bf16[2,2,2,256,128]{4,3,2,1,0:T(8,128)(2,1)}, bf16[2,2,2,256,128]{4,3,2,1,0:T(8,128)(2,1)S(1)}, u32[]{:S(2)}, u32[]{:S(2)}) collective-permute-start(bf16[2,2,2,256,128]{4,3,2,1,0:T(8,128)(2,1)} %get-tuple-element.17), channel_id=1, source_target_pairs={{0,4},{4,0},{8,12},{12,8},{16,20},{20,16},{24,28},{28,24},{1,5},{5... | collective-permute-start | bytes 1572872 | tf_op jit(solution)/shard_map/ppermute | solution.py:108
  19.5 0.8 %copy-start.11 = (bf16[2,2,512,128]{3,2,1,0:T(8,128)(2,1)}, bf16[2,2,512,128]{3,2,1,0:T(8,128)(2,1)S(1)}, u32[]{:S(2)}) copy-start(bf16[2,2,512,128]{3,2,1,0:T(8,128)(2,1)S(1)} %collective-permute-done.2.member) | copy-start | bytes 1572868
  20.3 1.0 %copy-start.12 = (bf16[2,2,512,128]{3,2,1,0:T(8,128)(2,1)S(1)}, bf16[2,2,512,128]{3,2,1,0:T(8,128)(2,1)}, u32[]{:S(2)}) copy-start(bf16[2,2,512,128]{3,2,1,0:T(8,128)(2,1)} %copy-done.11) | copy-start | bytes 1572868
  21.4 3.7 %copy-start.13 = (f32[2,9,2,512,128]{4,3,2,1,0:T(8,128)S(1)}, f32[2,9,2,512,128]{4,3,2,1,0:T(8,128)}, u32[]{:S(2)}) copy-start(f32[2,9,2,512,128]{4,3,2,1,0:T(8,128)} %constant.36.clone.table_hbm) | copy-start | bytes 28311556
  25.6 2.1 %copy-start = (f32[9,2,512,128]{3,2,1,0:T(8,128)}, f32[9,2,512,128]{3,2,1,0:T(8,128)S(1)}, u32[]{:S(2)}) copy-start(f32[9,2,512,128]{3,2,1,0:T(8,128)S(1)} %get-tuple-element.24.refs_5_) | copy-start | bytes 14155780
  27.8 0.8 copy-start.6
  28.6 12.9 %copy-start.5 = (bf16[2,2,2,256,128]{4,3,2,1,0:T(8,128)(2,1)S(1)}, bf16[2,2,2,256,128]{4,3,2,1,0:T(8,128)(2,1)}, u32[]{:S(2)}) copy-start(bf16[2,2,2,256,128]{4,3,2,1,0:T(8,128)(2,1)} %get-tuple-element.16.refs_0_) | copy-start | bytes 1572868
  37.2 4.3 %copy-start.7 = (bf16[2,2,2,256,128]{4,3,2,1,0:T(8,128)(2,1)S(1)}, bf16[2,2,2,256,128]{4,3,2,1,0:T(8,128)(2,1)}, u32[]{:S(2)}) copy-start(bf16[2,2,2,256,128]{4,3,2,1,0:T(8,128)(2,1)} %copy-done.6) | copy-start | bytes 1572868
  41.5 4.0 %copy-start.1 = (f32[9,2,512,128]{3,2,1,0:T(8,128)S(1)}, f32[9,2,512,128]{3,2,1,0:T(8,128)}, u32[]{:S(2)}) copy-start(f32[9,2,512,128]{3,2,1,0:T(8,128)} %copy-done) | copy-start | bytes 14155780
  47.8 31.0 %copy-start.3 = (bf16[128,2048]{1,0:T(8,128)(2,1)S(1)}, bf16[128,2048]{1,0:T(8,128)(2,1)}, u32[]{:S(2)}) copy-start(bf16[128,2048]{1,0:T(8,128)(2,1)} %key_ref.1) | copy-start | bytes 1572868
  47.8 31.0 %copy-start.4 = (bf16[128,2048]{1,0:T(8,128)(2,1)S(1)}, bf16[128,2048]{1,0:T(8,128)(2,1)}, u32[]{:S(2)}) copy-start(bf16[128,2048]{1,0:T(8,128)(2,1)} %value_ref.1) | copy-start | bytes 1572868
  47.8 30.9 %copy-start.8 = (bf16[128,2048]{1,0:T(8,128)(2,1)S(1)}, bf16[128,2048]{1,0:T(8,128)(2,1)}, u32[]{:S(2)}) copy-start(bf16[128,2048]{1,0:T(8,128)(2,1)} %gate_ref.1) | copy-start | bytes 1572868
  47.8 30.9 %copy-start.9 = (f32[2048]{0:T(1024)S(1)}, f32[2048]{0:T(1024)}, u32[]{:S(2)}) copy-start(f32[2048]{0:T(1024)} %param.13) | copy-start | bytes 24580

commit v6 on v5

--- a/solution.py
+++ b/solution.py
@@ -363,7 +363,7 @@
             lax.fori_loop(0, short // STEP, functools.partial(rows_of, last=last), 0, unroll=2)
 
 
-def table_kernel(member, table_hbm, near_hbm, table, near, out_ref, held, sems):
+def table_kernel(member, table_hbm, near_hbm, key_ref, value_ref, skip_ref, table, near, out_ref, direct, held, sems):
     half = lax.axis_index("seq") // HALF
     copies = [
         pltpu.make_async_copy(source.at[half], to, sems.at[index])
@@ -371,6 +371,11 @@
     ]
     for copy in copies:
         copy.start()
+    for ch in range(CH):
+        width = key_ref.shape[1] // CH
+        at = pl.ds(ch * width, width)
+        product = (key_ref[:, at].astype(jnp.float32) * value_ref[:, at].astype(jnp.float32)).astype(jnp.bfloat16)
+        direct[:, at] = skip_ref[:, at] * product.astype(jnp.float32)
     rows = out_ref.shape[3]
     for part in range(2):
         for odd in range(2):
@@ -381,15 +386,14 @@
         copy.wait()
 
 
-def gate_kernel(gate_ref, key_ref, value_ref, skip_ref, field_ref, out_hbm, held, sems):
+def gate_kernel(gate_ref, direct, field_ref, out_hbm, held, sems):
     copies = []
     for ch in range(CH):
         for member in range(HALF):
             device = member * CH + ch
             at = columns_of(device)
-            product = (key_ref[:, at].astype(jnp.float32) * value_ref[:, at].astype(jnp.float32)).astype(jnp.bfloat16)
             field = field_ref[device].astype(jnp.float32) + field_ref[device + DEVICES // 2].astype(jnp.float32)
-            gated = gate_ref[:, at].astype(jnp.float32) * (field + skip_ref[:, at] * product.astype(jnp.float32))
+            gated = gate_ref[:, at].astype(jnp.float32) * (field + direct[:, at])
             held[:, at] = gated.astype(jnp.bfloat16)
         columns = pl.ds(ch * HALF * LANES, HALF * LANES)
         copies.append(pltpu.make_async_copy(held.at[:, columns], out_hbm.at[:, columns], sems.at[ch]))
@@ -437,11 +441,11 @@
     last = lax.dynamic_slice_in_dim(spectrum, opposite * LANES, LANES, axis=3).astype(bf16)
     last = swap(last, "seq", 3, SEQ)
     cost = pl.CostEstimate(flops=40000000000, bytes_accessed=1 << 20, transcendentals=0)
-    table, near, last = call(
+    table, near, last, direct = call(
         table_kernel,
         "table",
-        [last, table, near],
-        [(table.shape[1:], f32), (near.shape[1:], f32), ((2, 2, 2, short, LANES), bf16)],
+        [last, table, near, key_rows, value_rows, skip_bias.reshape(1, channels)],
+        [(table.shape[1:], f32), (near.shape[1:], f32), ((2, 2, 2, short, LANES), bf16), ((rows, channels), f32)],
         [pltpu.VMEM((size, LANES), f32), pltpu.SemaphoreType.DMA((2,))],
         hbm=(1, 2),
         cost=cost,
@@ -475,7 +479,7 @@
     return call(
         gate_kernel,
         "gate",
-        [gate_rows, key_rows, value_rows, skip_bias.reshape(1, channels), field],
+        [gate_rows, direct, field],
         [((rows, channels), bf16)],
         [pltpu.VMEM((rows, channels), bf16), pltpu.SemaphoreType.DMA((CH,))],
         to_hbm=True,

time: 80.3 us -> 80.1 us (level)
  waiting for transfers between devices: 11.6 us -> 9.97 us
  Pallas kernels: 16.3 us -> 17.6 us
    ppermute x3, waiting for transfers between devices: 2.9 us -> 1.6 us  [swap(): return lax.ppermute(array, axis, [(i, i ^ mask) for i in range(count)])]
    pallas_call x6, Pallas kernels: 12.3 us -> 13.5 us  [call(): pl.pallas_call(kernel, out_shape=tuple((jax.ShapeDtypeStruct(shape, dtype...]
  transfers between devices with their start and end apart: 4 -> 4, of which waited for: 3 -> 3; matrix products, arithmetic and copies ran while one was open for 0% -> 0% of each run, Pallas kernels for 16% -> 18%
where the time goes in v6:
time: 80.1 us; the launch traced here: 79.6 us
  blocking collectives  30.9 us (39%)
  Pallas kernels  17.6 us (22%)
  starting transfers between devices  11.2 us (14%)
  waiting for transfers between devices  9.97 us (12%)
  local copies, waits for them, and re-layouts  9.78 us (12%)
    all_to_all x1, blocking collectives, halves(): lax.all_to_all(shares, everywhere, split_axis=0, concat_axis=0, tiled=True)  30.9 us
    pallas_call x6, Pallas kernels, call(): pl.pallas_call(kernel, out_shape=tuple((jax.ShapeDtypeStruct(shape, dtype...  13.5 us
    unnamed x30, local copies, waits for them, and re-layouts  8.48 us
    all_to_all x1, waiting for transfers between devices, halves(): lax.all_to_all(sends, everywhere, split_axis=0, concat_axis=0, tiled=True)  8.38 us
    ppermute x3, starting transfers between devices, swap(): return lax.ppermute(array, axis, [(i, i ^ mask) for i in range(count)])  7.25 us
    pallas_call x1, Pallas kernels, members_of(): pl.pallas_call(spectrum_kernel, grid_spec=pltpu.PrefetchScalarGridSpec(nu...  4.12 us
    all_to_all x1, starting transfers between devices, halves(): lax.all_to_all(sends, everywhere, split_axis=0, concat_axis=0, tiled=True)  3.92 us
  transfers between devices with their start and end apart: 4, of which 3 were waited for; matrix products, arithmetic and copies ran while one was open for 0% of the time, Pallas kernels for 18%

profile of v6, /device:TPU:0, one launch (start us, length us, event | category | flops | bytes accessed | tf_op | source)
XLA Modules:
  0.0 79.6 jit_solution(11375390073174968520)
XLA Ops:
  0.0 1.3 %dynamic-slice_convert_fusion = bf16[2,2,512,128]{3,2,1,0:T(8,128)(2,1)S(1)} fusion(f32[2,2,512,512]{3,2,1,0:T(8,128)} %refs_2_.1, s32[]{:T(128)S(6)} %select_n.13), kind=kLoop, calls=%fused_computation | loop fusion | bytes 1048580 | tf_op jit(solution)/shard_map/convert_element_type | solution.py:441
  1.3 4.0 %collective-permute-start = (bf16[2,2,512,128]{3,2,1,0:T(8,128)(2,1)S(1)}, bf16[2,2,512,128]{3,2,1,0:T(8,128)(2,1)S(1)}, u32[]{:S(2)}, u32[]{:S(2)}) collective-permute-start(bf16[2,2,512,128]{3,2,1,0:T(8,128)(2,1)S(1)} %dynamic-slice_convert_fusion), channel_id=1, source_target_pairs={{0,12},{4,8},{8,4},{12,0},{16,28},{20,24},{24,20},{28,16},{1,13},{... | collective-permute-start | bytes 1572872 | tf_op jit(solution)/shard_map/ppermute | solution.py:108
  5.3 2.4 %product.1 = bf16[32,128,128]{2,1,0:T(8,128)(2,1)} custom-call(bf16[128,2048]{1,0:T(8,128)(2,1)} %key_hbm.1, bf16[128,2048]{1,0:T(8,128)(2,1)} %value_hbm.1), custom_call_target="tpu_custom_call" | custom-call | tf_op jit(solution)/shard_map/product/pallas_call | solution.py:406
  7.7 3.9 %all-to-all-start = ((bf16[32,128,128]{2,1,0:T(8,128)(2,1)}), bf16[32,128,128]{2,1,0:T(8,128)(2,1)S(1)}, u32[]{:S(2)}, u32[]{:S(2)}) async-start(bf16[32,128,128]{2,1,0:T(8,128)(2,1)} %product.1), calls=%async_computation | async-start | bytes 2097152 | tf_op jit(solution)/shard_map/all_to_all | solution.py:454
  11.6 0.0 copy-start.6
  11.6 0.0 copy-start.7
  11.6 0.0 copy-start.12
  11.7 0.0 copy-start.14
  11.7 4.1 %spectrum.1 = (bf16[2,2,2,256,128]{4,3,2,1,0:T(8,128)(2,1)}, bf16[2,2,2,256,128]{4,3,2,1,0:T(8,128)(2,1)}, bf16[2,2,2,256,128]{4,3,2,1,0:T(8,128)(2,1)}) custom-call(s32[1]{0:T(128)} %bitcast.1.place_ref, f32[2,2,512,512]{3,2,1,0:T(8,128)} %refs_2_.1, f32[2,2,512,512]{3,2,1,0:T(8,128)} %refs_2_.1, f32[2,2,512,512]{3,2,1,0:T(8,128)} %refs_2_.1), custom_call_target="tpu_custom_call" | custom-call | tf_op jit(solution)/shard_map/spectrum/pallas_call | solution.py:173
  15.8 1.8 %collective-permute-start.1 = (bf16[2,2,2,256,128]{4,3,2,1,0:T(8,128)(2,1)}, bf16[2,2,2,256,128]{4,3,2,1,0:T(8,128)(2,1)S(1)}, u32[]{:S(2)}, u32[]{:S(2)}) collective-permute-start(bf16[2,2,2,256,128]{4,3,2,1,0:T(8,128)(2,1)} %get-tuple-element.17), channel_id=1, source_target_pairs={{0,8},{4,12},{8,0},{12,4},{16,24},{20,28},{24,16},{28,20},{1,9},{5... | collective-permute-start | bytes 1572872 | tf_op jit(solution)/shard_map/ppermute | solution.py:108
  17.6 1.5 %collective-permute-start.2 = (bf16[2,2,2,256,128]{4,3,2,1,0:T(8,128)(2,1)}, bf16[2,2,2,256,128]{4,3,2,1,0:T(8,128)(2,1)}, u32[]{:S(2)}, u32[]{:S(2)}) collective-permute-start(bf16[2,2,2,256,128]{4,3,2,1,0:T(8,128)(2,1)} %get-tuple-element.19), channel_id=1, source_target_pairs={{0,4},{4,0},{8,12},{12,8},{16,20},{20,16},{24,28},{28,24},{1,5},{5... | collective-permute-start | bytes 1572872 | tf_op jit(solution)/shard_map/ppermute | solution.py:108
  19.0 0.5 collective-permute-done.member
  19.5 0.0 copy-start.10
  19.5 0.8 copy-done.10
  20.3 0.0 copy-done.6
  20.3 0.0 copy-done.7
  20.3 0.0 copy-done.12
  20.3 0.0 copy-done.14
  20.3 0.0 copy-start.11
  20.3 1.0 %copy-done.11 = bf16[2,2,512,128]{3,2,1,0:T(8,128)(2,1)S(1)} copy-done((bf16[2,2,512,128]{3,2,1,0:T(8,128)(2,1)S(1)}, bf16[2,2,512,128]{3,2,1,0:T(8,128)(2,1)}, u32[]{:S(2)}) %copy-start.11) | copy-done | bytes 524312
  21.4 0.0 copy-start.13
  21.4 3.7 %copy-done.13 = f32[2,9,2,512,128]{4,3,2,1,0:T(8,128)S(1)} copy-done((f32[2,9,2,512,128]{4,3,2,1,0:T(8,128)S(1)}, f32[2,9,2,512,128]{4,3,2,1,0:T(8,128)}, u32[]{:S(2)}) %copy-start.13) | copy-done | bytes 9437208
  25.0 0.0 copy-start.2
  25.0 0.0 copy-start.9
  25.1 0.9 %table.1 = (f32[9,2,512,128]{3,2,1,0:T(8,128)S(1)}, f32[9,2,64,128]{3,2,1,0:T(8,128)S(1)}, bf16[2,2,2,256,128]{4,3,2,1,0:T(8,128)(2,1)S(1)}, f32[128,2048]{1,0:T(8,128)S(1)}) custom-call(bf16[2,2,512,128]{3,2,1,0:T(8,128)(2,1)S(1)} %copy-done.11, f32[2,9,2,512,128]{4,3,2,1,0:T(8,128)S(1)} %copy-done.13, f32[2,9,2,64,128]{4,3,2,1,0:T(8,128)S(1)} %copy-done.14, ...), custom_call_target="tpu_custom_call" | custom-call | flops 40000000000 | bytes 1048576 | tf_op jit(solution)/shard_map/table/pallas_call | solution.py:406
  25.9 0.0 copy-start
  25.9 2.1 %copy-done = f32[9,2,512,128]{3,2,1,0:T(8,128)} copy-done((f32[9,2,512,128]{3,2,1,0:T(8,128)}, f32[9,2,512,128]{3,2,1,0:T(8,128)S(1)}, u32[]{:S(2)}) %copy-start) | copy-done | bytes 4718616
  28.1 0.0 copy-start.4
  28.1 0.8 copy-done.4
  28.8 8.4 %all-to-all-done = bf16[32,128,128]{2,1,0:T(8,128)(2,1)S(1)} async-done(((bf16[32,128,128]{2,1,0:T(8,128)(2,1)}), bf16[32,128,128]{2,1,0:T(8,128)(2,1)S(1)}, u32[]{:S(2)}, u32[]{:S(2)}) %all-to-all-start) | async-done | bytes 1048608 | tf_op jit(solution)/shard_map/all_to_all | solution.py:454
  37.2 0.0 copy-start.3
  37.2 0.0 copy-start.5
  37.2 0.0 copy-done.2
  37.2 0.0 copy-done.9
  37.2 4.2 %forward.1 = (f32[256,2048]{1,0:T(8,128)S(1)}, f32[256,2048]{1,0:T(8,128)S(1)}) custom-call(bf16[8,512,128]{2,1,0:T(8,128)(2,1)S(1)} %bitcast.5, f32[9,2,64,128]{3,2,1,0:T(8,128)S(1)} %get-tuple-element.21.near, f32[288]{0:T(512)S(1)} %copy-done.9, bf16[256,512]{1,0:T(8,128)(2,1)S(1)} %copy-done.2), custom_call_target="tpu_custom_call" | custom-call | tf_op jit(solution)/shard_map/forward/pallas_call | solution.py:406
  41.5 0.0 collective-permute-done.2.refs_1_
  41.5 0.0 copy-done.3
  41.5 0.0 copy-done.5
  41.5 0.0 copy-start.1
  41.5 2.9 %early_members.1 = (f32[4,256,512]{2,1,0:T(8,128)S(1)}, f32[4,256,512]{2,1,0:T(8,128)S(1)}) custom-call(bf16[2,2,2,256,128]{4,3,2,1,0:T(8,128)(2,1)S(1)} %copy-done.3, bf16[2,2,2,256,128]{4,3,2,1,0:T(8,128)(2,1)} %collective-permute-done.2.refs_1_, bf16[2,2,2,256,128]{4,3,2,1,0:T(8,128)(2,1)S(1)} %copy-done.5, f32[256,2048]{1,0:T(8,128)S(1)} %get-tuple-element.22.refs_3_, ...), custom_call_target="tpu_custom_call" | custom-call | tf_op jit(solution)/shard_map/early_members/pallas_call | solution.py:406
  44.4 1.1 %collective-permute-done.1.refs_0_ = bf16[2,2,2,256,128]{4,3,2,1,0:T(8,128)(2,1)S(1)} collective-permute-done((bf16[2,2,2,256,128]{4,3,2,1,0:T(8,128)(2,1)}, bf16[2,2,2,256,128]{4,3,2,1,0:T(8,128)(2,1)S(1)}, u32[]{:S(2)}, u32[]{:S(2)}) %collective-permute-start.1) | collective-permute-done | bytes 524320 | tf_op jit(solution)/shard_map/ppermute | solution.py:108
  45.5 0.0 copy-done.1
  45.5 2.2 %late_member.1 = bf16[8,512,128]{2,1,0:T(8,128)(2,1)S(1)} custom-call(bf16[2,2,2,256,128]{4,3,2,1,0:T(8,128)(2,1)S(1)} %collective-permute-done.1.refs_0_, f32[4,256,512]{2,1,0:T(8,128)S(1)} %get-tuple-element.24.refs_1_, f32[4,256,512]{2,1,0:T(8,128)S(1)} %get-tuple-element.25.refs_2_, f32[256,2048]{1,0:T(8,128)S(1)} %get-tuple-element.22.refs_3_, ...), custom_call_target="tpu_custom_call" | custom-call | tf_op jit(solution)/shard_map/late_member/pallas_call | solution.py:406
  47.8 0.0 copy-start.8
  47.8 30.9 %all_to_all.10.field_ref = bf16[32,128,128]{2,1,0:T(8,128)(2,1)S(1)} all-to-all(bf16[32,128,128]{2,1,0:T(8,128)(2,1)S(1)} %bitcast.4), channel_id=1, replica_groups=mesh['seq'=8,'ch'=4] {'seq','ch'}, dimensions={0} | all-to-all | bytes 2097152 | tf_op jit(solution)/shard_map/all_to_all | solution.py:478
  78.7 0.0 copy-done.8
  78.7 0.9 %gate.1 = bf16[128,2048]{1,0:T(8,128)(2,1)} custom-call(bf16[128,2048]{1,0:T(8,128)(2,1)S(1)} %copy-done.8, f32[128,2048]{1,0:T(8,128)S(1)} %get-tuple-element.16.direct, bf16[32,128,128]{2,1,0:T(8,128)(2,1)S(1)} %all_to_all.10.field_ref), custom_call_target="tpu_custom_call" | custom-call | tf_op jit(solution)/shard_map/gate/pallas_call | solution.py:406
Async XLA Ops:
  1.3 18.2 %collective-permute-start = (bf16[2,2,512,128]{3,2,1,0:T(8,128)(2,1)S(1)}, bf16[2,2,512,128]{3,2,1,0:T(8,128)(2,1)S(1)}, u32[]{:S(2)}, u32[]{:S(2)}) collective-permute-start(bf16[2,2,512,128]{3,2,1,0:T(8,128)(2,1)S(1)} %dynamic-slice_convert_fusion), channel_id=1, source_target_pairs={{0,12},{4,8},{8,4},{12,0},{16,28},{20,24},{24,20},{28,16},{1,13},{... | collective-permute-start | bytes 1572872 | tf_op jit(solution)/shard_map/ppermute | solution.py:108
  7.7 29.5 %all-to-all-start = ((bf16[32,128,128]{2,1,0:T(8,128)(2,1)}), bf16[32,128,128]{2,1,0:T(8,128)(2,1)S(1)}, u32[]{:S(2)}, u32[]{:S(2)}) async-start(bf16[32,128,128]{2,1,0:T(8,128)(2,1)} %product.1), calls=%async_computation | async-start | bytes 2097152 | tf_op jit(solution)/shard_map/all_to_all | solution.py:454
  11.6 8.7 %copy-start.6 = (bf16[128,2048]{1,0:T(8,128)(2,1)S(1)}, bf16[128,2048]{1,0:T(8,128)(2,1)}, u32[]{:S(2)}) copy-start(bf16[128,2048]{1,0:T(8,128)(2,1)} %key_hbm.1) | copy-start | bytes 1572868
  11.6 8.7 %copy-start.7 = (bf16[128,2048]{1,0:T(8,128)(2,1)S(1)}, bf16[128,2048]{1,0:T(8,128)(2,1)}, u32[]{:S(2)}) copy-start(bf16[128,2048]{1,0:T(8,128)(2,1)} %value_hbm.1) | copy-start | bytes 1572868
  11.6 8.7 %copy-start.12 = (f32[2048]{0:T(1024)S(1)}, f32[2048]{0:T(1024)}, u32[]{:S(2)}) copy-start(f32[2048]{0:T(1024)} %param.13) | copy-start | bytes 24580
  11.7 8.7 %copy-start.14 = (f32[2,9,2,64,128]{4,3,2,1,0:T(8,128)S(1)}, f32[2,9,2,64,128]{4,3,2,1,0:T(8,128)}, u32[]{:S(2)}) copy-start(f32[2,9,2,64,128]{4,3,2,1,0:T(8,128)} %constant.37.clone.near_hbm) | copy-start | bytes 3538948
  15.8 29.7 %collective-permute-start.1 = (bf16[2,2,2,256,128]{4,3,2,1,0:T(8,128)(2,1)}, bf16[2,2,2,256,128]{4,3,2,1,0:T(8,128)(2,1)S(1)}, u32[]{:S(2)}, u32[]{:S(2)}) collective-permute-start(bf16[2,2,2,256,128]{4,3,2,1,0:T(8,128)(2,1)} %get-tuple-element.17), channel_id=1, source_target_pairs={{0,8},{4,12},{8,0},{12,4},{16,24},{20,28},{24,16},{28,20},{1,9},{5... | collective-permute-start | bytes 1572872 | tf_op jit(solution)/shard_map/ppermute | solution.py:108
  17.6 23.9 %collective-permute-start.2 = (bf16[2,2,2,256,128]{4,3,2,1,0:T(8,128)(2,1)}, bf16[2,2,2,256,128]{4,3,2,1,0:T(8,128)(2,1)}, u32[]{:S(2)}, u32[]{:S(2)}) collective-permute-start(bf16[2,2,2,256,128]{4,3,2,1,0:T(8,128)(2,1)} %get-tuple-element.19), channel_id=1, source_target_pairs={{0,4},{4,0},{8,12},{12,8},{16,20},{20,16},{24,28},{28,24},{1,5},{5... | collective-permute-start | bytes 1572872 | tf_op jit(solution)/shard_map/ppermute | solution.py:108
  19.5 0.8 copy-start.10
  20.3 1.0 %copy-start.11 = (bf16[2,2,512,128]{3,2,1,0:T(8,128)(2,1)S(1)}, bf16[2,2,512,128]{3,2,1,0:T(8,128)(2,1)}, u32[]{:S(2)}) copy-start(bf16[2,2,512,128]{3,2,1,0:T(8,128)(2,1)} %copy-done.10) | copy-start | bytes 1572868
  21.4 3.7 %copy-start.13 = (f32[2,9,2,512,128]{4,3,2,1,0:T(8,128)S(1)}, f32[2,9,2,512,128]{4,3,2,1,0:T(8,128)}, u32[]{:S(2)}) copy-start(f32[2,9,2,512,128]{4,3,2,1,0:T(8,128)} %constant.36.clone.table_hbm) | copy-start | bytes 28311556
  25.0 12.2 %copy-start.2 = (bf16[256,512]{1,0:T(8,128)(2,1)S(1)}, bf16[256,512]{1,0:T(8,128)(2,1)}, u32[]{:S(2)}) copy-start(bf16[256,512]{1,0:T(8,128)(2,1)} %constant.35.clone.dft_ref.refs_5_.refs_6_) | copy-start | bytes 786436
  25.0 12.2 %copy-start.9 = (f32[288]{0:T(512)S(1)}, f32[288]{0:T(512)}, u32[]{:S(2)}) copy-start(f32[288]{0:T(512)} %constant.38.clone.far) | copy-start | bytes 3460
  25.9 2.1 %copy-start = (f32[9,2,512,128]{3,2,1,0:T(8,128)}, f32[9,2,512,128]{3,2,1,0:T(8,128)S(1)}, u32[]{:S(2)}) copy-start(f32[9,2,512,128]{3,2,1,0:T(8,128)S(1)} %get-tuple-element.26.refs_5_) | copy-start | bytes 14155780
  28.1 0.8 copy-start.4
  37.2 4.3 %copy-start.3 = (bf16[2,2,2,256,128]{4,3,2,1,0:T(8,128)(2,1)S(1)}, bf16[2,2,2,256,128]{4,3,2,1,0:T(8,128)(2,1)}, u32[]{:S(2)}) copy-start(bf16[2,2,2,256,128]{4,3,2,1,0:T(8,128)(2,1)} %get-tuple-element.18.refs_0_) | copy-start | bytes 1572868
  37.2 4.3 %copy-start.5 = (bf16[2,2,2,256,128]{4,3,2,1,0:T(8,128)(2,1)S(1)}, bf16[2,2,2,256,128]{4,3,2,1,0:T(8,128)(2,1)}, u32[]{:S(2)}) copy-start(bf16[2,2,2,256,128]{4,3,2,1,0:T(8,128)(2,1)} %copy-done.4) | copy-start | bytes 1572868
  41.5 4.0 %copy-start.1 = (f32[9,2,512,128]{3,2,1,0:T(8,128)S(1)}, f32[9,2,512,128]{3,2,1,0:T(8,128)}, u32[]{:S(2)}) copy-start(f32[9,2,512,128]{3,2,1,0:T(8,128)} %copy-done) | copy-start | bytes 14155780
  47.8 30.9 %copy-start.8 = (bf16[128,2048]{1,0:T(8,128)(2,1)S(1)}, bf16[128,2048]{1,0:T(8,128)(2,1)}, u32[]{:S(2)}) copy-start(bf16[128,2048]{1,0:T(8,128)(2,1)} %gate_ref.1) | copy-start | bytes 1572868

commit v7 on v6

--- a/solution.py
+++ b/solution.py
@@ -312,15 +312,14 @@
                 y_re, y_im = times((re_ref[:, at], im_ref[:, at]), h)
                 y_re, y_im = y_re.astype(jnp.bfloat16), y_im.astype(jnp.bfloat16)
                 to = pl.ds((odd * 2 + bit) * LANES, LANES)
+                beside = pl.ds((4 + odd * 2 + bit) * LANES, LANES)
                 stage[index, pl.ds(0, short), to] = y_im
                 stage[index, pl.ds(short, short), to] = y_re
-                stage[index, pl.ds(size, short), to] = -y_im
-        back_im[place ^ member] = jnp.dot(
-            dft_ref[...], stage[index, pl.ds(0, size), :], preferred_element_type=jnp.float32
-        )
-        back_re[place ^ member] = jnp.dot(
-            dft_ref[...], stage[index, pl.ds(short, size), :], preferred_element_type=jnp.float32
-        )
+                stage[index, pl.ds(0, short), beside] = y_re
+                stage[index, pl.ds(short, short), beside] = -y_im
+        both = jnp.dot(dft_ref[...], stage[index], preferred_element_type=jnp.float32)
+        back_im[place ^ member] = both[:, : 4 * LANES]
+        back_re[place ^ member] = both[:, 4 * LANES :]
 
 
 def early_kernel(*refs):
@@ -466,14 +465,14 @@
         "early_members",
         [*[spec[member] for member in EARLY], *freq, dft],
         [back] * 2,
-        [pltpu.VMEM((len(EARLY), 3 * short, 4 * LANES), bf16)],
+        [pltpu.VMEM((len(EARLY), 2 * short, 8 * LANES), bf16)],
     )
     shares = call(
         late_kernel,
         "late_member",
         [*[spec[member] for member in LATE], *early, *freq, table, dft],
         [((SEQ, size, LANES), bf16)],
-        [pltpu.VMEM(*back)] * 2 + [pltpu.VMEM((len(LATE), 3 * short, 4 * LANES), bf16)],
+        [pltpu.VMEM(*back)] * 2 + [pltpu.VMEM((len(LATE), 2 * short, 8 * LANES), bf16)],
     )[0].reshape(DEVICES, rows, LANES)
     field = lax.all_to_all(shares, everywhere, split_axis=0, concat_axis=0, tiled=True)
     return call(

time: 80.1 us -> 80.1 us (level)
  no operation moved by 1% of the time
where the time goes in v7:
time: 80.1 us; the launch traced here: 79.7 us
  blocking collectives  30.9 us (39%)
  Pallas kernels  17.7 us (22%)
  starting transfers between devices  11.2 us (14%)
  waiting for transfers between devices  9.93 us (12%)
  local copies, waits for them, and re-layouts  9.78 us (12%)
    all_to_all x1, blocking collectives, halves(): lax.all_to_all(shares, everywhere, split_axis=0, concat_axis=0, tiled=True)  30.9 us
    pallas_call x6, Pallas kernels, call(): pl.pallas_call(kernel, out_shape=tuple((jax.ShapeDtypeStruct(shape, dtype...  13.6 us
    unnamed x30, local copies, waits for them, and re-layouts  8.48 us
    all_to_all x1, waiting for transfers between devices, halves(): lax.all_to_all(sends, everywhere, split_axis=0, concat_axis=0, tiled=True)  8.38 us
    ppermute x3, starting transfers between devices, swap(): return lax.ppermute(array, axis, [(i, i ^ mask) for i in range(count)])  7.25 us
    pallas_call x1, Pallas kernels, members_of(): pl.pallas_call(spectrum_kernel, grid_spec=pltpu.PrefetchScalarGridSpec(nu...  4.12 us
    all_to_all x1, starting transfers between devices, halves(): lax.all_to_all(sends, everywhere, split_axis=0, concat_axis=0, tiled=True)  3.92 us
  transfers between devices with their start and end apart: 4, of which 3 were waited for; matrix products, arithmetic and copies ran while one was open for 0% of the time, Pallas kernels for 18%

profile of v7, /device:TPU:0, one launch (start us, length us, event | category | flops | bytes accessed | tf_op | source)
XLA Modules:
  0.0 79.7 jit_solution(9135446397379297392)
XLA Ops:
  0.0 1.3 %dynamic-slice_convert_fusion = bf16[2,2,512,128]{3,2,1,0:T(8,128)(2,1)S(1)} fusion(f32[2,2,512,512]{3,2,1,0:T(8,128)} %refs_2_.1, s32[]{:T(128)S(6)} %select_n.13), kind=kLoop, calls=%fused_computation | loop fusion | bytes 1048580 | tf_op jit(solution)/shard_map/convert_element_type | solution.py:440
  1.3 4.0 %collective-permute-start = (bf16[2,2,512,128]{3,2,1,0:T(8,128)(2,1)S(1)}, bf16[2,2,512,128]{3,2,1,0:T(8,128)(2,1)S(1)}, u32[]{:S(2)}, u32[]{:S(2)}) collective-permute-start(bf16[2,2,512,128]{3,2,1,0:T(8,128)(2,1)S(1)} %dynamic-slice_convert_fusion), channel_id=1, source_target_pairs={{0,12},{4,8},{8,4},{12,0},{16,28},{20,24},{24,20},{28,16},{1,13},{... | collective-permute-start | bytes 1572872 | tf_op jit(solution)/shard_map/ppermute | solution.py:108
  5.3 2.4 %product.1 = bf16[32,128,128]{2,1,0:T(8,128)(2,1)} custom-call(bf16[128,2048]{1,0:T(8,128)(2,1)} %key_hbm.1, bf16[128,2048]{1,0:T(8,128)(2,1)} %value_hbm.1), custom_call_target="tpu_custom_call" | custom-call | tf_op jit(solution)/shard_map/product/pallas_call | solution.py:405
  7.7 3.9 %all-to-all-start = ((bf16[32,128,128]{2,1,0:T(8,128)(2,1)}), bf16[32,128,128]{2,1,0:T(8,128)(2,1)S(1)}, u32[]{:S(2)}, u32[]{:S(2)}) async-start(bf16[32,128,128]{2,1,0:T(8,128)(2,1)} %product.1), calls=%async_computation | async-start | bytes 2097152 | tf_op jit(solution)/shard_map/all_to_all | solution.py:453
  11.6 0.0 copy-start.6
  11.6 0.0 copy-start.7
  11.6 0.0 copy-start.12
  11.7 0.0 copy-start.14
  11.7 4.1 %spectrum.1 = (bf16[2,2,2,256,128]{4,3,2,1,0:T(8,128)(2,1)}, bf16[2,2,2,256,128]{4,3,2,1,0:T(8,128)(2,1)}, bf16[2,2,2,256,128]{4,3,2,1,0:T(8,128)(2,1)}) custom-call(s32[1]{0:T(128)} %bitcast.1.place_ref, f32[2,2,512,512]{3,2,1,0:T(8,128)} %refs_2_.1, f32[2,2,512,512]{3,2,1,0:T(8,128)} %refs_2_.1, f32[2,2,512,512]{3,2,1,0:T(8,128)} %refs_2_.1), custom_call_target="tpu_custom_call" | custom-call | tf_op jit(solution)/shard_map/spectrum/pallas_call | solution.py:173
  15.8 1.8 %collective-permute-start.1 = (bf16[2,2,2,256,128]{4,3,2,1,0:T(8,128)(2,1)}, bf16[2,2,2,256,128]{4,3,2,1,0:T(8,128)(2,1)S(1)}, u32[]{:S(2)}, u32[]{:S(2)}) collective-permute-start(bf16[2,2,2,256,128]{4,3,2,1,0:T(8,128)(2,1)} %get-tuple-element.17), channel_id=1, source_target_pairs={{0,8},{4,12},{8,0},{12,4},{16,24},{20,28},{24,16},{28,20},{1,9},{5... | collective-permute-start | bytes 1572872 | tf_op jit(solution)/shard_map/ppermute | solution.py:108
  17.6 1.5 %collective-permute-start.2 = (bf16[2,2,2,256,128]{4,3,2,1,0:T(8,128)(2,1)}, bf16[2,2,2,256,128]{4,3,2,1,0:T(8,128)(2,1)}, u32[]{:S(2)}, u32[]{:S(2)}) collective-permute-start(bf16[2,2,2,256,128]{4,3,2,1,0:T(8,128)(2,1)} %get-tuple-element.19), channel_id=1, source_target_pairs={{0,4},{4,0},{8,12},{12,8},{16,20},{20,16},{24,28},{28,24},{1,5},{5... | collective-permute-start | bytes 1572872 | tf_op jit(solution)/shard_map/ppermute | solution.py:108
  19.0 0.5 collective-permute-done.member
  19.5 0.0 copy-start.10
  19.5 0.8 copy-done.10
  20.3 0.0 copy-done.6
  20.3 0.0 copy-done.7
  20.3 0.0 copy-done.12
  20.3 0.0 copy-done.14
  20.3 0.0 copy-start.11
  20.3 1.0 %copy-done.11 = bf16[2,2,512,128]{3,2,1,0:T(8,128)(2,1)S(1)} copy-done((bf16[2,2,512,128]{3,2,1,0:T(8,128)(2,1)S(1)}, bf16[2,2,512,128]{3,2,1,0:T(8,128)(2,1)}, u32[]{:S(2)}) %copy-start.11) | copy-done | bytes 524312
  21.4 0.0 copy-start.13
  21.4 3.7 %copy-done.13 = f32[2,9,2,512,128]{4,3,2,1,0:T(8,128)S(1)} copy-done((f32[2,9,2,512,128]{4,3,2,1,0:T(8,128)S(1)}, f32[2,9,2,512,128]{4,3,2,1,0:T(8,128)}, u32[]{:S(2)}) %copy-start.13) | copy-done | bytes 9437208
  25.0 0.0 copy-start.2
  25.0 0.0 copy-start.9
  25.1 0.9 %table.1 = (f32[9,2,512,128]{3,2,1,0:T(8,128)S(1)}, f32[9,2,64,128]{3,2,1,0:T(8,128)S(1)}, bf16[2,2,2,256,128]{4,3,2,1,0:T(8,128)(2,1)S(1)}, f32[128,2048]{1,0:T(8,128)S(1)}) custom-call(bf16[2,2,512,128]{3,2,1,0:T(8,128)(2,1)S(1)} %copy-done.11, f32[2,9,2,512,128]{4,3,2,1,0:T(8,128)S(1)} %copy-done.13, f32[2,9,2,64,128]{4,3,2,1,0:T(8,128)S(1)} %copy-done.14, ...), custom_call_target="tpu_custom_call" | custom-call | flops 40000000000 | bytes 1048576 | tf_op jit(solution)/shard_map/table/pallas_call | solution.py:405
  25.9 0.0 copy-start
  25.9 2.1 %copy-done = f32[9,2,512,128]{3,2,1,0:T(8,128)} copy-done((f32[9,2,512,128]{3,2,1,0:T(8,128)}, f32[9,2,512,128]{3,2,1,0:T(8,128)S(1)}, u32[]{:S(2)}) %copy-start) | copy-done | bytes 4718616
  28.1 0.0 copy-start.4
  28.1 0.8 copy-done.4
  28.8 8.4 %all-to-all-done = bf16[32,128,128]{2,1,0:T(8,128)(2,1)S(1)} async-done(((bf16[32,128,128]{2,1,0:T(8,128)(2,1)}), bf16[32,128,128]{2,1,0:T(8,128)(2,1)S(1)}, u32[]{:S(2)}, u32[]{:S(2)}) %all-to-all-start) | async-done | bytes 1048608 | tf_op jit(solution)/shard_map/all_to_all | solution.py:453
  37.2 0.0 copy-start.3
  37.2 0.0 copy-start.5
  37.2 0.0 copy-done.2
  37.2 0.0 copy-done.9
  37.2 4.2 %forward.1 = (f32[256,2048]{1,0:T(8,128)S(1)}, f32[256,2048]{1,0:T(8,128)S(1)}) custom-call(bf16[8,512,128]{2,1,0:T(8,128)(2,1)S(1)} %bitcast.5, f32[9,2,64,128]{3,2,1,0:T(8,128)S(1)} %get-tuple-element.21.near, f32[288]{0:T(512)S(1)} %copy-done.9, bf16[256,512]{1,0:T(8,128)(2,1)S(1)} %copy-done.2), custom_call_target="tpu_custom_call" | custom-call | tf_op jit(solution)/shard_map/forward/pallas_call | solution.py:405
  41.5 0.0 collective-permute-done.2.refs_1_
  41.5 0.0 copy-done.3
  41.5 0.0 copy-done.5
  41.5 0.0 copy-start.1
  41.5 3.0 %early_members.1 = (f32[4,256,512]{2,1,0:T(8,128)S(1)}, f32[4,256,512]{2,1,0:T(8,128)S(1)}) custom-call(bf16[2,2,2,256,128]{4,3,2,1,0:T(8,128)(2,1)S(1)} %copy-done.3, bf16[2,2,2,256,128]{4,3,2,1,0:T(8,128)(2,1)} %collective-permute-done.2.refs_1_, bf16[2,2,2,256,128]{4,3,2,1,0:T(8,128)(2,1)S(1)} %copy-done.5, f32[256,2048]{1,0:T(8,128)S(1)} %get-tuple-element.22.refs_3_, ...), custom_call_target="tpu_custom_call" | custom-call | tf_op jit(solution)/shard_map/early_members/pallas_call | solution.py:405
  44.5 1.1 %collective-permute-done.1.refs_0_ = bf16[2,2,2,256,128]{4,3,2,1,0:T(8,128)(2,1)S(1)} collective-permute-done((bf16[2,2,2,256,128]{4,3,2,1,0:T(8,128)(2,1)}, bf16[2,2,2,256,128]{4,3,2,1,0:T(8,128)(2,1)S(1)}, u32[]{:S(2)}, u32[]{:S(2)}) %collective-permute-start.1) | collective-permute-done | bytes 524320 | tf_op jit(solution)/shard_map/ppermute | solution.py:108
  45.5 0.0 copy-done.1
  45.5 2.3 %late_member.1 = bf16[8,512,128]{2,1,0:T(8,128)(2,1)S(1)} custom-call(bf16[2,2,2,256,128]{4,3,2,1,0:T(8,128)(2,1)S(1)} %collective-permute-done.1.refs_0_, f32[4,256,512]{2,1,0:T(8,128)S(1)} %get-tuple-element.24.refs_1_, f32[4,256,512]{2,1,0:T(8,128)S(1)} %get-tuple-element.25.refs_2_, f32[256,2048]{1,0:T(8,128)S(1)} %get-tuple-element.22.refs_3_, ...), custom_call_target="tpu_custom_call" | custom-call | tf_op jit(solution)/shard_map/late_member/pallas_call | solution.py:405
  47.8 0.0 copy-start.8
  47.8 30.9 %all_to_all.10.field_ref = bf16[32,128,128]{2,1,0:T(8,128)(2,1)S(1)} all-to-all(bf16[32,128,128]{2,1,0:T(8,128)(2,1)S(1)} %bitcast.4), channel_id=1, replica_groups=mesh['seq'=8,'ch'=4] {'seq','ch'}, dimensions={0} | all-to-all | bytes 2097152 | tf_op jit(solution)/shard_map/all_to_all | solution.py:477
  78.8 0.0 copy-done.8
  78.8 0.9 %gate.1 = bf16[128,2048]{1,0:T(8,128)(2,1)} custom-call(bf16[128,2048]{1,0:T(8,128)(2,1)S(1)} %copy-done.8, f32[128,2048]{1,0:T(8,128)S(1)} %get-tuple-element.16.direct, bf16[32,128,128]{2,1,0:T(8,128)(2,1)S(1)} %all_to_all.10.field_ref), custom_call_target="tpu_custom_call" | custom-call | tf_op jit(solution)/shard_map/gate/pallas_call | solution.py:405
Async XLA Ops:
  1.3 18.2 %collective-permute-start = (bf16[2,2,512,128]{3,2,1,0:T(8,128)(2,1)S(1)}, bf16[2,2,512,128]{3,2,1,0:T(8,128)(2,1)S(1)}, u32[]{:S(2)}, u32[]{:S(2)}) collective-permute-start(bf16[2,2,512,128]{3,2,1,0:T(8,128)(2,1)S(1)} %dynamic-slice_convert_fusion), channel_id=1, source_target_pairs={{0,12},{4,8},{8,4},{12,0},{16,28},{20,24},{24,20},{28,16},{1,13},{... | collective-permute-start | bytes 1572872 | tf_op jit(solution)/shard_map/ppermute | solution.py:108
  7.7 29.5 %all-to-all-start = ((bf16[32,128,128]{2,1,0:T(8,128)(2,1)}), bf16[32,128,128]{2,1,0:T(8,128)(2,1)S(1)}, u32[]{:S(2)}, u32[]{:S(2)}) async-start(bf16[32,128,128]{2,1,0:T(8,128)(2,1)} %product.1), calls=%async_computation | async-start | bytes 2097152 | tf_op jit(solution)/shard_map/all_to_all | solution.py:453
  11.6 8.7 %copy-start.6 = (bf16[128,2048]{1,0:T(8,128)(2,1)S(1)}, bf16[128,2048]{1,0:T(8,128)(2,1)}, u32[]{:S(2)}) copy-start(bf16[128,2048]{1,0:T(8,128)(2,1)} %key_hbm.1) | copy-start | bytes 1572868
  11.6 8.7 %copy-start.7 = (bf16[128,2048]{1,0:T(8,128)(2,1)S(1)}, bf16[128,2048]{1,0:T(8,128)(2,1)}, u32[]{:S(2)}) copy-start(bf16[128,2048]{1,0:T(8,128)(2,1)} %value_hbm.1) | copy-start | bytes 1572868
  11.6 8.7 %copy-start.12 = (f32[2048]{0:T(1024)S(1)}, f32[2048]{0:T(1024)}, u32[]{:S(2)}) copy-start(f32[2048]{0:T(1024)} %param.13) | copy-start | bytes 24580
  11.7 8.7 %copy-start.14 = (f32[2,9,2,64,128]{4,3,2,1,0:T(8,128)S(1)}, f32[2,9,2,64,128]{4,3,2,1,0:T(8,128)}, u32[]{:S(2)}) copy-start(f32[2,9,2,64,128]{4,3,2,1,0:T(8,128)} %constant.37.clone.near_hbm) | copy-start | bytes 3538948
  15.8 29.7 %collective-permute-start.1 = (bf16[2,2,2,256,128]{4,3,2,1,0:T(8,128)(2,1)}, bf16[2,2,2,256,128]{4,3,2,1,0:T(8,128)(2,1)S(1)}, u32[]{:S(2)}, u32[]{:S(2)}) collective-permute-start(bf16[2,2,2,256,128]{4,3,2,1,0:T(8,128)(2,1)} %get-tuple-element.17), channel_id=1, source_target_pairs={{0,8},{4,12},{8,0},{12,4},{16,24},{20,28},{24,16},{28,20},{1,9},{5... | collective-permute-start | bytes 1572872 | tf_op jit(solution)/shard_map/ppermute | solution.py:108
  17.6 23.9 %collective-permute-start.2 = (bf16[2,2,2,256,128]{4,3,2,1,0:T(8,128)(2,1)}, bf16[2,2,2,256,128]{4,3,2,1,0:T(8,128)(2,1)}, u32[]{:S(2)}, u32[]{:S(2)}) collective-permute-start(bf16[2,2,2,256,128]{4,3,2,1,0:T(8,128)(2,1)} %get-tuple-element.19), channel_id=1, source_target_pairs={{0,4},{4,0},{8,12},{12,8},{16,20},{20,16},{24,28},{28,24},{1,5},{5... | collective-permute-start | bytes 1572872 | tf_op jit(solution)/shard_map/ppermute | solution.py:108
  19.5 0.8 copy-start.10
  20.3 1.0 %copy-start.11 = (bf16[2,2,512,128]{3,2,1,0:T(8,128)(2,1)S(1)}, bf16[2,2,512,128]{3,2,1,0:T(8,128)(2,1)}, u32[]{:S(2)}) copy-start(bf16[2,2,512,128]{3,2,1,0:T(8,128)(2,1)} %copy-done.10) | copy-start | bytes 1572868
  21.4 3.7 %copy-start.13 = (f32[2,9,2,512,128]{4,3,2,1,0:T(8,128)S(1)}, f32[2,9,2,512,128]{4,3,2,1,0:T(8,128)}, u32[]{:S(2)}) copy-start(f32[2,9,2,512,128]{4,3,2,1,0:T(8,128)} %constant.36.clone.table_hbm) | copy-start | bytes 28311556
  25.0 12.2 %copy-start.2 = (bf16[256,512]{1,0:T(8,128)(2,1)S(1)}, bf16[256,512]{1,0:T(8,128)(2,1)}, u32[]{:S(2)}) copy-start(bf16[256,512]{1,0:T(8,128)(2,1)} %constant.35.clone.dft_ref.refs_5_.refs_6_) | copy-start | bytes 786436
  25.0 12.2 %copy-start.9 = (f32[288]{0:T(512)S(1)}, f32[288]{0:T(512)}, u32[]{:S(2)}) copy-start(f32[288]{0:T(512)} %constant.38.clone.far) | copy-start | bytes 3460
  25.9 2.1 %copy-start = (f32[9,2,512,128]{3,2,1,0:T(8,128)}, f32[9,2,512,128]{3,2,1,0:T(8,128)S(1)}, u32[]{:S(2)}) copy-start(f32[9,2,512,128]{3,2,1,0:T(8,128)S(1)} %get-tuple-element.26.refs_5_) | copy-start | bytes 14155780
  28.1 0.8 copy-start.4
  37.2 4.3 %copy-start.3 = (bf16[2,2,2,256,128]{4,3,2,1,0:T(8,128)(2,1)S(1)}, bf16[2,2,2,256,128]{4,3,2,1,0:T(8,128)(2,1)}, u32[]{:S(2)}) copy-start(bf16[2,2,2,256,128]{4,3,2,1,0:T(8,128)(2,1)} %get-tuple-element.18.refs_0_) | copy-start | bytes 1572868
  37.2 4.3 %copy-start.5 = (bf16[2,2,2,256,128]{4,3,2,1,0:T(8,128)(2,1)S(1)}, bf16[2,2,2,256,128]{4,3,2,1,0:T(8,128)(2,1)}, u32[]{:S(2)}) copy-start(bf16[2,2,2,256,128]{4,3,2,1,0:T(8,128)(2,1)} %copy-done.4) | copy-start | bytes 1572868
  41.5 4.0 %copy-start.1 = (f32[9,2,512,128]{3,2,1,0:T(8,128)S(1)}, f32[9,2,512,128]{3,2,1,0:T(8,128)}, u32[]{:S(2)}) copy-start(f32[9,2,512,128]{3,2,1,0:T(8,128)} %copy-done) | copy-start | bytes 14155780
  47.8 30.9 %copy-start.8 = (bf16[128,2048]{1,0:T(8,128)(2,1)S(1)}, bf16[128,2048]{1,0:T(8,128)(2,1)}, u32[]{:S(2)}) copy-start(bf16[128,2048]{1,0:T(8,128)(2,1)} %gate_ref.1) | copy-start | bytes 1572868
